TPU v7x, 32 devices: a whole 2x2x4 slice. The times are simulated.
32 devices in a mesh: slab: 16 (over z, y, x), sub: 2 (over core).
Axes of the slice: x: 2, y: 2, z: 4, core: 2. Of those that a mesh axis runs over, the one named last changes fastest.
Arguments:
- part_cells: int32 [32, 32, 1024], P(('slab', 'sub')), may hold values from 0 to 8191
- part_offsets: float32 [32, 32, 3, 1024], P(('slab', 'sub')), may hold values from 0 to 1
- part_counts: int32 [32, 32], P(('slab', 'sub')), may hold values from 128 to 1024, as said below
- w_first: bfloat16 [16, 27], replicated, may hold values from -1.25 to 1.25
- w_mid: bfloat16 [16, 432], replicated, may hold values from -0.3125 to 0.3125
- w_last: bfloat16 [16, 432], replicated, may hold values from -0.3125 to 0.3125
- w_head: bfloat16 [3, 32], replicated, may hold values from -1 to 1
- cotangent: bfloat16 [3, 64, 16, 256], P(None, 'slab', 'sub'), may hold values from -6 to 6
Outputs:
- force: bfloat16 [3, 64, 16, 256], P(None, 'slab', 'sub')
- grad_first: float32 [16, 27], replicated
- grad_mid: float32 [16, 432], replicated
- grad_last: float32 [16, 432], replicated
- grad_head: float32 [3, 32], replicated
Inputs may be any that keep to these rules, and one draw needn't show every extreme that they name: part_counts[s, d] is the number of used slots among the 1024 slots from device s to brick d; one brick, drawn from the seed, gets 1024 from every device. part_cells[s, d, k] is the cell (i * 8 + j) * 256 + l in brick d's own cells; slots at or above part_counts[s, d] are unused.
All inputs are finite; a program needn't handle non-finite values.
Results may differ from a plain program's by a relative error of at most 0.003.
The roundings to bfloat16 on the way count: a program that leaves them out, or rounds other values in their place, can miss the bound.
Values may be sent and summed in bfloat16 or wider, within the bound.
No kernel may reach another device: no remote copies, remote signals or barrier semaphores. Data moves between devices by JAX's collectives and lax.ppermute only.
A program may use at most 192 MiB of HBM per device.

v0:
```python
import math

import jax
import jax.numpy as jnp
from jax import lax
from jax.sharding import PartitionSpec as P


def padded_2(x, sides, width):
    for axis, dim in sides:
        devices, length = (lax.axis_size(axis), x.shape[dim])
        up = [(i, (i + 1) % devices) for i in range(devices)]
        down = [(j, i) for i, j in up]
        last = lax.slice_in_dim(x, length - width, length, axis=dim)
        initial = lax.slice_in_dim(x, 0, width, axis=dim)
        before = lax.ppermute(last, axis, up)
        after = lax.ppermute(initial, axis, down)
        x = jnp.concatenate([before, x, after], axis=dim)
    return x


def passed_along(x, axis, by):
    devices = lax.axis_size(axis)
    return lax.ppermute(x, axis, [(i, (i + by) % devices) for i in range(devices)])


def silu_slope(value):
    sigma = jax.nn.sigmoid(value)
    return sigma * (1.0 + value * (1.0 - sigma))


def z_stack(plane):
    return jnp.concatenate([jnp.roll(plane, 1, axis=2), plane, jnp.roll(plane, -1, axis=2)], 0)


def conv_planes(padded, kernel, stacker):
    chans = padded.shape[0]
    out_x = padded.shape[1] - 2
    out_y = padded.shape[2] - 2
    out_chans = kernel.shape[0]
    blocks = kernel.reshape(out_chans, 3, 3, 3 * chans)
    stacks = [stacker(padded[:, plane]) for plane in range(out_x + 2)]
    depth_z = stacks[0].shape[2]
    results = []
    for plane in range(out_x):
        total = jnp.zeros((out_chans, out_y * depth_z), jnp.float32)
        for shift_x in range(3):
            for shift_y in range(3):
                piece = stacks[plane + shift_x][:, shift_y : shift_y + out_y].reshape(
                    3 * chans, out_y * depth_z
                )
                total = total + jnp.dot(
                    blocks[:, shift_x, shift_y], piece, preferred_element_type=jnp.float32
                )
        results.append(total.reshape(out_chans, out_y, depth_z))
    return jnp.stack(results, 1)


def weight_grad(padded, grad, stacker):
    chans = padded.shape[0]
    out_x = grad.shape[1]
    out_y = grad.shape[2]
    depth_z = grad.shape[3]
    out_chans = grad.shape[0]
    totals = [
        [jnp.zeros((out_chans, 3 * chans), jnp.float32) for shift_y in range(3)]
        for shift_x in range(3)
    ]
    for plane in range(out_x):
        grad_plane = grad[:, plane].reshape(out_chans, out_y * depth_z)
        for shift_x in range(3):
            stacked = stacker(padded[:, plane + shift_x])
            for shift_y in range(3):
                piece = stacked[:, shift_y : shift_y + out_y].reshape(3 * chans, out_y * depth_z)
                totals[shift_x][shift_y] = totals[shift_x][shift_y] + lax.dot_general(
                    grad_plane, piece, (((1,), (1,)), ((), ())), preferred_element_type=jnp.float32
                )
    joined = jnp.stack([jnp.stack(totals[shift_x], axis=1) for shift_x in range(3)], axis=1)
    return joined.reshape(out_chans, 27 * chans)


def flip_kernel(weights, chans):
    out_chans = weights.shape[0]
    shaped = weights.reshape(out_chans, 3, 3, 3, chans)[:, ::-1, ::-1, ::-1, :]
    return shaped.transpose(4, 1, 2, 3, 0).reshape(chans, 27 * out_chans)


def with_rims(field):
    return padded_2(field, (("slab", 1), ("sub", 2)), 1)


def finish(
    density_rim,
    pre_one,
    hidden_one,
    hidden_one_rim,
    pre_two,
    hidden_two_rim,
    w_mid,
    w_last,
    w_head,
    ct_field,
    rims,
    stacker,
):
    channels = w_mid.shape[0]
    extent = pre_one.shape[1:]
    pre_three = conv_planes(hidden_two_rim, w_last, stacker)
    hidden_three = jax.nn.silu(pre_three).astype(jnp.bfloat16)
    features = jnp.concatenate([hidden_three, hidden_one], 0).reshape(2 * channels, -1)
    ct_flat = ct_field.reshape(3, -1)
    force = jnp.dot(w_head, features, preferred_element_type=jnp.float32).astype(jnp.bfloat16)
    force = force.reshape((3,) + extent)
    grad_head = lax.dot_general(
        ct_flat, features, (((1,), (1,)), ((), ())), preferred_element_type=jnp.float32
    )
    back_features = jnp.dot(w_head.T, ct_flat, preferred_element_type=jnp.float32)
    grad_three = (back_features[:channels] * silu_slope(pre_three.reshape(channels, -1))).astype(
        jnp.bfloat16
    )
    grad_three = grad_three.reshape((channels,) + extent)
    grad_last = weight_grad(hidden_two_rim, grad_three, stacker)
    back_two = conv_planes(rims(grad_three), flip_kernel(w_last, channels), stacker)
    grad_two = (back_two * silu_slope(pre_two)).astype(jnp.bfloat16)
    grad_mid = weight_grad(hidden_one_rim, grad_two, stacker)
    back_one = conv_planes(rims(grad_two), flip_kernel(w_mid, channels), stacker)
    back_one = back_one + back_features[channels:].reshape((channels,) + extent)
    grad_one = (back_one * silu_slope(pre_one)).astype(jnp.bfloat16)
    grad_first = weight_grad(density_rim, grad_one, stacker)
    return (force, grad_first, grad_mid, grad_last, grad_head)


def per_device(part_cells, part_offsets, part_counts, w_first, w_mid, w_last, w_head, cotangent):
    n_slab = lax.axis_size("slab")
    n_sub = lax.axis_size("sub")
    width_x = cotangent.shape[1]
    width_y = cotangent.shape[2]
    depth_z = cotangent.shape[3]
    slot_cap = part_cells.shape[2]
    got_cells, got_offsets, got_counts = (
        lax.all_to_all(part_cells, ("slab", "sub"), split_axis=1, concat_axis=0, tiled=True),
        lax.all_to_all(part_offsets, ("slab", "sub"), split_axis=1, concat_axis=0, tiled=True),
        lax.all_to_all(part_counts, ("slab", "sub"), split_axis=1, concat_axis=0, tiled=True),
    )
    slot_cells = got_cells.reshape(-1, slot_cap)
    offsets = got_offsets.reshape(-1, 3, slot_cap)
    counts = got_counts.reshape(-1)
    slot_ids = jnp.arange(slot_cap, dtype=jnp.int32)
    live = (slot_ids[None, :] < counts[:, None]).astype(jnp.float32)
    cell_x = slot_cells // (width_y * depth_z)
    cell_y = slot_cells // depth_z % width_y
    cell_z = slot_cells % depth_z
    frac_x = offsets[:, 0]
    frac_y = offsets[:, 1]
    frac_z = offsets[:, 2]
    padded = jnp.zeros(((width_x + 1) * (width_y + 1) * depth_z,), jnp.float32)
    for corner_x in (0, 1):
        weight_x = frac_x if corner_x else 1.0 - frac_x
        for corner_y in (0, 1):
            weight_y = frac_y if corner_y else 1.0 - frac_y
            for corner_z in (0, 1):
                weight_z = frac_z if corner_z else 1.0 - frac_z
                share = live * weight_x * weight_y * weight_z
                index = ((cell_x + corner_x) * (width_y + 1) + cell_y + corner_y) * depth_z + (
                    cell_z + corner_z
                ) % depth_z
                padded = padded.at[index.reshape(-1)].add(share.reshape(-1))
    padded = padded.reshape(width_x + 1, width_y + 1, depth_z)
    from_below = passed_along(padded[width_x], "slab", 1)
    core = padded[:width_x].at[0].add(from_below)
    from_side = passed_along(core[:, width_y], "sub", 1)
    density = core[:, :width_y].at[:, 0].add(from_side)
    density_b = density.astype(jnp.bfloat16)[None]
    density_rim = with_rims(density_b)
    pre_one = conv_planes(density_rim, w_first, z_stack)
    hidden_one = jax.nn.silu(pre_one).astype(jnp.bfloat16)
    hidden_one_rim = with_rims(hidden_one)
    pre_two = conv_planes(hidden_one_rim, w_mid, z_stack)
    hidden_two = jax.nn.silu(pre_two).astype(jnp.bfloat16)
    hidden_two_rim = with_rims(hidden_two)
    force, grad_first, grad_mid, grad_last, grad_head = finish(
        density_rim,
        pre_one,
        hidden_one,
        hidden_one_rim,
        pre_two,
        hidden_two_rim,
        w_mid,
        w_last,
        w_head,
        cotangent,
        with_rims,
        z_stack,
    )
    sum_first, sum_mid, sum_last, sum_head = lax.psum(
        (grad_first, grad_mid, grad_last, grad_head), ("slab", "sub")
    )
    loss_scale = 1.0 / math.sqrt(width_x * n_slab * width_y * n_sub * depth_z)
    return (
        force,
        loss_scale * sum_first,
        loss_scale * sum_mid,
        loss_scale * sum_last,
        loss_scale * sum_head,
    )


def solution(mesh):
    in_specs = (
        P(("slab", "sub"), None, None),
        P(("slab", "sub"), None, None, None),
        P(("slab", "sub"), None),
        P(),
        P(),
        P(),
        P(),
        P(None, "slab", "sub", None),
    )
    out_specs = (P(None, "slab", "sub", None), P(), P(), P(), P())
    return jax.shard_map(
        per_device, mesh=mesh, in_specs=in_specs, out_specs=out_specs, check_vma=False
    )
```

profile of v0, /device:TPU:0, one launch (start us, length us, event | category | flops | bytes accessed | tf_op | source)
XLA Modules:
  0.0 1631.4 jit_solution(4376491950484383725)
XLA Ops:
  2.0 7.3 all-to-all-start.1
  11.0 5.4 all-to-all-done.1
  16.4 2.6 all-to-all-start
  18.9 2.1 copy.242
  21.8 5.4 all-to-all-done
  27.2 2.6 all-to-all-start.2
  29.8 3.0 compare_select_fusion
  35.9 9.5 all-to-all-done.2
  46.5 171.0 %scatter_custom_fusion = f32[11520]{0:T(1024)S(1)} fusion(s32[32768]{0:T(1024)S(1)} %bitcast.1771, f32[32768]{0:T(1024)S(1)} %get-tuple-element.95, f32[]{:T(128)} %constant.137.clone.1), kind=kCustom, calls=%fused_computation.493 | custom fusion | flops 32768 | bytes 46084 | tf_op jit(solution)/shard_map/scatter-add | solution.py:167
  217.5 174.7 %scatter_fusion = f32[11520]{0:T(1024)S(1)} fusion(f32[11520]{0:T(1024)S(1)} %scatter_custom_fusion, s32[32768]{0:T(1024)S(1)} %bitcast.1649, f32[32768]{0:T(1024)S(1)} %get-tuple-element.94), kind=kCustom, calls=%fused_computation.1 | custom fusion | flops 32768 | bytes 524288 | tf_op jit(solution)/shard_map/scatter-add | solution.py:167
  392.2 174.7 %scatter_fusion.1 = f32[11520]{0:T(1024)S(1)} fusion(f32[11520]{0:T(1024)S(1)} %scatter_fusion, s32[32768]{0:T(1024)S(1)} %bitcast.1648, f32[32768]{0:T(1024)S(1)} %get-tuple-element.89), kind=kCustom, calls=%fused_computation.2 | custom fusion | flops 32768 | bytes 524288 | tf_op jit(solution)/shard_map/scatter-add | solution.py:167
  567.0 174.7 %scatter_fusion.2 = f32[11520]{0:T(1024)S(1)} fusion(f32[11520]{0:T(1024)S(1)} %scatter_fusion.1, s32[32768]{0:T(1024)S(1)} %bitcast.1646, f32[32768]{0:T(1024)S(1)} %copy-done.25), kind=kCustom, calls=%fused_computation.3 | custom fusion | flops 32768 | bytes 524288 | tf_op jit(solution)/shard_map/scatter-add | solution.py:167
  741.7 175.2 %scatter_fusion.3 = f32[11520]{0:T(1024)S(1)} fusion(f32[11520]{0:T(1024)S(1)} %scatter_fusion.2, s32[32768]{0:T(1024)S(1)} %bitcast.1647, f32[32768]{0:T(1024)S(1)} %copy-done.24), kind=kCustom, calls=%fused_computation.4 | custom fusion | flops 32768 | bytes 524288 | tf_op jit(solution)/shard_map/scatter-add | solution.py:167
  916.9 174.7 %scatter_fusion.4 = f32[11520]{0:T(1024)S(1)} fusion(f32[11520]{0:T(1024)S(1)} %scatter_fusion.3, s32[32768]{0:T(1024)S(1)} %bitcast.1645, f32[32768]{0:T(1024)S(1)} %copy-done.23), kind=kCustom, calls=%fused_computation.5 | custom fusion | flops 32768 | bytes 524288 | tf_op jit(solution)/shard_map/scatter-add | solution.py:167
  1091.7 174.7 %scatter_fusion.5 = f32[11520]{0:T(1024)S(1)} fusion(f32[11520]{0:T(1024)S(1)} %scatter_fusion.4, s32[32768]{0:T(1024)S(1)} %bitcast.1644, f32[32768]{0:T(1024)S(1)} %copy-done.22), kind=kCustom, calls=%fused_computation.6 | custom fusion | flops 32768 | bytes 524288 | tf_op jit(solution)/shard_map/scatter-add | solution.py:167
  1266.4 174.7 %scatter_fusion.6 = f32[11520]{0:T(1024)S(1)} fusion(f32[11520]{0:T(1024)S(1)} %scatter_fusion.5, s32[32768]{0:T(1024)S(1)} %bitcast.1643, f32[32768]{0:T(1024)S(1)} %copy-done.21), kind=kCustom, calls=%fused_computation.7 | custom fusion | flops 32768 | bytes 524288 | tf_op jit(solution)/shard_map/scatter-add | solution.py:167
  1442.2 6.4 collective-permute-done
  1449.9 5.6 collective-permute-start.3
  1468.8 5.8 collective-permute-start.7
  1489.5 5.6 collective-permute-start.11
  1541.3 2.8 collective-permute-done.14
  1561.8 2.9 collective-permute-start.19
  1569.8 3.1 collective-permute-done.18
  1590.4 38.0 %all-reduce = (f32[16,27]{0,1:T(8,128)S(1)}, f32[16,432]{1,0:T(8,128)S(1)}, f32[16,432]{1,0:T(8,128)S(1)}, f32[3,32]{1,0:T(4,128)S(1)}) all-reduce(f32[16,27]{0,1:T(8,128)S(1)} %reshape.1267, f32[16,432]{1,0:T(8,128)S(1)} %reshape.1268, f32[16,432]{1,0:T(8,128)S(1)} %copy-done.44, ...), channel_id=1, replica_groups=mesh['slab'=16,'sub'=2] {'slab','sub'}, use_global_device_ids=true, to_apply=%region_8.9 | all-reduce | flops 14352 | bytes 114816 | tf_op jit(solution)/shard_map/psum | solution.py:195
  (842 shorter events, 124.7 us)
Async XLA Ops:
  2.0 14.4 all-to-all-start.1
  16.4 10.8 all-to-all-start
  27.2 18.2 %all-to-all-start.2 = ((f32[1,32,3,1024]{3,2,0,1:T(4,128)}), f32[1,32,3,1024]{3,2,0,1:T(4,128)S(1)}, u32[]{:S(2)}, u32[]{:S(2)}) async-start(f32[1,32,3,1024]{3,2,0,1:T(4,128)} %copy.242), calls=%async_computation.2 | async-start | bytes 1048576 | tf_op jit(solution)/shard_map/all_to_all | solution.py:142
  1441.2 7.4 collective-permute-start
  1448.6 1.2 collective-permute-start.1
  1449.9 7.3 collective-permute-start.2
  1449.9 7.2 collective-permute-start.3
  1457.2 1.2 collective-permute-start.4
  1457.2 1.3 collective-permute-start.5
  1468.8 8.3 collective-permute-start.6
  1468.8 8.2 collective-permute-start.7
  1477.1 1.3 collective-permute-start.8
  1477.1 1.4 collective-permute-start.9
  1489.5 28.2 %collective-permute-start.10 = (bf16[16,1,8,256]{3,0,2,1:T(8,128)(2,1)}, bf16[16,1,8,256]{3,0,2,1:T(8,128)(2,1)}, u32[]{:S(2)}, u32[]{:S(2)}) collective-permute-start(bf16[16,1,8,256]{3,0,2,1:T(8,128)(2,1)} %get-tuple-element.134), channel_id=1, source_target_pairs={{0,2},{2,4},{4,6},{6,8},{8,10},{10,12},{12,14},{14,16},{16,18},{18... | collective-permute-start | bytes 196616 | tf_op jit(solution)/shard_map/ppermute | solution.py:16
  1489.5 28.2 %collective-permute-start.11 = (bf16[16,1,8,256]{3,0,2,1:T(8,128)(2,1)}, bf16[16,1,8,256]{3,0,2,1:T(8,128)(2,1)}, u32[]{:S(2)}, u32[]{:S(2)}) collective-permute-start(bf16[16,1,8,256]{3,0,2,1:T(8,128)(2,1)} %get-tuple-element.135), channel_id=1, source_target_pairs={{2,0},{4,2},{6,4},{8,6},{10,8},{12,10},{14,12},{16,14},{18,16},{20... | collective-permute-start | bytes 196616 | tf_op jit(solution)/shard_map/ppermute | solution.py:17
  1518.5 1.3 collective-permute-start.12
  1518.6 1.4 collective-permute-start.13
  1533.6 10.5 collective-permute-start.15
  1535.9 8.1 collective-permute-start.14
  1544.9 2.9 collective-permute-start.16
  1544.9 2.9 collective-permute-start.17
  1561.8 8.0 collective-permute-start.19
  1564.7 8.2 collective-permute-start.18
  1572.9 1.3 collective-permute-start.20
  (71 other events, 3748.3 us)
where the time goes:
time: 1640 us; the launch traced here: 1630 us
  other arithmetic  1410 us (86%)
  local copies, waits for them, and re-layouts  49.8 us (3%)
  matrix products  48.5 us (3%)
  waiting for transfers between devices  39.1 us (2%)
  starting transfers between devices  38.5 us (2%)
  blocking collectives  38 us (2%)
    scatter-add x8, other arithmetic, per_device(): padded = padded.at[index.reshape(-1)].add(share.reshape(-1))  1390 us
    psum x1, blocking collectives, per_device(): lax.psum((grad_first, grad_mid, grad_last, grad_head), ('slab', 'sub'))  38 us
  transfers between devices with their start and end apart: 25, of which 17 were waited for; matrix products, arithmetic and copies ran while one was open for 3% of the time, Pallas kernels for 0%

commit v1 on v0

v1 whole, which is shorter than its diff:
```python
import functools
import math

import jax
import jax.numpy as jnp
from jax import lax
from jax.experimental import pallas as pl
from jax.experimental.pallas import tpu as pltpu
from jax.sharding import PartitionSpec as P

BITS = 21
STEPS = 1 << BITS


def pack_kernel(dead, cells_hbm, offsets_hbm, counts_hbm, words_ref, cells_ref, offsets_ref, counts_ref, sems):
    dests, cap = cells_ref.shape
    copies = [
        pltpu.make_async_copy(source, target, sems.at[i])
        for i, (source, target) in enumerate(
            ((counts_hbm, counts_ref), (cells_hbm, cells_ref), (offsets_hbm, offsets_ref))
        )
    ]
    for copy in copies:
        copy.start()
    for copy in copies:
        copy.wait()
    eye = lax.broadcasted_iota(jnp.int32, (dests, dests), 0) == lax.broadcasted_iota(jnp.int32, (dests, dests), 1)
    counts = jnp.where(eye, counts_ref[...].astype(jnp.float32), 0.0)
    counts = jnp.sum(counts, axis=1, keepdims=True).astype(jnp.int32)
    live = lax.broadcasted_iota(jnp.int32, (dests, cap), 1) < counts
    code = jnp.where(live, cells_ref[...], dead)
    fixed = [
        jnp.minimum((offsets_ref[i] * STEPS + 0.5).astype(jnp.int32), STEPS - 1) for i in range(3)
    ]
    first = fixed[0] | (fixed[2] << BITS)
    second = fixed[1] | ((fixed[2] >> (32 - BITS)) << BITS)
    codes = code[:, : cap // 2] | (code[:, cap // 2 :] << 16)
    for dest in range(dests):
        words_ref[dest, :, 0:cap] = first[dest : dest + 1]
        words_ref[dest, :, cap : 2 * cap] = second[dest : dest + 1]
        words_ref[dest, :, 2 * cap :] = codes[dest : dest + 1]


def packed_slots(cells, offsets, counts, width_x, width_y, depth_z):
    dests, cap = cells.shape
    return pl.pallas_call(
        functools.partial(pack_kernel, 2 * width_x * width_y * depth_z),
        out_shape=jax.ShapeDtypeStruct((dests, 1, 5 * cap // 2), jnp.int32),
        in_specs=[pl.BlockSpec(memory_space=pltpu.HBM)] * 3,
        out_specs=pl.BlockSpec(memory_space=pltpu.VMEM),
        scratch_shapes=[
            pltpu.VMEM((dests, cap), jnp.int32),
            pltpu.VMEM((3, dests, cap), jnp.float32),
            pltpu.VMEM((1, dests), jnp.int32),
            pltpu.SemaphoreType.DMA((3,)),
        ],
        compiler_params=pltpu.CompilerParams(vmem_limit_bytes=60 * 1024 * 1024),
        name="pack",
    )(cells, offsets.transpose(1, 0, 2), counts)


def deposit_kernel(width_x, width_y, depth_z, cap, words_ref, after_ref, late_ref, out_ref, acc_ref):
    rows = out_ref.shape[0]
    acc_ref[...] = jnp.zeros_like(acc_ref)
    slot_rows = cap // 128
    source_rows = slot_rows * 5 // 2
    group = 16 // slot_rows
    row_id = lax.broadcasted_iota(jnp.int32, (8, 128), 0)
    z_id = lax.broadcasted_iota(jnp.int32, (depth_z, 128), 0).astype(jnp.float32).astype(jnp.bfloat16)
    one, zero = jnp.bfloat16(1.0), jnp.bfloat16(0.0)

    def body(i, carry):
        block = words_ref[pl.ds(pl.multiple_of(i * group * source_rows, 8), group * source_rows), :]

        def gathered(start, length):
            parts = [block[k * source_rows + start : k * source_rows + start + length] for k in range(group)]
            return parts

        first = jnp.concatenate(gathered(0, slot_rows), axis=0)
        second = jnp.concatenate(gathered(slot_rows, slot_rows), axis=0)
        halves = gathered(2 * slot_rows, slot_rows // 2)
        code = jnp.concatenate([part for half in halves for part in (half & 0xFFFF, (half >> 16) & 0xFFFF)], axis=0)
        inv = 1.0 / STEPS
        fixed_z = ((first >> BITS) & ((1 << (32 - BITS)) - 1)) | ((second >> BITS) << (32 - BITS))
        frac_x = (first & (STEPS - 1)).astype(jnp.float32) * inv
        frac_y = (second & (STEPS - 1)).astype(jnp.float32) * inv
        frac_z = fixed_z.astype(jnp.float32) * inv
        cell_z = (code % depth_z).astype(jnp.float32)
        column = code // depth_z
        cell_y = column % width_y
        cell_x = column // width_y
        past = jnp.where(cell_y == width_y - 1, frac_y, 0.0)
        rest_x, rest_y, rest_z = 1.0 - frac_x, 1.0 - frac_y, 1.0 - frac_z
        weights, hot = [], []
        for k in range(16):
            row = slice(k, k + 1)
            at_y, at_x = cell_y[row], cell_x[row]
            wy = jnp.where(at_y == row_id, rest_y[row], jnp.where(at_y + 1 == row_id, frac_y[row], 0.0))
            wx = jnp.where(at_x == row_id, rest_x[row], jnp.where(at_x + 1 == row_id, frac_x[row], 0.0))
            parts = [wx[x : x + 1] * wy for x in range(width_x + 1)] + [wx * past[row]]
            area = jnp.concatenate(parts, axis=0)
            low, high = area * rest_z[row], area * frac_z[row]
            low_a, high_a = low.astype(jnp.bfloat16), high.astype(jnp.bfloat16)
            low_b = (low - low_a.astype(jnp.float32)).astype(jnp.bfloat16)
            high_b = (high - high_a.astype(jnp.float32)).astype(jnp.bfloat16)
            weights.append(jnp.concatenate([low_a, low_b, high_a, high_b], axis=0))
            at_z = jnp.broadcast_to(cell_z[row], (depth_z, 128)).astype(jnp.bfloat16)
            hot.append(jnp.where(at_z == z_id, one, zero))
        acc_ref[...] += lax.dot_general(
            jnp.concatenate(weights, axis=1),
            jnp.concatenate(hot, axis=1),
            (((1,), (1,)), ((), ())),
            preferred_element_type=jnp.float32,
        )
        return carry

    lax.fori_loop(0, words_ref.shape[0] // (group * source_rows), body, 0, unroll=8)
    low = acc_ref[0:rows] + acc_ref[rows : 2 * rows]
    high = acc_ref[2 * rows : 3 * rows] + acc_ref[3 * rows : 4 * rows]
    out_ref[...] = low + pltpu.roll(high, 1, axis=1)


def deposit(words, after, late, cap, width_x, width_y, depth_z):
    rows = (width_x + 1) * width_y + 8
    return pl.pallas_call(
        functools.partial(deposit_kernel, width_x, width_y, depth_z, cap),
        out_shape=jax.ShapeDtypeStruct((rows, depth_z), jnp.float32),
        in_specs=[pl.BlockSpec(memory_space=pltpu.VMEM)] * 3,
        out_specs=pl.BlockSpec(memory_space=pltpu.VMEM),
        scratch_shapes=[pltpu.VMEM((4 * rows, depth_z), jnp.float32)],
        compiler_params=pltpu.CompilerParams(vmem_limit_bytes=16 * 1024 * 1024),
        name="deposit",
    )(words.reshape(-1, 128), after, late)


def combine_kernel(width_x, width_y, own_ref, other_ref, near_ref, far_ref):
    full_y = 2 * width_y
    spill = (width_x + 1) * width_y
    top = lax.broadcasted_iota(jnp.int32, (width_y, own_ref.shape[1]), 0) == 0
    planes = []
    for x in range(width_x + 1):
        rows, edge = slice(x * width_y, (x + 1) * width_y), slice(spill + x, spill + x + 1)
        upper = own_ref[rows] + jnp.where(top, other_ref[edge], 0.0)
        lower = other_ref[rows] + jnp.where(top, own_ref[edge], 0.0)
        near_ref[x * full_y : x * full_y + width_y] = upper
        near_ref[x * full_y + width_y : (x + 1) * full_y] = lower
        planes.append((upper, lower))
    upward = lax.axis_index("sub") == 0
    for i, (up, down) in enumerate(((width_x - 1, 0), (width_x, 0))):
        for half in range(2):
            start = i * full_y + half * width_y
            far_ref[start : start + width_y] = jnp.where(upward, planes[up][half], planes[down][half])


def combined(own, other, width_x, width_y):
    depth_z = own.shape[1]
    full_y = 2 * width_y
    return pl.pallas_call(
        functools.partial(combine_kernel, width_x, width_y),
        out_shape=(
            jax.ShapeDtypeStruct(((width_x + 1) * full_y, depth_z), jnp.float32),
            jax.ShapeDtypeStruct((2 * full_y, depth_z), jnp.float32),
        ),
        in_specs=[pl.BlockSpec(memory_space=pltpu.VMEM)] * 2,
        out_specs=(pl.BlockSpec(memory_space=pltpu.VMEM),) * 2,
        compiler_params=pltpu.CompilerParams(vmem_limit_bytes=4 * 1024 * 1024),
        name="combine",
    )(own, other)


CH = 16


def dot(a, b, dims=((1,), (0,))):
    return lax.dot_general(a, b, (dims, ((), ())), preferred_element_type=jnp.float32)


def iota(shape, axis):
    return lax.broadcasted_iota(jnp.int32, shape, axis)


def weights_kernel(
    full_y, raw_ref, after_ref, mats_ref, wfirst_ref, whead_ref, square, taps_ref
):
    lanes = full_y * CH
    f32, bf16 = jnp.float32, jnp.bfloat16
    slot = iota((CH, 128), 1) // CH

    def turned(x, by):
        return x if by % 128 == 0 else pltpu.roll(x, by % 128, axis=1)

    square[...] = jnp.zeros_like(square)
    for which in range(2):
        square[0:CH, :] = raw_ref[:, which * 512 : (which + 1) * 512].astype(f32)
        flipped = jnp.transpose(square[...])
        for dx in range(3):
            for dz in range(3):
                ahead = back = jnp.zeros((CH, 128), f32)
                for dy in range(3):
                    start = (dx * 9 + dy * 3 + dz) * CH
                    ahead = ahead + turned(flipped[start : start + CH], dy * CH)
                    block = start // 128 * 128
                    picked = jnp.where(slot == (start - block) // CH, square[0:CH, block : block + 128], 0.0)
                    back = back + turned(picked, dy * CH - (start - block))
                rows = slice((dx * 3 + dz) * CH, (dx * 3 + dz + 1) * CH)
                taps_ref[which, rows, :] = ahead.astype(bf16)
                taps_ref[2 + which, rows, :] = back.astype(bf16)

    row, lane = iota((128, lanes), 0), iota((128, lanes), 1)
    same = row % CH == lane % CH
    shift, lane_y = row // CH - 1, lane // CH

    def body(y, carry):
        forward = jnp.where(same & (lane_y == (y - shift + full_y) % full_y), 1.0, 0.0).astype(bf16)
        back = jnp.where(same & (lane_y == (y + shift + full_y) % full_y), 1.0, 0.0).astype(bf16)
        for which in range(4):
            spread = dot(taps_ref[which], forward if which < 2 else back).astype(bf16)
            for dx in range(3):
                for dz in range(3):
                    tap = dx * 3 + dz if which < 2 else (2 - dx) * 3 + 2 - dz
                    start = pl.multiple_of(dz * lanes + y * CH, CH)
                    mats_ref[which, dx, pl.ds(start, CH), :] = spread[tap * CH : (tap + 1) * CH]
        return carry

    lax.fori_loop(0, full_y, body, 0, unroll=4)

    rows = 9 * full_y
    at_y, at_lane = iota((rows, lanes), 0) % full_y, iota((rows, lanes), 1) // CH
    square[...] = jnp.zeros_like(square)
    square[0:CH, 0:128] = raw_ref[:, 1024:1152].astype(f32)
    flipped = jnp.transpose(square[:, 0:128])
    spread_rows = []
    for dx in range(3):
        for dz in range(3):
            line = jnp.zeros((1, 128), f32)
            for dy in range(3):
                tap = dx * 9 + dy * 3 + dz
                line = line + turned(flipped[tap : tap + 1], dy * CH)
            spread_rows.append(jnp.broadcast_to(line, (full_y, 128)))
    first = jnp.concatenate(spread_rows, axis=0).astype(bf16)
    total = jnp.zeros((rows, lanes), f32)
    for dy in range(3):
        pick = jnp.where(same & (row // CH == dy), 1.0, 0.0).astype(bf16)
        total = jnp.where(at_y == (at_lane + dy - 1 + full_y) % full_y, dot(first, pick), total)
    wfirst_ref[...] = total.astype(bf16)

    rows = 3 * full_y
    at_y, at_lane = iota((rows, lanes), 0) % full_y, iota((rows, lanes), 1) // CH
    square[...] = jnp.zeros_like(square)
    square[0:CH, 0:128] = raw_ref[:, 1152:1280].astype(f32)
    head = [jnp.broadcast_to(square[k : k + 1, 0:128], (full_y, 128)) for k in range(3)]
    head = jnp.concatenate(head, axis=0).astype(bf16)
    for half in range(2):
        pick = jnp.where(row == lane % CH + half * CH, 1.0, 0.0).astype(bf16)
        whead_ref[half] = jnp.where(at_y == at_lane, dot(head, pick), 0.0).astype(bf16)


def side_by_side(w_first, w_mid, w_last, w_head):
    def widened(w, columns):
        return jnp.pad(w, ((0, CH - w.shape[0]), (0, columns - w.shape[1])))

    return jnp.concatenate([widened(w_mid, 512), widened(w_last, 512), widened(w_first, 128), widened(w_head, 128)], axis=1)


def weight_matrices(raw, after, full_y):
    lanes = full_y * CH
    return pl.pallas_call(
        functools.partial(weights_kernel, full_y),
        out_shape=(
            jax.ShapeDtypeStruct((4, 3, 3 * lanes, lanes), jnp.bfloat16),
            jax.ShapeDtypeStruct((9 * full_y, lanes), jnp.bfloat16),
            jax.ShapeDtypeStruct((2, 3 * full_y, lanes), jnp.bfloat16),
        ),
        in_specs=[pl.BlockSpec(memory_space=pltpu.VMEM)] * 2,
        out_specs=(pl.BlockSpec(memory_space=pltpu.VMEM),) * 3,
        scratch_shapes=[pltpu.VMEM((128, 512), jnp.float32), pltpu.VMEM((4, 9 * CH, 128), jnp.bfloat16)],
        compiler_params=pltpu.CompilerParams(vmem_limit_bytes=16 * 1024 * 1024),
        cost_estimate=pl.CostEstimate(flops=2 * 4 * 9 * CH * 128 * lanes * full_y, bytes_accessed=8 << 20, transcendentals=0),
        name="weights",
    )(raw, after)


def edges_kernel(width_x, width_y, own_ref, other_ref, middle_ref, edge_ref):
    full_y = 2 * width_y
    upward = lax.axis_index("sub") == 0
    for k in range(3):
        rows = slice(k * full_y, (k + 1) * full_y)
        planes = []
        for x in range(width_x):
            both = [own_ref[k, x].astype(jnp.float32), other_ref[k, x].astype(jnp.float32)]
            planes.append(jnp.concatenate(both, axis=0))
            middle_ref[x, rows] = planes[x].astype(jnp.bfloat16)
        for i in range(2):
            edge_ref[i, rows] = jnp.where(upward, planes[width_x - 2 + i], planes[i]).astype(jnp.bfloat16)


def edges(own, other):
    _, width_x, width_y, depth_z = own.shape
    return pl.pallas_call(
        functools.partial(edges_kernel, width_x, width_y),
        out_shape=(
            jax.ShapeDtypeStruct((width_x, 6 * width_y, depth_z), jnp.bfloat16),
            jax.ShapeDtypeStruct((2, 6 * width_y, depth_z), jnp.bfloat16),
        ),
        in_specs=[pl.BlockSpec(memory_space=pltpu.VMEM)] * 2,
        out_specs=(pl.BlockSpec(memory_space=pltpu.VMEM),) * 2,
        compiler_params=pltpu.CompilerParams(vmem_limit_bytes=4 * 1024 * 1024),
        name="edges",
    )(own, other)


def sigmoid(v):
    return 0.5 + 0.5 * jnp.tanh(0.5 * v)


def chain_kernel(
    width_x,
    width_y,
    near_ref,
    near_mine,
    near_theirs,
    far_mine,
    far_theirs,
    ct_middle,
    ct_mine,
    ct_theirs,
    mats_ref,
    wfirst_ref,
    whead_ref,
    force_ref,
    mine_ref,
    ct_ref,
    dens,
    fields,
    three,
    grads,
    pre_one,
    pre_two,
    wg,
):
    full_y = 2 * width_y
    depth = ct_ref.shape[2]
    lanes = full_y * CH
    own = width_y * CH
    first_core = lax.axis_index("sub") == 0

    def turned(ref, plane):
        start = plane * full_y
        return jnp.concatenate([ref[start + width_y : start + full_y], ref[start : start + width_y]], axis=0)

    def straight(ref, plane):
        return ref[plane * full_y : (plane + 1) * full_y]

    planes = [straight(near_ref, x) for x in range(width_x + 1)]
    below = [jnp.where(first_core, straight(near_mine, x), turned(near_theirs, x)) for x in range(width_x + 1)]
    above = [jnp.where(first_core, turned(near_theirs, x), straight(near_mine, x)) for x in range(width_x + 1)]
    tail = [jnp.where(first_core, straight(far_mine, x), turned(far_theirs, x)) for x in range(2)]
    ahead = jnp.where(first_core, turned(far_theirs, 0), straight(far_mine, 0))
    column = [tail[0], tail[1] + below[0], *below[1:width_x], below[width_x] + planes[0], *planes[1:width_x]]
    column = column + [planes[width_x] + above[0], *above[1:width_x], above[width_x] + ahead]
    n_dens = 3 * width_x + 2
    for j in range(n_dens):
        plane = column[j]
        around = [pltpu.roll(plane, 1, axis=1), plane, pltpu.roll(plane, depth - 1, axis=1)]
        dens[3 * full_y * j : 3 * full_y * (j + 1)] = jnp.concatenate(around, axis=0).astype(jnp.bfloat16)

    for x in range(width_x):
        ct_ref[x + 2] = ct_middle[x]
    for x in range(2):
        mine, theirs = ct_mine[x].astype(jnp.float32), ct_theirs[x].astype(jnp.float32)
        halves = [theirs[i * width_y : (i + 1) * width_y] for i in (1, 0, 3, 2, 5, 4)]
        theirs = jnp.concatenate(halves, axis=0)
        ct_ref[x] = jnp.where(first_core, mine, theirs).astype(jnp.bfloat16)
        ct_ref[x + 2 + width_x] = jnp.where(first_core, theirs, mine).astype(jnp.bfloat16)

    def window(x):
        return dens[pl.ds(pl.multiple_of(3 * full_y * x, 3 * full_y), 9 * full_y), :]

    def put(ref, x, field):
        ref[x, :, 0:lanes] = pltpu.roll(field, 1, axis=0).astype(jnp.bfloat16)
        ref[x, :, lanes : 2 * lanes] = field.astype(jnp.bfloat16)
        ref[x, :, 2 * lanes : 3 * lanes] = pltpu.roll(field, depth - 1, axis=0).astype(jnp.bfloat16)

    def conv(ref, x, which, columns=lanes):
        field = jnp.concatenate([ref[x + dx : x + dx + 2].reshape(2 * depth, 3 * lanes) for dx in range(3)], axis=1)
        weights = mats_ref[which].reshape(9 * lanes, lanes)[:, 0:columns]
        return dot(field, weights).reshape(2, depth, columns)

    def slope(v):
        s = sigmoid(v)
        return s * (1.0 + v * (1.0 - s))

    one, two = 0, n_dens - 2
    g_three, g_two = 0, n_dens - 6

    for x in range(n_dens - 2):
        v = dot(window(x), wfirst_ref[...], ((0,), (0,)))
        if 0 <= x - 4 < width_x:
            pre_one[x - 4] = v[:, 0:own]
        put(fields, one + x, v * sigmoid(v))

    for i in range((n_dens - 4) // 2):
        both = conv(fields, one + 2 * i, 0)
        for k in range(2):
            v, x = both[k], 2 * i + k
            if 0 <= x - 2 < width_x + 2:
                pre_two[x - 2] = v
            put(fields, two + x, v * sigmoid(v))

    for i in range((n_dens - 6) // 2):
        both = conv(fields, two + 2 * i, 1)
        for k in range(2):
            v, x = both[k], 2 * i + k
            s = sigmoid(v)
            if 0 <= x - 2 < width_x:
                three[x - 2] = (v * s).astype(jnp.bfloat16)
            back = dot(ct_ref[x], whead_ref[0], ((0,), (0,)))
            put(grads, g_three + x, back * (s * (1.0 + v * (1.0 - s))))

    ct_own = jnp.concatenate([ct_ref[x + 2] for x in range(width_x)], axis=1)
    heads = [
        dot(ct_own, three[:, :, 0:own].reshape(width_x * depth, own)),
        dot(ct_own, fields[one + 4 : one + 4 + width_x, :, lanes : lanes + own].reshape(width_x * depth, own)),
    ]
    for x in range(width_x):
        h_three, h_one = three[x], fields[one + x + 4, :, lanes : 2 * lanes]
        rows = dot(whead_ref[0], h_three, ((1,), (1,))) + dot(whead_ref[1], h_one, ((1,), (1,)))
        for k in range(3):
            force_ref[k, x] = rows[k * full_y : k * full_y + width_y].astype(jnp.bfloat16)

    for i in range((width_x + 2) // 2):
        both = conv(grads, g_three + 2 * i, 3)
        for k in range(2):
            x = 2 * i + k
            put(grads, g_two + x, both[k] * slope(pre_two[x]))

    grad_base = jnp.where(first_core, g_three + 2, g_two + 1)
    field_base = jnp.where(first_core, two + 2, one + 3)
    across = []
    for x in range(width_x):
        grad = grads[grad_base + x, :, lanes : 2 * lanes].astype(jnp.float32)
        across.append(jnp.transpose(grad).astype(jnp.bfloat16))
    across = jnp.concatenate(across, axis=1)
    for dx in range(3):
        field = fields[pl.ds(field_base + dx, width_x)].reshape(width_x * depth, 3 * lanes)
        wg[dx] = dot(across, field)
    grad_one = []
    for i in range(width_x // 2):
        both = conv(grads, g_two + 2 * i, 2, own)
        for k in range(2):
            x = 2 * i + k
            total = both[k] + dot(ct_ref[x + 2], whead_ref[1, :, 0:own], ((0,), (0,)))
            grad_one.append((total * slope(pre_one[x])).astype(jnp.bfloat16))
    windows = jnp.concatenate([window(x + 4) for x in range(width_x)], axis=1)
    firsts = dot(windows, jnp.concatenate(grad_one, axis=0))

    lane = iota((CH, 128), 1)
    blocks = [jnp.zeros((CH, 128), jnp.float32) for _ in range(4)]
    for dx in range(3):
        for dz in range(3):
            lined = jnp.zeros((CH, lanes), jnp.float32)
            for y in range(full_y):
                piece = wg[dx, y * CH : (y + 1) * CH, dz * lanes : (dz + 1) * lanes]
                turn = (lanes - CH * (y - 1)) % lanes
                lined = lined + (piece if turn == 0 else pltpu.roll(piece, turn, axis=1))
            for dy in range(3):
                target = (dx * 9 + dy * 3 + dz) * CH
                turn = (target - dy * CH) % 128
                piece = jnp.where(lane // CH == dy, lined[:, 0:128], 0.0)
                blocks[target // 128] += piece if turn == 0 else pltpu.roll(piece, turn, axis=1)
    def folded(rows):
        for turn in (64, 32, 16):
            rows = rows + pltpu.roll(rows, turn, axis=1)
        return rows

    at_y, at_lane = iota((full_y, own), 0), iota((full_y, own), 1) // CH
    first_rows = []
    for dx in range(3):
        for dy in range(3):
            match = at_y == (at_lane + dy - 1 + full_y) % full_y
            for dz in range(3):
                tap = (dx * 3 + dz) * full_y
                part = jnp.where(match, firsts[tap : tap + full_y, :], 0.0)
                first_rows.append(jnp.sum(part, axis=0, keepdims=True))
    first = folded(jnp.concatenate(first_rows + [jnp.zeros((5, own), jnp.float32)], axis=0))
    gap = jnp.zeros((48, own), jnp.float32)
    blocks[3] += jnp.transpose(jnp.concatenate([gap, first, gap], axis=0))[0:CH]
    for half in range(2):
        rows = []
        for k in range(3):
            part = jnp.where(at_y == at_lane, heads[half][k * full_y : (k + 1) * full_y], 0.0)
            rows.append(jnp.sum(part, axis=0, keepdims=True))
        head = folded(jnp.concatenate(rows + [jnp.zeros((CH - 3, own), jnp.float32)], axis=0))
        blocks[3] += jnp.where(lane // CH == 5 + half, head, 0.0)
    for block in range(4):
        mine_ref[:, block * 128 : (block + 1) * 128] = blocks[block]


def chain(pieces, mats, wfirst, whead, width_x, width_y, depth_z):
    full_y = 2 * width_y
    lanes, own = full_y * CH, width_y * CH
    n_dens = 3 * width_x + 2
    bf16, f32 = jnp.bfloat16, jnp.float32
    args = (*pieces, mats, wfirst, whead)
    return pl.pallas_call(
        functools.partial(chain_kernel, width_x, width_y),
        out_shape=(
            jax.ShapeDtypeStruct((3, width_x, width_y, depth_z), bf16),
            jax.ShapeDtypeStruct((CH, 512), f32),
        ),
        in_specs=[pl.BlockSpec(memory_space=pltpu.VMEM)] * len(args),
        out_specs=(pl.BlockSpec(memory_space=pltpu.VMEM),) * 2,
        scratch_shapes=[
            pltpu.VMEM((width_x + 4, 3 * full_y, depth_z), bf16),
            pltpu.VMEM((n_dens * 3 * full_y, depth_z), bf16),
            pltpu.VMEM((2 * n_dens - 6, depth_z, 3 * lanes), bf16),
            pltpu.VMEM((width_x, depth_z, lanes), bf16),
            pltpu.VMEM((2 * n_dens - 14, depth_z, 3 * lanes), bf16),
            pltpu.VMEM((width_x, depth_z, own), f32),
            pltpu.VMEM((width_x + 2, depth_z, lanes), f32),
            pltpu.VMEM((3, lanes, 3 * lanes), f32),
        ],
        compiler_params=pltpu.CompilerParams(vmem_limit_bytes=36 * 1024 * 1024),
        name="chain",
    )(*args)


def passed_along(x, axis, by):
    devices = lax.axis_size(axis)
    return lax.ppermute(x, axis, [(i, (i + by) % devices) for i in range(devices)])


def exchanged(x, axis, mask):
    return lax.ppermute(x, axis, [(i, i ^ mask) for i in range(lax.axis_size(axis))])


def summed(total):
    stride, chips = 1, lax.axis_size("slab")
    while stride < chips:
        if chips // stride >= 4:
            got = [exchanged(total, "slab", stride * i) for i in (1, 2, 3)]
            total = (total + got[0]) + (got[1] + got[2])
            stride *= 4
        else:
            total = total + exchanged(total, "slab", stride)
            stride *= 2
    return total, exchanged(total, "sub", 1)


def finish_kernel(loss_scale, mine_ref, theirs_ref, first_ref, mid_ref, last_ref, head_ref):
    first_core = lax.axis_index("sub") == 0
    taps = 27 * CH
    mine, theirs = mine_ref[...] * loss_scale, theirs_ref[...] * loss_scale
    mid = jnp.where(first_core, theirs, mine)
    last = jnp.where(first_core, mine, theirs)
    mid_ref[...] = mid[:, :taps]
    last_ref[...] = last[:, :taps]
    both = mine[:, 384:] + theirs[:, 384:]
    first_ref[...] = pltpu.roll(both, 80, axis=1)[:, :27]
    head_ref[...] = pltpu.roll(both, 48, axis=1)[:3, : 2 * CH]


def finished(mine, theirs, loss_scale):
    f32 = jnp.float32
    return pl.pallas_call(
        functools.partial(finish_kernel, loss_scale),
        out_shape=(
            jax.ShapeDtypeStruct((CH, 27), f32),
            jax.ShapeDtypeStruct((CH, 27 * CH), f32),
            jax.ShapeDtypeStruct((CH, 27 * CH), f32),
            jax.ShapeDtypeStruct((3, 2 * CH), f32),
        ),
        in_specs=[pl.BlockSpec(memory_space=pltpu.VMEM)] * 2,
        out_specs=(pl.BlockSpec(memory_space=pltpu.VMEM),) * 4,
        compiler_params=pltpu.CompilerParams(vmem_limit_bytes=4 * 1024 * 1024),
        name="finish",
    )(mine, theirs)


def per_device(part_cells, part_offsets, part_counts, w_first, w_mid, w_last, w_head, cotangent):
    n_slab = lax.axis_size("slab")
    n_sub = lax.axis_size("sub")
    axes = ("slab", "sub")
    width_x = cotangent.shape[1]
    width_y = cotangent.shape[2]
    depth_z = cotangent.shape[3]
    cap = part_cells.shape[2]

    def outward(x, by):
        pairs = []
        for i in range(n_slab):
            pairs.append((i * n_sub, (i + by) % n_slab * n_sub))
            pairs.append((i * n_sub + 1, (i - by) % n_slab * n_sub + 1))
        return lax.ppermute(x, axes, pairs)

    raw = side_by_side(w_first, w_mid, w_last, w_head)
    words = packed_slots(part_cells[0], part_offsets[0], part_counts, width_x, width_y, depth_z)
    ct_other = exchanged(cotangent, "sub", 1)
    words, ct_other = lax.optimization_barrier((words, ct_other))
    ct_middle, ct_edge = edges(cotangent, ct_other)
    ct_mine = outward(ct_edge, 1)
    ct_theirs = exchanged(ct_mine, "sub", 1)
    got = lax.all_to_all(words, axes, split_axis=0, concat_axis=0, tiled=True)
    own = deposit(got, ct_mine, raw, cap, width_x, width_y, depth_z)
    near, far = combined(own, exchanged(own, "sub", 1), width_x, width_y)
    mats, wfirst, whead = weight_matrices(raw, far, n_sub * width_y)
    near_mine, far_mine, whead = lax.optimization_barrier((outward(near, 1), outward(far, 2), whead))
    near_theirs, far_theirs = exchanged(near_mine, "sub", 1), exchanged(far_mine, "sub", 1)
    pieces = (near, near_mine, near_theirs, far_mine, far_theirs, ct_middle, ct_mine, ct_theirs)
    force, mine = chain(pieces, mats, wfirst, whead, width_x, width_y, depth_z)
    loss_scale = 1.0 / math.sqrt(width_x * n_slab * width_y * n_sub * depth_z)
    return (force, *finished(*summed(mine), loss_scale))


def solution(mesh):
    in_specs = (
        P(("slab", "sub"), None, None),
        P(("slab", "sub"), None, None, None),
        P(("slab", "sub"), None),
        P(),
        P(),
        P(),
        P(),
        P(None, "slab", "sub", None),
    )
    out_specs = (P(None, "slab", "sub", None), P(), P(), P(), P())
    return jax.shard_map(
        per_device, mesh=mesh, in_specs=in_specs, out_specs=out_specs, check_vma=False
    )
```

time: 1640 us -> 68.9 us (0.04)
  other arithmetic: 1410 us -> 0.8 us
  local copies, waits for them, and re-layouts: 49.8 us -> 0.79 us
  matrix products: 48.5 us -> 0 us
  blocking collectives: 38 us -> 0 us
  Pallas kernels: 0 us -> 25.7 us
  starting transfers between devices: 38.5 us -> 19.7 us
  waiting for transfers between devices: 39.1 us -> 20.9 us
    scatter-add x9 -> x0, other arithmetic: 1390 us -> none  [the longest x8 1390 us: per_device(): padded = padded.at[index.reshape(-1)].add(share.reshape(-1))]
    dot_general x291 -> x0, matrix products: 48.5 us -> none  [the longest x180 29.6 us: conv_planes(): jnp.dot(blocks[:, shift_x, shift_y], piece, preferred_element_type=jnp.fl...]
    psum x1 -> x0, blocking collectives: 38 us -> none  [per_device(): lax.psum((grad_first, grad_mid, grad_last, grad_head), ('slab', 'sub'))]
    pallas_call x0 -> x7, Pallas kernels: none -> 25.7 us  [the longest x1 13.9 us: chain(): pl.pallas_call(functools.partial(chain_kernel, width_x, width_y), out_sha...]
    unnamed x273 -> x2, local copies, waits for them, and re-layouts: 25.8 us -> 0.79 us
    all_to_all x3 -> x1, waiting for transfers between devices: 20.2 us -> 0.16 us  [per_device(): got = lax.all_to_all(words, axes, split_axis=0, concat_axis=0, tiled=True)]
  transfers between devices with their start and end apart: 25 -> 16, of which waited for: 17 -> 13; matrix products, arithmetic and copies ran while one was open for 3% -> 1% of each run, Pallas kernels for 0% -> 8%
where the time goes in v1:
time: 68.9 us; the launch traced here: 68.6 us
  Pallas kernels  25.7 us (37%)
  waiting for transfers between devices  20.9 us (30%)
  starting transfers between devices  19.7 us (29%)
  other arithmetic  0.8 us (1%)
  local copies, waits for them, and re-layouts  0.79 us (1%)
  between operations  0.72 us (1%)
    pallas_call x1, Pallas kernels, chain(): pl.pallas_call(functools.partial(chain_kernel, width_x, width_y), out_sha...  13.9 us
    ppermute x3, waiting for transfers between devices, outward(): return lax.ppermute(x, axes, pairs)  12.1 us
    ppermute x12, starting transfers between devices, exchanged(): lax.ppermute(x, axis, [(i, i ^ mask) for i in range(lax.axis_size(axis))])  9.11 us
    ppermute x12, waiting for transfers between devices, exchanged(): lax.ppermute(x, axis, [(i, i ^ mask) for i in range(lax.axis_size(axis))])  8.63 us
    all_to_all x1, starting transfers between devices, per_device(): got = lax.all_to_all(words, axes, split_axis=0, concat_axis=0, tiled=True)  6.97 us
    pallas_call x1, Pallas kernels, deposit(): pl.pallas_call(functools.partial(deposit_kernel, width_x, width_y, depth_...  5.99 us
    ppermute x3, starting transfers between devices, outward(): return lax.ppermute(x, axes, pairs)  3.63 us
    pallas_call x1, Pallas kernels, weight_matrices(): pl.pallas_call(functools.partial(weights_kernel, full_y), out_shape=(jax....  3.1 us
  transfers between devices with their start and end apart: 16, of which 13 were waited for; matrix products, arithmetic and copies ran while one was open for 1% of the time, Pallas kernels for 8%

profile of v1, /device:TPU:0, one launch (start us, length us, event | category | flops | bytes accessed | tf_op | source)
XLA Modules:
  0.0 68.6 jit_solution(12952123265466778604)
XLA Ops:
  1.1 2.0 %pack.1 = s32[32,1,2560]{2,1,0:T(1,128)} custom-call(s32[32,1024]{1,0:T(8,128)} %bitcast.7, f32[3,32,1024]{2,1,0:T(8,128)} %bitcast.6, s32[1,32]{1,0:T(1,128)} %counts_hbm.1), custom_call_target="tpu_custom_call" | custom-call | tf_op jit(solution)/shard_map/pack/pallas_call | solution.py:46
  3.2 7.0 %all-to-all-start = ((s32[32,1,2560]{2,1,0:T(1,128)}), s32[32,1,2560]{2,1,0:T(1,128)S(1)}, u32[]{:S(2)}, u32[]{:S(2)}) async-start(s32[32,1,2560]{2,1,0:T(1,128)} %pack.1), calls=%async_computation | async-start | bytes 655360 | tf_op jit(solution)/shard_map/all_to_all | solution.py:603
  10.2 0.8 %copy-done = bf16[3,4,8,256]{3,2,1,0:T(8,128)(2,1)S(1)} copy-done((bf16[3,4,8,256]{3,2,1,0:T(8,128)(2,1)S(1)}, bf16[3,4,8,256]{3,2,1,0:T(8,128)(2,1)}, u32[]{:S(2)}) %copy-start) | copy-done | bytes 49176
  11.0 1.8 %collective-permute-start.1 = (bf16[2,48,256]{2,1,0:T(8,128)(2,1)S(1)}, bf16[2,48,256]{2,1,0:T(8,128)(2,1)S(1)}, u32[]{:S(2)}, u32[]{:S(2)}) collective-permute-start(bf16[2,48,256]{2,1,0:T(8,128)(2,1)S(1)} %get-tuple-element.25), channel_id=1, source_target_pairs={{0,2},{1,31},{2,4},{3,1},{4,6},{5,3},{6,8},{7,5},{8,10},{9,7},{10,... | collective-permute-start | bytes 147464 | tf_op jit(solution)/shard_map/ppermute | solution.py:594
  12.8 0.8 %fusion.7.late_ref.raw_ref = bf16[16,1280]{1,0:T(8,128)(2,1)S(1)} fusion(bf16[3,32]{1,0:T(4,128)(2,1)} %param.14, bf16[16,27]{1,0:T(8,128)(2,1)} %param.11, bf16[16,432]{1,0:T(8,128)(2,1)} %param.13, bf16[16,432]{1,0:T(8,128)(2,1)} %param.12), kind=kLoop, calls=%fused_computation.13 | loop fusion | flops 409600 | bytes 69664 | tf_op jit(solution)/shard_map/concatenate | solution.py:262
  13.6 8.9 %collective-permute-done.1.after_ref.ct_mine = bf16[2,48,256]{2,1,0:T(8,128)(2,1)S(1)} collective-permute-done((bf16[2,48,256]{2,1,0:T(8,128)(2,1)S(1)}, bf16[2,48,256]{2,1,0:T(8,128)(2,1)S(1)}, u32[]{:S(2)}, u32[]{:S(2)}) %collective-permute-start.1) | collective-permute-done | bytes 49184 | tf_op jit(solution)/shard_map/ppermute | solution.py:594
  22.7 6.0 %deposit.1.own_ref = f32[48,256]{1,0:T(8,128)S(1)} custom-call(s32[640,128]{1,0:T(8,128)S(1)} %bitcast.5, bf16[2,48,256]{2,1,0:T(8,128)(2,1)S(1)} %collective-permute-done.1.after_ref.ct_mine, bf16[16,1280]{1,0:T(8,128)(2,1)S(1)} %fusion.7.late_ref.raw_ref), custom_call_target="tpu_custom_call" | custom-call | tf_op jit(solution)/shard_map/deposit/pallas_call | solution.py:125
  28.8 1.2 %collective-permute-done.2.other_ref = f32[48,256]{1,0:T(8,128)S(1)} collective-permute-done((f32[48,256]{1,0:T(8,128)S(1)}, f32[48,256]{1,0:T(8,128)S(1)}, u32[]{:S(2)}, u32[]{:S(2)}) %collective-permute-start.2) | collective-permute-done | bytes 49184 | tf_op jit(solution)/shard_map/ppermute | solution.py:534
  30.5 1.3 %collective-permute-start.4 = (f32[32,256]{1,0:T(8,128)S(1)}, f32[32,256]{1,0:T(8,128)S(1)}, u32[]{:S(2)}, u32[]{:S(2)}) collective-permute-start(f32[32,256]{1,0:T(8,128)S(1)} %get-tuple-element.27.after_ref), channel_id=1, source_target_pairs={{0,4},{1,29},{2,6},{3,31},{4,8},{5,1},{6,10},{7,3},{8,12},{9,5},{1... | collective-permute-start | bytes 98312 | tf_op jit(solution)/shard_map/ppermute | solution.py:594
  31.8 3.1 %weights.1 = (bf16[4,3,768,256]{3,2,1,0:T(8,128)(2,1)S(1)}, bf16[144,256]{1,0:T(8,128)(2,1)S(1)}, bf16[2,48,256]{2,1,0:T(8,128)(2,1)S(1)}) custom-call(bf16[16,1280]{1,0:T(8,128)(2,1)S(1)} %fusion.7.late_ref.raw_ref, f32[32,256]{1,0:T(8,128)S(1)} %get-tuple-element.27.after_ref), custom_call_target="tpu_custom_call" | custom-call | flops 603979776 | bytes 8388608 | tf_op jit(solution)/shard_map/weights/pallas_call | solution.py:267
  34.9 2.2 %collective-permute-done.4.far_mine = f32[32,256]{1,0:T(8,128)S(1)} collective-permute-done((f32[32,256]{1,0:T(8,128)S(1)}, f32[32,256]{1,0:T(8,128)S(1)}, u32[]{:S(2)}, u32[]{:S(2)}) %collective-permute-start.4) | collective-permute-done | bytes 32800 | tf_op jit(solution)/shard_map/ppermute | solution.py:594
  37.1 1.0 %collective-permute-done.3.near_mine = f32[80,256]{1,0:T(8,128)S(1)} collective-permute-done((f32[80,256]{1,0:T(8,128)S(1)}, f32[80,256]{1,0:T(8,128)S(1)}, u32[]{:S(2)}, u32[]{:S(2)}) %collective-permute-start.3) | collective-permute-done | bytes 81952 | tf_op jit(solution)/shard_map/ppermute | solution.py:594
  38.6 0.9 %collective-permute-done.7.ct_theirs = bf16[2,48,256]{2,1,0:T(8,128)(2,1)S(1)} collective-permute-done((bf16[2,48,256]{2,1,0:T(8,128)(2,1)S(1)}, bf16[2,48,256]{2,1,0:T(8,128)(2,1)S(1)}, u32[]{:S(2)}, u32[]{:S(2)}) %collective-permute-start.7) | collective-permute-done | bytes 49184 | tf_op jit(solution)/shard_map/ppermute | solution.py:534
  39.8 13.9 %chain.1 = (bf16[3,4,8,256]{3,2,1,0:T(8,128)(2,1)}, f32[16,512]{1,0:T(8,128)S(1)}) custom-call(f32[80,256]{1,0:T(8,128)S(1)} %get-tuple-element.26.near_ref, f32[80,256]{1,0:T(8,128)S(1)} %collective-permute-done.3.near_mine, f32[80,256]{1,0:T(8,128)S(1)} %collective-permute-done.5.near_theirs, f32[32,256]{1,0:T(8,128)S(1)} %collective-permute-done.4.far_mine, ...), custom_call_target="tpu_custom_call" | custom-call | tf_op jit(solution)/shard_map/chain/pallas_call | solution.py:505
  53.7 2.4 %collective-permute-start.9 = (f32[16,512]{1,0:T(8,128)S(1)}, f32[16,512]{1,0:T(8,128)S(1)}, u32[]{:S(2)}, u32[]{:S(2)}) collective-permute-start(f32[16,512]{1,0:T(8,128)S(1)} %get-tuple-element.36), channel_id=1, source_target_pairs={{0,4},{2,6},{4,0},{6,2},{8,12},{10,14},{12,8},{14,10},{16,20},{18,... | collective-permute-start | bytes 98312 | tf_op jit(solution)/shard_map/ppermute | solution.py:534
  56.1 1.1 %collective-permute-start.8 = (f32[16,512]{1,0:T(8,128)S(1)}, f32[16,512]{1,0:T(8,128)S(1)}, u32[]{:S(2)}, u32[]{:S(2)}) collective-permute-start(f32[16,512]{1,0:T(8,128)S(1)} %get-tuple-element.36), channel_id=1, source_target_pairs={{0,2},{2,0},{4,6},{6,4},{8,10},{10,8},{12,14},{14,12},{16,18},{18,... | collective-permute-start | bytes 98312 | tf_op jit(solution)/shard_map/ppermute | solution.py:534
  57.2 1.5 %collective-permute-done.10 = f32[16,512]{1,0:T(8,128)S(1)} collective-permute-done((f32[16,512]{1,0:T(8,128)S(1)}, f32[16,512]{1,0:T(8,128)S(1)}, u32[]{:S(2)}, u32[]{:S(2)}) %collective-permute-start.10) | collective-permute-done | bytes 32800 | tf_op jit(solution)/shard_map/ppermute | solution.py:534
  58.7 1.3 %collective-permute-done.8 = f32[16,512]{1,0:T(8,128)S(1)} collective-permute-done((f32[16,512]{1,0:T(8,128)S(1)}, f32[16,512]{1,0:T(8,128)S(1)}, u32[]{:S(2)}, u32[]{:S(2)}) %collective-permute-start.8) | collective-permute-done | bytes 32800 | tf_op jit(solution)/shard_map/ppermute | solution.py:534
  60.0 1.1 %collective-permute-start.13 = (f32[16,512]{1,0:T(8,128)S(1)}, f32[16,512]{1,0:T(8,128)S(1)}, u32[]{:S(2)}, u32[]{:S(2)}) collective-permute-start(f32[16,512]{1,0:T(8,128)S(1)} %add_add_fusion.1), channel_id=1, source_target_pairs={{0,24},{2,26},{4,28},{6,30},{8,16},{10,18},{12,20},{14,22},{16,8},... | collective-permute-start | bytes 98312 | tf_op jit(solution)/shard_map/ppermute | solution.py:534
  61.1 3.4 %collective-permute-start.11 = (f32[16,512]{1,0:T(8,128)S(1)}, f32[16,512]{1,0:T(8,128)S(1)}, u32[]{:S(2)}, u32[]{:S(2)}) collective-permute-start(f32[16,512]{1,0:T(8,128)S(1)} %add_add_fusion.1), channel_id=1, source_target_pairs={{0,8},{2,10},{4,12},{6,14},{8,0},{10,2},{12,4},{14,6},{16,24},{18,... | collective-permute-start | bytes 98312 | tf_op jit(solution)/shard_map/ppermute | solution.py:534
  64.5 1.4 %collective-permute-done.13 = f32[16,512]{1,0:T(8,128)S(1)} collective-permute-done((f32[16,512]{1,0:T(8,128)S(1)}, f32[16,512]{1,0:T(8,128)S(1)}, u32[]{:S(2)}, u32[]{:S(2)}) %collective-permute-start.13) | collective-permute-done | bytes 32800 | tf_op jit(solution)/shard_map/ppermute | solution.py:534
  65.8 0.8 %collective-permute-done.12 = f32[16,512]{1,0:T(8,128)S(1)} collective-permute-done((f32[16,512]{1,0:T(8,128)S(1)}, f32[16,512]{1,0:T(8,128)S(1)}, u32[]{:S(2)}, u32[]{:S(2)}) %collective-permute-start.12) | collective-permute-done | bytes 32800 | tf_op jit(solution)/shard_map/ppermute | solution.py:534
  66.7 1.2 %collective-permute-done.14.theirs_ref = f32[16,512]{1,0:T(8,128)S(1)} collective-permute-done((f32[16,512]{1,0:T(8,128)S(1)}, f32[16,512]{1,0:T(8,128)S(1)}, u32[]{:S(2)}, u32[]{:S(2)}) %collective-permute-start.14) | collective-permute-done | bytes 32800 | tf_op jit(solution)/shard_map/ppermute | solution.py:534
  67.9 0.7 finish.1
  (20 shorter events, 2.3 us)
Async XLA Ops:
  0.6 2.6 %collective-permute-start = (bf16[3,4,8,256]{3,2,1,0:T(8,128)(2,1)}, bf16[3,4,8,256]{3,2,1,0:T(8,128)(2,1)S(1)}, u32[]{:S(2)}, u32[]{:S(2)}) collective-permute-start(bf16[3,4,8,256]{3,2,1,0:T(8,128)(2,1)} %own_ref.1), channel_id=1, source_target_pairs={{0,1},{1,0},{2,3},{3,2},{4,5},{5,4},{6,7},{7,6},{8,9},{9,8},{10,11... | collective-permute-start | bytes 147464 | tf_op jit(solution)/shard_map/ppermute | solution.py:534
  3.2 19.5 %all-to-all-start = ((s32[32,1,2560]{2,1,0:T(1,128)}), s32[32,1,2560]{2,1,0:T(1,128)S(1)}, u32[]{:S(2)}, u32[]{:S(2)}) async-start(s32[32,1,2560]{2,1,0:T(1,128)} %pack.1), calls=%async_computation | async-start | bytes 655360 | tf_op jit(solution)/shard_map/all_to_all | solution.py:603
  10.2 0.8 %copy-start = (bf16[3,4,8,256]{3,2,1,0:T(8,128)(2,1)S(1)}, bf16[3,4,8,256]{3,2,1,0:T(8,128)(2,1)}, u32[]{:S(2)}) copy-start(bf16[3,4,8,256]{3,2,1,0:T(8,128)(2,1)} %own_ref.1) | copy-start | bytes 147460
  11.0 11.5 %collective-permute-start.1 = (bf16[2,48,256]{2,1,0:T(8,128)(2,1)S(1)}, bf16[2,48,256]{2,1,0:T(8,128)(2,1)S(1)}, u32[]{:S(2)}, u32[]{:S(2)}) collective-permute-start(bf16[2,48,256]{2,1,0:T(8,128)(2,1)S(1)} %get-tuple-element.25), channel_id=1, source_target_pairs={{0,2},{1,31},{2,4},{3,1},{4,6},{5,3},{6,8},{7,5},{8,10},{9,7},{10,... | collective-permute-start | bytes 147464 | tf_op jit(solution)/shard_map/ppermute | solution.py:594
  28.7 1.3 %collective-permute-start.2 = (f32[48,256]{1,0:T(8,128)S(1)}, f32[48,256]{1,0:T(8,128)S(1)}, u32[]{:S(2)}, u32[]{:S(2)}) collective-permute-start(f32[48,256]{1,0:T(8,128)S(1)} %deposit.1.own_ref), channel_id=1, source_target_pairs={{0,1},{1,0},{2,3},{3,2},{4,5},{5,4},{6,7},{7,6},{8,9},{9,8},{10,11... | collective-permute-start | bytes 147464 | tf_op jit(solution)/shard_map/ppermute | solution.py:534
  30.0 8.1 %collective-permute-start.3 = (f32[80,256]{1,0:T(8,128)S(1)}, f32[80,256]{1,0:T(8,128)S(1)}, u32[]{:S(2)}, u32[]{:S(2)}) collective-permute-start(f32[80,256]{1,0:T(8,128)S(1)} %get-tuple-element.26.near_ref), channel_id=1, source_target_pairs={{0,2},{1,31},{2,4},{3,1},{4,6},{5,3},{6,8},{7,5},{8,10},{9,7},{10,... | collective-permute-start | bytes 245768 | tf_op jit(solution)/shard_map/ppermute | solution.py:594
  30.5 6.6 %collective-permute-start.4 = (f32[32,256]{1,0:T(8,128)S(1)}, f32[32,256]{1,0:T(8,128)S(1)}, u32[]{:S(2)}, u32[]{:S(2)}) collective-permute-start(f32[32,256]{1,0:T(8,128)S(1)} %get-tuple-element.27.after_ref), channel_id=1, source_target_pairs={{0,4},{1,29},{2,6},{3,31},{4,8},{5,1},{6,10},{7,3},{8,12},{9,5},{1... | collective-permute-start | bytes 98312 | tf_op jit(solution)/shard_map/ppermute | solution.py:594
  38.1 1.7 %collective-permute-start.5 = (f32[80,256]{1,0:T(8,128)S(1)}, f32[80,256]{1,0:T(8,128)S(1)}, u32[]{:S(2)}, u32[]{:S(2)}) collective-permute-start(f32[80,256]{1,0:T(8,128)S(1)} %collective-permute-done.3.near_mine), channel_id=1, source_target_pairs={{0,1},{1,0},{2,3},{3,2},{4,5},{5,4},{6,7},{7,6},{8,9},{9,8},{10,11... | collective-permute-start | bytes 245768 | tf_op jit(solution)/shard_map/ppermute | solution.py:534
  38.1 1.4 %collective-permute-start.7 = (bf16[2,48,256]{2,1,0:T(8,128)(2,1)S(1)}, bf16[2,48,256]{2,1,0:T(8,128)(2,1)S(1)}, u32[]{:S(2)}, u32[]{:S(2)}) collective-permute-start(bf16[2,48,256]{2,1,0:T(8,128)(2,1)S(1)} %collective-permute-done.1.after_ref.ct_mine), channel_id=1, source_target_pairs={{0,1},{1,0},{2,3},{3,2},{4,5},{5,4},{6,7},{7,6},{8,9},{9,8},{10,11... | collective-permute-start | bytes 147464 | tf_op jit(solution)/shard_map/ppermute | solution.py:534
  38.6 1.2 %collective-permute-start.6 = (f32[32,256]{1,0:T(8,128)S(1)}, f32[32,256]{1,0:T(8,128)S(1)}, u32[]{:S(2)}, u32[]{:S(2)}) collective-permute-start(f32[32,256]{1,0:T(8,128)S(1)} %collective-permute-done.4.far_mine), channel_id=1, source_target_pairs={{0,1},{1,0},{2,3},{3,2},{4,5},{5,4},{6,7},{7,6},{8,9},{9,8},{10,11... | collective-permute-start | bytes 98312 | tf_op jit(solution)/shard_map/ppermute | solution.py:534
  53.7 5.0 %collective-permute-start.10 = (f32[16,512]{1,0:T(8,128)S(1)}, f32[16,512]{1,0:T(8,128)S(1)}, u32[]{:S(2)}, u32[]{:S(2)}) collective-permute-start(f32[16,512]{1,0:T(8,128)S(1)} %get-tuple-element.36), channel_id=1, source_target_pairs={{0,6},{2,4},{4,2},{6,0},{8,14},{10,12},{12,10},{14,8},{16,22},{18,... | collective-permute-start | bytes 98312 | tf_op jit(solution)/shard_map/ppermute | solution.py:534
  53.7 5.0 %collective-permute-start.9 = (f32[16,512]{1,0:T(8,128)S(1)}, f32[16,512]{1,0:T(8,128)S(1)}, u32[]{:S(2)}, u32[]{:S(2)}) collective-permute-start(f32[16,512]{1,0:T(8,128)S(1)} %get-tuple-element.36), channel_id=1, source_target_pairs={{0,4},{2,6},{4,0},{6,2},{8,12},{10,14},{12,8},{14,10},{16,20},{18,... | collective-permute-start | bytes 98312 | tf_op jit(solution)/shard_map/ppermute | solution.py:534
  56.1 3.9 %collective-permute-start.8 = (f32[16,512]{1,0:T(8,128)S(1)}, f32[16,512]{1,0:T(8,128)S(1)}, u32[]{:S(2)}, u32[]{:S(2)}) collective-permute-start(f32[16,512]{1,0:T(8,128)S(1)} %get-tuple-element.36), channel_id=1, source_target_pairs={{0,2},{2,0},{4,6},{6,4},{8,10},{10,8},{12,14},{14,12},{16,18},{18,... | collective-permute-start | bytes 98312 | tf_op jit(solution)/shard_map/ppermute | solution.py:534
  60.0 5.8 %collective-permute-start.13 = (f32[16,512]{1,0:T(8,128)S(1)}, f32[16,512]{1,0:T(8,128)S(1)}, u32[]{:S(2)}, u32[]{:S(2)}) collective-permute-start(f32[16,512]{1,0:T(8,128)S(1)} %add_add_fusion.1), channel_id=1, source_target_pairs={{0,24},{2,26},{4,28},{6,30},{8,16},{10,18},{12,20},{14,22},{16,8},... | collective-permute-start | bytes 98312 | tf_op jit(solution)/shard_map/ppermute | solution.py:534
  61.1 5.5 %collective-permute-start.12 = (f32[16,512]{1,0:T(8,128)S(1)}, f32[16,512]{1,0:T(8,128)S(1)}, u32[]{:S(2)}, u32[]{:S(2)}) collective-permute-start(f32[16,512]{1,0:T(8,128)S(1)} %add_add_fusion.1), channel_id=1, source_target_pairs={{0,16},{2,18},{4,20},{6,22},{8,24},{10,26},{12,28},{14,30},{16,0},... | collective-permute-start | bytes 98312 | tf_op jit(solution)/shard_map/ppermute | solution.py:534
  61.1 5.6 %collective-permute-start.11 = (f32[16,512]{1,0:T(8,128)S(1)}, f32[16,512]{1,0:T(8,128)S(1)}, u32[]{:S(2)}, u32[]{:S(2)}) collective-permute-start(f32[16,512]{1,0:T(8,128)S(1)} %add_add_fusion.1), channel_id=1, source_target_pairs={{0,8},{2,10},{4,12},{6,14},{8,0},{10,2},{12,4},{14,6},{16,24},{18,... | collective-permute-start | bytes 98312 | tf_op jit(solution)/shard_map/ppermute | solution.py:534
  66.7 1.3 %collective-permute-start.14 = (f32[16,512]{1,0:T(8,128)S(1)}, f32[16,512]{1,0:T(8,128)S(1)}, u32[]{:S(2)}, u32[]{:S(2)}) collective-permute-start(f32[16,512]{1,0:T(8,128)S(1)} %add_add_fusion.mine_ref), channel_id=1, source_target_pairs={{0,1},{1,0},{2,3},{3,2},{4,5},{5,4},{6,7},{7,6},{8,9},{9,8},{10,11... | collective-permute-start | bytes 98312 | tf_op jit(solution)/shard_map/ppermute | solution.py:534

commit v2 on v1

--- a/solution.py
+++ b/solution.py
@@ -114,7 +114,7 @@
         )
         return carry
 
-    lax.fori_loop(0, words_ref.shape[0] // (group * source_rows), body, 0, unroll=8)
+    lax.fori_loop(0, words_ref.shape[0] // (group * source_rows), body, 0, unroll=16)
     low = acc_ref[0:rows] + acc_ref[rows : 2 * rows]
     high = acc_ref[2 * rows : 3 * rows] + acc_ref[3 * rows : 4 * rows]
     out_ref[...] = low + pltpu.roll(high, 1, axis=1)
@@ -331,9 +331,11 @@
     mine_ref,
     ct_ref,
     dens,
-    fields,
+    one,
+    two,
     three,
-    grads,
+    g_three,
+    g_two,
     pre_one,
     pre_two,
     wg,
@@ -381,76 +383,98 @@
         ref[x, :, lanes : 2 * lanes] = field.astype(jnp.bfloat16)
         ref[x, :, 2 * lanes : 3 * lanes] = pltpu.roll(field, depth - 1, axis=0).astype(jnp.bfloat16)
 
-    def conv(ref, x, which, columns=lanes):
-        field = jnp.concatenate([ref[x + dx : x + dx + 2].reshape(2 * depth, 3 * lanes) for dx in range(3)], axis=1)
-        weights = mats_ref[which].reshape(9 * lanes, lanes)[:, 0:columns]
-        return dot(field, weights).reshape(2, depth, columns)
+    def conv(ref, x, which):
+        total = None
+        for dx in range(3):
+            part = dot(ref[x + dx : x + dx + 2].reshape(2 * depth, 3 * lanes), mats_ref[which, dx])
+            total = part if total is None else total + part
+        return total.reshape(2, depth, lanes)
 
     def slope(v):
         s = sigmoid(v)
         return s * (1.0 + v * (1.0 - s))
 
-    one, two = 0, n_dens - 2
-    g_three, g_two = 0, n_dens - 6
-
-    for x in range(n_dens - 2):
+    def first_plane(x):
         v = dot(window(x), wfirst_ref[...], ((0,), (0,)))
         if 0 <= x - 4 < width_x:
             pre_one[x - 4] = v[:, 0:own]
-        put(fields, one + x, v * sigmoid(v))
-
-    for i in range((n_dens - 4) // 2):
-        both = conv(fields, one + 2 * i, 0)
+        put(one, x, v * sigmoid(v))
+
+    def second_done(i, both):
         for k in range(2):
             v, x = both[k], 2 * i + k
             if 0 <= x - 2 < width_x + 2:
                 pre_two[x - 2] = v
-            put(fields, two + x, v * sigmoid(v))
-
-    for i in range((n_dens - 6) // 2):
-        both = conv(fields, two + 2 * i, 1)
+            put(two, x, v * sigmoid(v))
+
+    def third_done(i, both):
         for k in range(2):
             v, x = both[k], 2 * i + k
             s = sigmoid(v)
             if 0 <= x - 2 < width_x:
                 three[x - 2] = (v * s).astype(jnp.bfloat16)
             back = dot(ct_ref[x], whead_ref[0], ((0,), (0,)))
-            put(grads, g_three + x, back * (s * (1.0 + v * (1.0 - s))))
+            put(g_three, x, back * (s * (1.0 + v * (1.0 - s))))
+
+    def back_done(i, both):
+        for k in range(2):
+            x = 2 * i + k
+            put(g_two, x, both[k] * slope(pre_two[x]))
+
+    layers = ((one, 0, second_done), (two, 1, third_done), (g_three, 3, back_done))
+    pairs = [(n_dens - 4 - 2 * layer) // 2 for layer in range(3)]
+    order = sorted(
+        ((i + 2.6 * layer, layer, i) for layer in range(3) for i in range(pairs[layer])),
+    )
+    firsts_done = 0
+    waiting = None
+    for _, layer, i in order:
+        if layer == 0:
+            while firsts_done < 2 * i + 4:
+                first_plane(firsts_done)
+                firsts_done += 1
+        elif waiting is not None and waiting[0] == layer - 1 and waiting[1] <= i + 1:
+            layers[waiting[0]][2](waiting[1], waiting[2])
+            waiting = None
+        ref, which, done = layers[layer]
+        both = conv(ref, 2 * i, which)
+        if waiting is not None:
+            layers[waiting[0]][2](waiting[1], waiting[2])
+        waiting = (layer, i, both)
+    layers[waiting[0]][2](waiting[1], waiting[2])
 
     ct_own = jnp.concatenate([ct_ref[x + 2] for x in range(width_x)], axis=1)
     heads = [
         dot(ct_own, three[:, :, 0:own].reshape(width_x * depth, own)),
-        dot(ct_own, fields[one + 4 : one + 4 + width_x, :, lanes : lanes + own].reshape(width_x * depth, own)),
+        dot(ct_own, one[4 : 4 + width_x, :, lanes : lanes + own].reshape(width_x * depth, own)),
     ]
     for x in range(width_x):
-        h_three, h_one = three[x], fields[one + x + 4, :, lanes : 2 * lanes]
-        rows = dot(whead_ref[0], h_three, ((1,), (1,))) + dot(whead_ref[1], h_one, ((1,), (1,)))
+        h_three, h_one = three[x], one[x + 4, :, lanes : 2 * lanes]
+        rows = dot(h_three, whead_ref[0], ((1,), (1,))) + dot(h_one, whead_ref[1], ((1,), (1,)))
+        rows = jnp.transpose(rows)
         for k in range(3):
             force_ref[k, x] = rows[k * full_y : k * full_y + width_y].astype(jnp.bfloat16)
 
-    for i in range((width_x + 2) // 2):
-        both = conv(grads, g_three + 2 * i, 3)
+    across = []
+    for x in range(width_x):
+        middle = slice(lanes, 2 * lanes)
+        across.append(jnp.transpose(jnp.where(first_core, g_three[x + 2, :, middle], g_two[x + 1, :, middle])))
+    across = jnp.concatenate(across, axis=1)
+    for dx in range(3):
+        field = jnp.where(first_core, two[2 + dx : 2 + dx + width_x], one[3 + dx : 3 + dx + width_x])
+        wg[dx] = dot(across, field.reshape(width_x * depth, 3 * lanes))
+    grad_one = []
+    for i in range(width_x // 2):
+        total = jnp.zeros((depth, 2 * own), jnp.float32)
+        for plane in range(4):
+            nothing = jnp.zeros((3 * lanes, own), jnp.bfloat16)
+            left = mats_ref[2, plane, :, 0:own] if plane < 3 else nothing
+            right = mats_ref[2, plane - 1, :, 0:own] if plane > 0 else nothing
+            total = total + dot(g_two[2 * i + plane], jnp.concatenate([left, right], axis=1))
         for k in range(2):
             x = 2 * i + k
-            put(grads, g_two + x, both[k] * slope(pre_two[x]))
-
-    grad_base = jnp.where(first_core, g_three + 2, g_two + 1)
-    field_base = jnp.where(first_core, two + 2, one + 3)
-    across = []
-    for x in range(width_x):
-        grad = grads[grad_base + x, :, lanes : 2 * lanes].astype(jnp.float32)
-        across.append(jnp.transpose(grad).astype(jnp.bfloat16))
-    across = jnp.concatenate(across, axis=1)
-    for dx in range(3):
-        field = fields[pl.ds(field_base + dx, width_x)].reshape(width_x * depth, 3 * lanes)
-        wg[dx] = dot(across, field)
-    grad_one = []
-    for i in range(width_x // 2):
-        both = conv(grads, g_two + 2 * i, 2, own)
-        for k in range(2):
-            x = 2 * i + k
-            total = both[k] + dot(ct_ref[x + 2], whead_ref[1, :, 0:own], ((0,), (0,)))
-            grad_one.append((total * slope(pre_one[x])).astype(jnp.bfloat16))
+            back = total[:, k * own : (k + 1) * own] + dot(ct_ref[x + 2], whead_ref[1, :, 0:own], ((0,), (0,)))
+            grad_one.append((back * slope(pre_one[x])).astype(jnp.bfloat16))
     windows = jnp.concatenate([window(x + 4) for x in range(width_x)], axis=1)
     firsts = dot(windows, jnp.concatenate(grad_one, axis=0))
 
@@ -513,9 +537,11 @@
         scratch_shapes=[
             pltpu.VMEM((width_x + 4, 3 * full_y, depth_z), bf16),
             pltpu.VMEM((n_dens * 3 * full_y, depth_z), bf16),
-            pltpu.VMEM((2 * n_dens - 6, depth_z, 3 * lanes), bf16),
+            pltpu.VMEM((n_dens - 2, depth_z, 3 * lanes), bf16),
+            pltpu.VMEM((n_dens - 4, depth_z, 3 * lanes), bf16),
             pltpu.VMEM((width_x, depth_z, lanes), bf16),
-            pltpu.VMEM((2 * n_dens - 14, depth_z, 3 * lanes), bf16),
+            pltpu.VMEM((n_dens - 6, depth_z, 3 * lanes), bf16),
+            pltpu.VMEM((n_dens - 8, depth_z, 3 * lanes), bf16),
             pltpu.VMEM((width_x, depth_z, own), f32),
             pltpu.VMEM((width_x + 2, depth_z, lanes), f32),
             pltpu.VMEM((3, lanes, 3 * lanes), f32),

time: 68.9 us -> 67.8 us (0.984)
  Pallas kernels: 25.7 us -> 24.5 us
    pallas_call x1, Pallas kernels: 13.9 us -> 12.9 us  [chain(): pl.pallas_call(functools.partial(chain_kernel, width_x, width_y), out_sha...]
where the time goes in v2:
time: 67.8 us; the launch traced here: 67.4 us
  Pallas kernels  24.5 us (36%)
  waiting for transfers between devices  20.9 us (31%)
  starting transfers between devices  19.7 us (29%)
  other arithmetic  0.8 us (1%)
  local copies, waits for them, and re-layouts  0.79 us (1%)
  between operations  0.72 us (1%)
    pallas_call x1, Pallas kernels, chain(): pl.pallas_call(functools.partial(chain_kernel, width_x, width_y), out_sha...  12.9 us
    ppermute x3, waiting for transfers between devices, outward(): return lax.ppermute(x, axes, pairs)  12.1 us
    ppermute x12, starting transfers between devices, exchanged(): lax.ppermute(x, axis, [(i, i ^ mask) for i in range(lax.axis_size(axis))])  9.11 us
    ppermute x12, waiting for transfers between devices, exchanged(): lax.ppermute(x, axis, [(i, i ^ mask) for i in range(lax.axis_size(axis))])  8.62 us
    all_to_all x1, starting transfers between devices, per_device(): got = lax.all_to_all(words, axes, split_axis=0, concat_axis=0, tiled=True)  6.97 us
    pallas_call x1, Pallas kernels, deposit(): pl.pallas_call(functools.partial(deposit_kernel, width_x, width_y, depth_...  5.83 us
    ppermute x3, starting transfers between devices, outward(): return lax.ppermute(x, axes, pairs)  3.63 us
    pallas_call x1, Pallas kernels, weight_matrices(): pl.pallas_call(functools.partial(weights_kernel, full_y), out_shape=(jax....  3.1 us
  transfers between devices with their start and end apart: 16, of which 13 were waited for; matrix products, arithmetic and copies ran while one was open for 1% of the time, Pallas kernels for 8%

profile of v2, /device:TPU:0, one launch (start us, length us, event | category | flops | bytes accessed | tf_op | source)
XLA Modules:
  0.0 67.4 jit_solution(1330728129591485929)
XLA Ops:
  1.1 2.0 %pack.1 = s32[32,1,2560]{2,1,0:T(1,128)} custom-call(s32[32,1024]{1,0:T(8,128)} %bitcast.7, f32[3,32,1024]{2,1,0:T(8,128)} %bitcast.6, s32[1,32]{1,0:T(1,128)} %counts_hbm.1), custom_call_target="tpu_custom_call" | custom-call | tf_op jit(solution)/shard_map/pack/pallas_call | solution.py:46
  3.2 7.0 %all-to-all-start = ((s32[32,1,2560]{2,1,0:T(1,128)}), s32[32,1,2560]{2,1,0:T(1,128)S(1)}, u32[]{:S(2)}, u32[]{:S(2)}) async-start(s32[32,1,2560]{2,1,0:T(1,128)} %pack.1), calls=%async_computation | async-start | bytes 655360 | tf_op jit(solution)/shard_map/all_to_all | solution.py:629
  10.2 0.8 %copy-done = bf16[3,4,8,256]{3,2,1,0:T(8,128)(2,1)S(1)} copy-done((bf16[3,4,8,256]{3,2,1,0:T(8,128)(2,1)S(1)}, bf16[3,4,8,256]{3,2,1,0:T(8,128)(2,1)}, u32[]{:S(2)}) %copy-start) | copy-done | bytes 49176
  11.0 1.8 %collective-permute-start.1 = (bf16[2,48,256]{2,1,0:T(8,128)(2,1)S(1)}, bf16[2,48,256]{2,1,0:T(8,128)(2,1)S(1)}, u32[]{:S(2)}, u32[]{:S(2)}) collective-permute-start(bf16[2,48,256]{2,1,0:T(8,128)(2,1)S(1)} %get-tuple-element.25), channel_id=1, source_target_pairs={{0,2},{1,31},{2,4},{3,1},{4,6},{5,3},{6,8},{7,5},{8,10},{9,7},{10,... | collective-permute-start | bytes 147464 | tf_op jit(solution)/shard_map/ppermute | solution.py:620
  12.8 0.8 %fusion.7.late_ref.raw_ref = bf16[16,1280]{1,0:T(8,128)(2,1)S(1)} fusion(bf16[3,32]{1,0:T(4,128)(2,1)} %param.14, bf16[16,27]{1,0:T(8,128)(2,1)} %param.11, bf16[16,432]{1,0:T(8,128)(2,1)} %param.13, bf16[16,432]{1,0:T(8,128)(2,1)} %param.12), kind=kLoop, calls=%fused_computation.13 | loop fusion | flops 409600 | bytes 69664 | tf_op jit(solution)/shard_map/concatenate | solution.py:262
  13.6 8.9 %collective-permute-done.1.after_ref.ct_mine = bf16[2,48,256]{2,1,0:T(8,128)(2,1)S(1)} collective-permute-done((bf16[2,48,256]{2,1,0:T(8,128)(2,1)S(1)}, bf16[2,48,256]{2,1,0:T(8,128)(2,1)S(1)}, u32[]{:S(2)}, u32[]{:S(2)}) %collective-permute-start.1) | collective-permute-done | bytes 49184 | tf_op jit(solution)/shard_map/ppermute | solution.py:620
  22.7 5.8 %deposit.1.own_ref = f32[48,256]{1,0:T(8,128)S(1)} custom-call(s32[640,128]{1,0:T(8,128)S(1)} %bitcast.5, bf16[2,48,256]{2,1,0:T(8,128)(2,1)S(1)} %collective-permute-done.1.after_ref.ct_mine, bf16[16,1280]{1,0:T(8,128)(2,1)S(1)} %fusion.7.late_ref.raw_ref), custom_call_target="tpu_custom_call" | custom-call | tf_op jit(solution)/shard_map/deposit/pallas_call | solution.py:125
  28.6 1.2 %collective-permute-done.2.other_ref = f32[48,256]{1,0:T(8,128)S(1)} collective-permute-done((f32[48,256]{1,0:T(8,128)S(1)}, f32[48,256]{1,0:T(8,128)S(1)}, u32[]{:S(2)}, u32[]{:S(2)}) %collective-permute-start.2) | collective-permute-done | bytes 49184 | tf_op jit(solution)/shard_map/ppermute | solution.py:560
  30.3 1.3 %collective-permute-start.4 = (f32[32,256]{1,0:T(8,128)S(1)}, f32[32,256]{1,0:T(8,128)S(1)}, u32[]{:S(2)}, u32[]{:S(2)}) collective-permute-start(f32[32,256]{1,0:T(8,128)S(1)} %get-tuple-element.27.after_ref), channel_id=1, source_target_pairs={{0,4},{1,29},{2,6},{3,31},{4,8},{5,1},{6,10},{7,3},{8,12},{9,5},{1... | collective-permute-start | bytes 98312 | tf_op jit(solution)/shard_map/ppermute | solution.py:620
  31.7 3.1 %weights.1 = (bf16[4,3,768,256]{3,2,1,0:T(8,128)(2,1)S(1)}, bf16[144,256]{1,0:T(8,128)(2,1)S(1)}, bf16[2,48,256]{2,1,0:T(8,128)(2,1)S(1)}) custom-call(bf16[16,1280]{1,0:T(8,128)(2,1)S(1)} %fusion.7.late_ref.raw_ref, f32[32,256]{1,0:T(8,128)S(1)} %get-tuple-element.27.after_ref), custom_call_target="tpu_custom_call" | custom-call | flops 603979776 | bytes 8388608 | tf_op jit(solution)/shard_map/weights/pallas_call | solution.py:267
  34.8 2.2 %collective-permute-done.4.far_mine = f32[32,256]{1,0:T(8,128)S(1)} collective-permute-done((f32[32,256]{1,0:T(8,128)S(1)}, f32[32,256]{1,0:T(8,128)S(1)}, u32[]{:S(2)}, u32[]{:S(2)}) %collective-permute-start.4) | collective-permute-done | bytes 32800 | tf_op jit(solution)/shard_map/ppermute | solution.py:620
  37.0 1.0 %collective-permute-done.3.near_mine = f32[80,256]{1,0:T(8,128)S(1)} collective-permute-done((f32[80,256]{1,0:T(8,128)S(1)}, f32[80,256]{1,0:T(8,128)S(1)}, u32[]{:S(2)}, u32[]{:S(2)}) %collective-permute-start.3) | collective-permute-done | bytes 81952 | tf_op jit(solution)/shard_map/ppermute | solution.py:620
  38.5 0.9 %collective-permute-done.7.ct_theirs = bf16[2,48,256]{2,1,0:T(8,128)(2,1)S(1)} collective-permute-done((bf16[2,48,256]{2,1,0:T(8,128)(2,1)S(1)}, bf16[2,48,256]{2,1,0:T(8,128)(2,1)S(1)}, u32[]{:S(2)}, u32[]{:S(2)}) %collective-permute-start.7) | collective-permute-done | bytes 49184 | tf_op jit(solution)/shard_map/ppermute | solution.py:560
  39.7 12.9 %chain.1 = (bf16[3,4,8,256]{3,2,1,0:T(8,128)(2,1)}, f32[16,512]{1,0:T(8,128)S(1)}) custom-call(f32[80,256]{1,0:T(8,128)S(1)} %get-tuple-element.26.near_ref, f32[80,256]{1,0:T(8,128)S(1)} %collective-permute-done.3.near_mine, f32[80,256]{1,0:T(8,128)S(1)} %collective-permute-done.5.near_theirs, f32[32,256]{1,0:T(8,128)S(1)} %collective-permute-done.4.far_mine, ...), custom_call_target="tpu_custom_call" | custom-call | tf_op jit(solution)/shard_map/chain/pallas_call | solution.py:529
  52.5 2.4 %collective-permute-start.9 = (f32[16,512]{1,0:T(8,128)S(1)}, f32[16,512]{1,0:T(8,128)S(1)}, u32[]{:S(2)}, u32[]{:S(2)}) collective-permute-start(f32[16,512]{1,0:T(8,128)S(1)} %get-tuple-element.36), channel_id=1, source_target_pairs={{0,4},{2,6},{4,0},{6,2},{8,12},{10,14},{12,8},{14,10},{16,20},{18,... | collective-permute-start | bytes 98312 | tf_op jit(solution)/shard_map/ppermute | solution.py:560
  54.9 1.1 %collective-permute-start.8 = (f32[16,512]{1,0:T(8,128)S(1)}, f32[16,512]{1,0:T(8,128)S(1)}, u32[]{:S(2)}, u32[]{:S(2)}) collective-permute-start(f32[16,512]{1,0:T(8,128)S(1)} %get-tuple-element.36), channel_id=1, source_target_pairs={{0,2},{2,0},{4,6},{6,4},{8,10},{10,8},{12,14},{14,12},{16,18},{18,... | collective-permute-start | bytes 98312 | tf_op jit(solution)/shard_map/ppermute | solution.py:560
  56.0 1.5 %collective-permute-done.10 = f32[16,512]{1,0:T(8,128)S(1)} collective-permute-done((f32[16,512]{1,0:T(8,128)S(1)}, f32[16,512]{1,0:T(8,128)S(1)}, u32[]{:S(2)}, u32[]{:S(2)}) %collective-permute-start.10) | collective-permute-done | bytes 32800 | tf_op jit(solution)/shard_map/ppermute | solution.py:560
  57.5 1.3 %collective-permute-done.8 = f32[16,512]{1,0:T(8,128)S(1)} collective-permute-done((f32[16,512]{1,0:T(8,128)S(1)}, f32[16,512]{1,0:T(8,128)S(1)}, u32[]{:S(2)}, u32[]{:S(2)}) %collective-permute-start.8) | collective-permute-done | bytes 32800 | tf_op jit(solution)/shard_map/ppermute | solution.py:560
  58.8 1.1 %collective-permute-start.13 = (f32[16,512]{1,0:T(8,128)S(1)}, f32[16,512]{1,0:T(8,128)S(1)}, u32[]{:S(2)}, u32[]{:S(2)}) collective-permute-start(f32[16,512]{1,0:T(8,128)S(1)} %add_add_fusion.1), channel_id=1, source_target_pairs={{0,24},{2,26},{4,28},{6,30},{8,16},{10,18},{12,20},{14,22},{16,8},... | collective-permute-start | bytes 98312 | tf_op jit(solution)/shard_map/ppermute | solution.py:560
  59.9 3.4 %collective-permute-start.11 = (f32[16,512]{1,0:T(8,128)S(1)}, f32[16,512]{1,0:T(8,128)S(1)}, u32[]{:S(2)}, u32[]{:S(2)}) collective-permute-start(f32[16,512]{1,0:T(8,128)S(1)} %add_add_fusion.1), channel_id=1, source_target_pairs={{0,8},{2,10},{4,12},{6,14},{8,0},{10,2},{12,4},{14,6},{16,24},{18,... | collective-permute-start | bytes 98312 | tf_op jit(solution)/shard_map/ppermute | solution.py:560
  63.3 1.3 %collective-permute-done.13 = f32[16,512]{1,0:T(8,128)S(1)} collective-permute-done((f32[16,512]{1,0:T(8,128)S(1)}, f32[16,512]{1,0:T(8,128)S(1)}, u32[]{:S(2)}, u32[]{:S(2)}) %collective-permute-start.13) | collective-permute-done | bytes 32800 | tf_op jit(solution)/shard_map/ppermute | solution.py:560
  64.6 0.8 %collective-permute-done.12 = f32[16,512]{1,0:T(8,128)S(1)} collective-permute-done((f32[16,512]{1,0:T(8,128)S(1)}, f32[16,512]{1,0:T(8,128)S(1)}, u32[]{:S(2)}, u32[]{:S(2)}) %collective-permute-start.12) | collective-permute-done | bytes 32800 | tf_op jit(solution)/shard_map/ppermute | solution.py:560
  65.6 1.2 %collective-permute-done.14.theirs_ref = f32[16,512]{1,0:T(8,128)S(1)} collective-permute-done((f32[16,512]{1,0:T(8,128)S(1)}, f32[16,512]{1,0:T(8,128)S(1)}, u32[]{:S(2)}, u32[]{:S(2)}) %collective-permute-start.14) | collective-permute-done | bytes 32800 | tf_op jit(solution)/shard_map/ppermute | solution.py:560
  66.8 0.7 %finish.1 = (f32[16,27]{1,0:T(8,128)}, f32[16,432]{1,0:T(8,128)}, f32[16,432]{1,0:T(8,128)}, f32[3,32]{1,0:T(4,128)}) custom-call(f32[16,512]{1,0:T(8,128)S(1)} %add_add_fusion.mine_ref, f32[16,512]{1,0:T(8,128)S(1)} %collective-permute-done.14.theirs_ref), custom_call_target="tpu_custom_call" | custom-call | tf_op jit(solution)/shard_map/finish/pallas_call | solution.py:591
  (20 shorter events, 2.3 us)
Async XLA Ops:
  0.6 2.6 %collective-permute-start = (bf16[3,4,8,256]{3,2,1,0:T(8,128)(2,1)}, bf16[3,4,8,256]{3,2,1,0:T(8,128)(2,1)S(1)}, u32[]{:S(2)}, u32[]{:S(2)}) collective-permute-start(bf16[3,4,8,256]{3,2,1,0:T(8,128)(2,1)} %own_ref.1), channel_id=1, source_target_pairs={{0,1},{1,0},{2,3},{3,2},{4,5},{5,4},{6,7},{7,6},{8,9},{9,8},{10,11... | collective-permute-start | bytes 147464 | tf_op jit(solution)/shard_map/ppermute | solution.py:560
  3.2 19.5 %all-to-all-start = ((s32[32,1,2560]{2,1,0:T(1,128)}), s32[32,1,2560]{2,1,0:T(1,128)S(1)}, u32[]{:S(2)}, u32[]{:S(2)}) async-start(s32[32,1,2560]{2,1,0:T(1,128)} %pack.1), calls=%async_computation | async-start | bytes 655360 | tf_op jit(solution)/shard_map/all_to_all | solution.py:629
  10.2 0.8 %copy-start = (bf16[3,4,8,256]{3,2,1,0:T(8,128)(2,1)S(1)}, bf16[3,4,8,256]{3,2,1,0:T(8,128)(2,1)}, u32[]{:S(2)}) copy-start(bf16[3,4,8,256]{3,2,1,0:T(8,128)(2,1)} %own_ref.1) | copy-start | bytes 147460
  11.0 11.5 %collective-permute-start.1 = (bf16[2,48,256]{2,1,0:T(8,128)(2,1)S(1)}, bf16[2,48,256]{2,1,0:T(8,128)(2,1)S(1)}, u32[]{:S(2)}, u32[]{:S(2)}) collective-permute-start(bf16[2,48,256]{2,1,0:T(8,128)(2,1)S(1)} %get-tuple-element.25), channel_id=1, source_target_pairs={{0,2},{1,31},{2,4},{3,1},{4,6},{5,3},{6,8},{7,5},{8,10},{9,7},{10,... | collective-permute-start | bytes 147464 | tf_op jit(solution)/shard_map/ppermute | solution.py:620
  28.5 1.3 %collective-permute-start.2 = (f32[48,256]{1,0:T(8,128)S(1)}, f32[48,256]{1,0:T(8,128)S(1)}, u32[]{:S(2)}, u32[]{:S(2)}) collective-permute-start(f32[48,256]{1,0:T(8,128)S(1)} %deposit.1.own_ref), channel_id=1, source_target_pairs={{0,1},{1,0},{2,3},{3,2},{4,5},{5,4},{6,7},{7,6},{8,9},{9,8},{10,11... | collective-permute-start | bytes 147464 | tf_op jit(solution)/shard_map/ppermute | solution.py:560
  29.9 8.1 %collective-permute-start.3 = (f32[80,256]{1,0:T(8,128)S(1)}, f32[80,256]{1,0:T(8,128)S(1)}, u32[]{:S(2)}, u32[]{:S(2)}) collective-permute-start(f32[80,256]{1,0:T(8,128)S(1)} %get-tuple-element.26.near_ref), channel_id=1, source_target_pairs={{0,2},{1,31},{2,4},{3,1},{4,6},{5,3},{6,8},{7,5},{8,10},{9,7},{10,... | collective-permute-start | bytes 245768 | tf_op jit(solution)/shard_map/ppermute | solution.py:620
  30.3 6.6 %collective-permute-start.4 = (f32[32,256]{1,0:T(8,128)S(1)}, f32[32,256]{1,0:T(8,128)S(1)}, u32[]{:S(2)}, u32[]{:S(2)}) collective-permute-start(f32[32,256]{1,0:T(8,128)S(1)} %get-tuple-element.27.after_ref), channel_id=1, source_target_pairs={{0,4},{1,29},{2,6},{3,31},{4,8},{5,1},{6,10},{7,3},{8,12},{9,5},{1... | collective-permute-start | bytes 98312 | tf_op jit(solution)/shard_map/ppermute | solution.py:620
  37.9 1.7 %collective-permute-start.5 = (f32[80,256]{1,0:T(8,128)S(1)}, f32[80,256]{1,0:T(8,128)S(1)}, u32[]{:S(2)}, u32[]{:S(2)}) collective-permute-start(f32[80,256]{1,0:T(8,128)S(1)} %collective-permute-done.3.near_mine), channel_id=1, source_target_pairs={{0,1},{1,0},{2,3},{3,2},{4,5},{5,4},{6,7},{7,6},{8,9},{9,8},{10,11... | collective-permute-start | bytes 245768 | tf_op jit(solution)/shard_map/ppermute | solution.py:560
  37.9 1.4 %collective-permute-start.7 = (bf16[2,48,256]{2,1,0:T(8,128)(2,1)S(1)}, bf16[2,48,256]{2,1,0:T(8,128)(2,1)S(1)}, u32[]{:S(2)}, u32[]{:S(2)}) collective-permute-start(bf16[2,48,256]{2,1,0:T(8,128)(2,1)S(1)} %collective-permute-done.1.after_ref.ct_mine), channel_id=1, source_target_pairs={{0,1},{1,0},{2,3},{3,2},{4,5},{5,4},{6,7},{7,6},{8,9},{9,8},{10,11... | collective-permute-start | bytes 147464 | tf_op jit(solution)/shard_map/ppermute | solution.py:560
  38.5 1.2 %collective-permute-start.6 = (f32[32,256]{1,0:T(8,128)S(1)}, f32[32,256]{1,0:T(8,128)S(1)}, u32[]{:S(2)}, u32[]{:S(2)}) collective-permute-start(f32[32,256]{1,0:T(8,128)S(1)} %collective-permute-done.4.far_mine), channel_id=1, source_target_pairs={{0,1},{1,0},{2,3},{3,2},{4,5},{5,4},{6,7},{7,6},{8,9},{9,8},{10,11... | collective-permute-start | bytes 98312 | tf_op jit(solution)/shard_map/ppermute | solution.py:560
  52.5 5.0 %collective-permute-start.10 = (f32[16,512]{1,0:T(8,128)S(1)}, f32[16,512]{1,0:T(8,128)S(1)}, u32[]{:S(2)}, u32[]{:S(2)}) collective-permute-start(f32[16,512]{1,0:T(8,128)S(1)} %get-tuple-element.36), channel_id=1, source_target_pairs={{0,6},{2,4},{4,2},{6,0},{8,14},{10,12},{12,10},{14,8},{16,22},{18,... | collective-permute-start | bytes 98312 | tf_op jit(solution)/shard_map/ppermute | solution.py:560
  52.5 5.0 %collective-permute-start.9 = (f32[16,512]{1,0:T(8,128)S(1)}, f32[16,512]{1,0:T(8,128)S(1)}, u32[]{:S(2)}, u32[]{:S(2)}) collective-permute-start(f32[16,512]{1,0:T(8,128)S(1)} %get-tuple-element.36), channel_id=1, source_target_pairs={{0,4},{2,6},{4,0},{6,2},{8,12},{10,14},{12,8},{14,10},{16,20},{18,... | collective-permute-start | bytes 98312 | tf_op jit(solution)/shard_map/ppermute | solution.py:560
  54.9 3.9 %collective-permute-start.8 = (f32[16,512]{1,0:T(8,128)S(1)}, f32[16,512]{1,0:T(8,128)S(1)}, u32[]{:S(2)}, u32[]{:S(2)}) collective-permute-start(f32[16,512]{1,0:T(8,128)S(1)} %get-tuple-element.36), channel_id=1, source_target_pairs={{0,2},{2,0},{4,6},{6,4},{8,10},{10,8},{12,14},{14,12},{16,18},{18,... | collective-permute-start | bytes 98312 | tf_op jit(solution)/shard_map/ppermute | solution.py:560
  58.8 5.8 %collective-permute-start.13 = (f32[16,512]{1,0:T(8,128)S(1)}, f32[16,512]{1,0:T(8,128)S(1)}, u32[]{:S(2)}, u32[]{:S(2)}) collective-permute-start(f32[16,512]{1,0:T(8,128)S(1)} %add_add_fusion.1), channel_id=1, source_target_pairs={{0,24},{2,26},{4,28},{6,30},{8,16},{10,18},{12,20},{14,22},{16,8},... | collective-permute-start | bytes 98312 | tf_op jit(solution)/shard_map/ppermute | solution.py:560
  59.9 5.5 %collective-permute-start.12 = (f32[16,512]{1,0:T(8,128)S(1)}, f32[16,512]{1,0:T(8,128)S(1)}, u32[]{:S(2)}, u32[]{:S(2)}) collective-permute-start(f32[16,512]{1,0:T(8,128)S(1)} %add_add_fusion.1), channel_id=1, source_target_pairs={{0,16},{2,18},{4,20},{6,22},{8,24},{10,26},{12,28},{14,30},{16,0},... | collective-permute-start | bytes 98312 | tf_op jit(solution)/shard_map/ppermute | solution.py:560
  59.9 5.6 %collective-permute-start.11 = (f32[16,512]{1,0:T(8,128)S(1)}, f32[16,512]{1,0:T(8,128)S(1)}, u32[]{:S(2)}, u32[]{:S(2)}) collective-permute-start(f32[16,512]{1,0:T(8,128)S(1)} %add_add_fusion.1), channel_id=1, source_target_pairs={{0,8},{2,10},{4,12},{6,14},{8,0},{10,2},{12,4},{14,6},{16,24},{18,... | collective-permute-start | bytes 98312 | tf_op jit(solution)/shard_map/ppermute | solution.py:560
  65.5 1.3 %collective-permute-start.14 = (f32[16,512]{1,0:T(8,128)S(1)}, f32[16,512]{1,0:T(8,128)S(1)}, u32[]{:S(2)}, u32[]{:S(2)}) collective-permute-start(f32[16,512]{1,0:T(8,128)S(1)} %add_add_fusion.mine_ref), channel_id=1, source_target_pairs={{0,1},{1,0},{2,3},{3,2},{4,5},{5,4},{6,7},{7,6},{8,9},{9,8},{10,11... | collective-permute-start | bytes 98312 | tf_op jit(solution)/shard_map/ppermute | solution.py:560

commit v3 on v2

--- a/solution.py
+++ b/solution.py
@@ -169,6 +169,7 @@
 
 
 CH = 16
+RIM = 16
 
 
 def dot(a, b, dims=((1,), (0,))):
@@ -327,10 +328,13 @@
     mats_ref,
     wfirst_ref,
     whead_ref,
-    force_ref,
+    force_mine,
+    force_theirs,
     mine_ref,
+    theirs_ref,
     ct_ref,
     dens,
+    dens_inner,
     one,
     two,
     three,
@@ -341,9 +345,11 @@
     wg,
 ):
     full_y = 2 * width_y
-    depth = ct_ref.shape[2]
+    full = ct_middle.shape[2]
+    half = full // 2
+    depth = half + 2 * RIM
+    inner = slice(RIM, RIM + half)
     lanes = full_y * CH
-    own = width_y * CH
     first_core = lax.axis_index("sub") == 0
 
     def turned(ref, plane):
@@ -361,19 +367,33 @@
     column = [tail[0], tail[1] + below[0], *below[1:width_x], below[width_x] + planes[0], *planes[1:width_x]]
     column = column + [planes[width_x] + above[0], *above[1:width_x], above[width_x] + ahead]
     n_dens = 3 * width_x + 2
+    def framed(field):
+        return jnp.where(first_core, pltpu.roll(field, RIM, axis=1), pltpu.roll(field, half + RIM, axis=1))
+
+    def around(plane):
+        return jnp.concatenate([pltpu.roll(plane, 1, axis=1), plane, pltpu.roll(plane, full - 1, axis=1)], axis=0)
+
+    def chosen(field):
+        return jnp.where(first_core, field[:, 0:half], field[:, half:full])
+
     for j in range(n_dens):
-        plane = column[j]
-        around = [pltpu.roll(plane, 1, axis=1), plane, pltpu.roll(plane, depth - 1, axis=1)]
-        dens[3 * full_y * j : 3 * full_y * (j + 1)] = jnp.concatenate(around, axis=0).astype(jnp.bfloat16)
-
+        rows = slice(3 * full_y * j, 3 * full_y * (j + 1))
+        dens[rows] = around(framed(column[j]))[:, 0:depth].astype(jnp.bfloat16)
+        if 0 <= j - 4 < width_x + 2:
+            rows = slice(3 * full_y * (j - 4), 3 * full_y * (j - 3))
+            dens_inner[rows] = chosen(around(column[j])).astype(jnp.bfloat16)
+
+    ct_inner = []
     for x in range(width_x):
-        ct_ref[x + 2] = ct_middle[x]
+        plane = ct_middle[x].astype(jnp.float32)
+        ct_ref[x + 2] = framed(plane)[:, 0:depth].astype(jnp.bfloat16)
+        ct_inner.append(chosen(plane).astype(jnp.bfloat16))
     for x in range(2):
-        mine, theirs = ct_mine[x].astype(jnp.float32), ct_theirs[x].astype(jnp.float32)
+        mine, theirs = framed(ct_mine[x].astype(jnp.float32)), framed(ct_theirs[x].astype(jnp.float32))
         halves = [theirs[i * width_y : (i + 1) * width_y] for i in (1, 0, 3, 2, 5, 4)]
         theirs = jnp.concatenate(halves, axis=0)
-        ct_ref[x] = jnp.where(first_core, mine, theirs).astype(jnp.bfloat16)
-        ct_ref[x + 2 + width_x] = jnp.where(first_core, theirs, mine).astype(jnp.bfloat16)
+        ct_ref[x] = jnp.where(first_core, mine, theirs)[:, 0:depth].astype(jnp.bfloat16)
+        ct_ref[x + 2 + width_x] = jnp.where(first_core, theirs, mine)[:, 0:depth].astype(jnp.bfloat16)
 
     def window(x):
         return dens[pl.ds(pl.multiple_of(3 * full_y * x, 3 * full_y), 9 * full_y), :]
@@ -397,7 +417,7 @@
     def first_plane(x):
         v = dot(window(x), wfirst_ref[...], ((0,), (0,)))
         if 0 <= x - 4 < width_x:
-            pre_one[x - 4] = v[:, 0:own]
+            pre_one[x - 4] = v
         put(one, x, v * sigmoid(v))
 
     def second_done(i, both):
@@ -443,61 +463,63 @@
         waiting = (layer, i, both)
     layers[waiting[0]][2](waiting[1], waiting[2])
 
-    ct_own = jnp.concatenate([ct_ref[x + 2] for x in range(width_x)], axis=1)
+    ct_own = jnp.concatenate(ct_inner, axis=1)
     heads = [
-        dot(ct_own, three[:, :, 0:own].reshape(width_x * depth, own)),
-        dot(ct_own, one[4 : 4 + width_x, :, lanes : lanes + own].reshape(width_x * depth, own)),
+        dot(ct_own, three[:, inner, :].reshape(width_x * half, lanes)),
+        dot(ct_own, one[4 : 4 + width_x, inner, lanes : 2 * lanes].reshape(width_x * half, lanes)),
     ]
     for x in range(width_x):
-        h_three, h_one = three[x], one[x + 4, :, lanes : 2 * lanes]
-        rows = dot(h_three, whead_ref[0], ((1,), (1,))) + dot(h_one, whead_ref[1], ((1,), (1,)))
-        rows = jnp.transpose(rows)
+        rows = dot(three[x, inner, :], whead_ref[0], ((1,), (1,)))
+        rows = jnp.transpose(rows + dot(one[x + 4, inner, lanes : 2 * lanes], whead_ref[1], ((1,), (1,))))
         for k in range(3):
-            force_ref[k, x] = rows[k * full_y : k * full_y + width_y].astype(jnp.bfloat16)
-
-    across = []
-    for x in range(width_x):
-        middle = slice(lanes, 2 * lanes)
-        across.append(jnp.transpose(jnp.where(first_core, g_three[x + 2, :, middle], g_two[x + 1, :, middle])))
-    across = jnp.concatenate(across, axis=1)
-    for dx in range(3):
-        field = jnp.where(first_core, two[2 + dx : 2 + dx + width_x], one[3 + dx : 3 + dx + width_x])
-        wg[dx] = dot(across, field.reshape(width_x * depth, 3 * lanes))
+            start = k * full_y
+            force_mine[k, x] = rows[start : start + width_y].astype(jnp.bfloat16)
+            force_theirs[k, x] = rows[start + width_y : start + full_y].astype(jnp.bfloat16)
+
+    for which, grads, fields, shift in ((0, g_three, two, (2, 2)), (1, g_two, one, (1, 3))):
+        across = [jnp.transpose(grads[x + shift[0], inner, lanes : 2 * lanes]) for x in range(width_x)]
+        across = jnp.concatenate(across, axis=1)
+        for dx in range(3):
+            field = fields[shift[1] + dx : shift[1] + dx + width_x, inner, :]
+            wg[which, dx] = dot(across, field.reshape(width_x * half, 3 * lanes))
     grad_one = []
     for i in range(width_x // 2):
-        total = jnp.zeros((depth, 2 * own), jnp.float32)
-        for plane in range(4):
-            nothing = jnp.zeros((3 * lanes, own), jnp.bfloat16)
-            left = mats_ref[2, plane, :, 0:own] if plane < 3 else nothing
-            right = mats_ref[2, plane - 1, :, 0:own] if plane > 0 else nothing
-            total = total + dot(g_two[2 * i + plane], jnp.concatenate([left, right], axis=1))
+        both = conv(g_two, 2 * i, 2)
         for k in range(2):
             x = 2 * i + k
-            back = total[:, k * own : (k + 1) * own] + dot(ct_ref[x + 2], whead_ref[1, :, 0:own], ((0,), (0,)))
-            grad_one.append((back * slope(pre_one[x])).astype(jnp.bfloat16))
-    windows = jnp.concatenate([window(x + 4) for x in range(width_x)], axis=1)
+            back = both[k] + dot(ct_ref[x + 2], whead_ref[1], ((0,), (0,)))
+            grad_one.append((back * slope(pre_one[x])).astype(jnp.bfloat16)[inner])
+    windows = jnp.concatenate(
+        [dens_inner[3 * full_y * x : 3 * full_y * (x + 3)] for x in range(width_x)], axis=1
+    )
     firsts = dot(windows, jnp.concatenate(grad_one, axis=0))
 
     lane = iota((CH, 128), 1)
-    blocks = [jnp.zeros((CH, 128), jnp.float32) for _ in range(4)]
-    for dx in range(3):
-        for dz in range(3):
-            lined = jnp.zeros((CH, lanes), jnp.float32)
-            for y in range(full_y):
-                piece = wg[dx, y * CH : (y + 1) * CH, dz * lanes : (dz + 1) * lanes]
-                turn = (lanes - CH * (y - 1)) % lanes
-                lined = lined + (piece if turn == 0 else pltpu.roll(piece, turn, axis=1))
-            for dy in range(3):
-                target = (dx * 9 + dy * 3 + dz) * CH
-                turn = (target - dy * CH) % 128
-                piece = jnp.where(lane // CH == dy, lined[:, 0:128], 0.0)
-                blocks[target // 128] += piece if turn == 0 else pltpu.roll(piece, turn, axis=1)
+
+    def gathered(which):
+        blocks = [jnp.zeros((CH, 128), jnp.float32) for _ in range(4)]
+        for dx in range(3):
+            for dz in range(3):
+                lined = jnp.zeros((CH, lanes), jnp.float32)
+                for y in range(full_y):
+                    piece = wg[which, dx, y * CH : (y + 1) * CH, dz * lanes : (dz + 1) * lanes]
+                    turn = (lanes - CH * (y - 1)) % lanes
+                    lined = lined + (piece if turn == 0 else pltpu.roll(piece, turn, axis=1))
+                for dy in range(3):
+                    target = (dx * 9 + dy * 3 + dz) * CH
+                    turn = (target - dy * CH) % 128
+                    piece = jnp.where(lane // CH == dy, lined[:, 0:128], 0.0)
+                    blocks[target // 128] += piece if turn == 0 else pltpu.roll(piece, turn, axis=1)
+        return blocks
+
     def folded(rows):
+        rows = sum(rows[:, i * 128 : (i + 1) * 128] for i in range(lanes // 128))
         for turn in (64, 32, 16):
             rows = rows + pltpu.roll(rows, turn, axis=1)
         return rows
 
-    at_y, at_lane = iota((full_y, own), 0), iota((full_y, own), 1) // CH
+    last, mid = gathered(0), gathered(1)
+    at_y, at_lane = iota((full_y, lanes), 0), iota((full_y, lanes), 1) // CH
     first_rows = []
     for dx in range(3):
         for dy in range(3):
@@ -506,45 +528,52 @@
                 tap = (dx * 3 + dz) * full_y
                 part = jnp.where(match, firsts[tap : tap + full_y, :], 0.0)
                 first_rows.append(jnp.sum(part, axis=0, keepdims=True))
-    first = folded(jnp.concatenate(first_rows + [jnp.zeros((5, own), jnp.float32)], axis=0))
-    gap = jnp.zeros((48, own), jnp.float32)
-    blocks[3] += jnp.transpose(jnp.concatenate([gap, first, gap], axis=0))[0:CH]
-    for half in range(2):
+    first = folded(jnp.concatenate(first_rows + [jnp.zeros((5, lanes), jnp.float32)], axis=0))
+    gap = jnp.zeros((48, 128), jnp.float32)
+    last[3] += jnp.transpose(jnp.concatenate([gap, first, gap], axis=0))[0:CH]
+    for part_of in range(2):
         rows = []
         for k in range(3):
-            part = jnp.where(at_y == at_lane, heads[half][k * full_y : (k + 1) * full_y], 0.0)
+            part = jnp.where(at_y == at_lane, heads[part_of][k * full_y : (k + 1) * full_y], 0.0)
             rows.append(jnp.sum(part, axis=0, keepdims=True))
-        head = folded(jnp.concatenate(rows + [jnp.zeros((CH - 3, own), jnp.float32)], axis=0))
-        blocks[3] += jnp.where(lane // CH == 5 + half, head, 0.0)
+        head = folded(jnp.concatenate(rows + [jnp.zeros((CH - 3, lanes), jnp.float32)], axis=0))
+        last[3] += jnp.where(lane // CH == 5 + part_of, head, 0.0)
     for block in range(4):
-        mine_ref[:, block * 128 : (block + 1) * 128] = blocks[block]
+        columns = slice(block * 128, (block + 1) * 128)
+        mine_ref[:, columns] = jnp.where(first_core, last[block], mid[block])
+        theirs_ref[:, columns] = jnp.where(first_core, mid[block], last[block])
 
 
 def chain(pieces, mats, wfirst, whead, width_x, width_y, depth_z):
     full_y = 2 * width_y
-    lanes, own = full_y * CH, width_y * CH
+    lanes = full_y * CH
+    half = depth_z // 2
+    depth = half + 2 * RIM
     n_dens = 3 * width_x + 2
     bf16, f32 = jnp.bfloat16, jnp.float32
     args = (*pieces, mats, wfirst, whead)
     return pl.pallas_call(
         functools.partial(chain_kernel, width_x, width_y),
         out_shape=(
-            jax.ShapeDtypeStruct((3, width_x, width_y, depth_z), bf16),
+            jax.ShapeDtypeStruct((3, width_x, width_y, half), bf16),
+            jax.ShapeDtypeStruct((3, width_x, width_y, half), bf16),
+            jax.ShapeDtypeStruct((CH, 512), f32),
             jax.ShapeDtypeStruct((CH, 512), f32),
         ),
         in_specs=[pl.BlockSpec(memory_space=pltpu.VMEM)] * len(args),
-        out_specs=(pl.BlockSpec(memory_space=pltpu.VMEM),) * 2,
+        out_specs=(pl.BlockSpec(memory_space=pltpu.VMEM),) * 4,
         scratch_shapes=[
-            pltpu.VMEM((width_x + 4, 3 * full_y, depth_z), bf16),
-            pltpu.VMEM((n_dens * 3 * full_y, depth_z), bf16),
-            pltpu.VMEM((n_dens - 2, depth_z, 3 * lanes), bf16),
-            pltpu.VMEM((n_dens - 4, depth_z, 3 * lanes), bf16),
-            pltpu.VMEM((width_x, depth_z, lanes), bf16),
-            pltpu.VMEM((n_dens - 6, depth_z, 3 * lanes), bf16),
-            pltpu.VMEM((n_dens - 8, depth_z, 3 * lanes), bf16),
-            pltpu.VMEM((width_x, depth_z, own), f32),
-            pltpu.VMEM((width_x + 2, depth_z, lanes), f32),
-            pltpu.VMEM((3, lanes, 3 * lanes), f32),
+            pltpu.VMEM((width_x + 4, 3 * full_y, depth), bf16),
+            pltpu.VMEM((n_dens * 3 * full_y, depth), bf16),
+            pltpu.VMEM(((width_x + 2) * 3 * full_y, half), bf16),
+            pltpu.VMEM((n_dens - 2, depth, 3 * lanes), bf16),
+            pltpu.VMEM((n_dens - 4, depth, 3 * lanes), bf16),
+            pltpu.VMEM((width_x, depth, lanes), bf16),
+            pltpu.VMEM((n_dens - 6, depth, 3 * lanes), bf16),
+            pltpu.VMEM((n_dens - 8, depth, 3 * lanes), bf16),
+            pltpu.VMEM((width_x, depth, lanes), f32),
+            pltpu.VMEM((width_x + 2, depth, lanes), f32),
+            pltpu.VMEM((2, 3, lanes, 3 * lanes), f32),
         ],
         compiler_params=pltpu.CompilerParams(vmem_limit_bytes=36 * 1024 * 1024),
         name="chain",
@@ -560,7 +589,8 @@
     return lax.ppermute(x, axis, [(i, i ^ mask) for i in range(lax.axis_size(axis))])
 
 
-def summed(total):
+def summed(mine, theirs):
+    total = mine + exchanged(theirs, "sub", 1)
     stride, chips = 1, lax.axis_size("slab")
     while stride < chips:
         if chips // stride >= 4:
@@ -573,7 +603,9 @@
     return total, exchanged(total, "sub", 1)
 
 
-def finish_kernel(loss_scale, mine_ref, theirs_ref, first_ref, mid_ref, last_ref, head_ref):
+def finish_kernel(
+    loss_scale, mine_ref, theirs_ref, force_mine, force_theirs, force_ref, first_ref, mid_ref, last_ref, head_ref
+):
     first_core = lax.axis_index("sub") == 0
     taps = 27 * CH
     mine, theirs = mine_ref[...] * loss_scale, theirs_ref[...] * loss_scale
@@ -581,26 +613,34 @@
     last = jnp.where(first_core, mine, theirs)
     mid_ref[...] = mid[:, :taps]
     last_ref[...] = last[:, :taps]
+    half = force_mine.shape[3]
+    for k in range(force_ref.shape[0]):
+        for x in range(force_ref.shape[1]):
+            ours, other = force_mine[k, x].astype(jnp.float32), force_theirs[k, x].astype(jnp.float32)
+            force_ref[k, x, :, 0:half] = jnp.where(first_core, ours, other).astype(jnp.bfloat16)
+            force_ref[k, x, :, half:] = jnp.where(first_core, other, ours).astype(jnp.bfloat16)
     both = mine[:, 384:] + theirs[:, 384:]
     first_ref[...] = pltpu.roll(both, 80, axis=1)[:, :27]
     head_ref[...] = pltpu.roll(both, 48, axis=1)[:3, : 2 * CH]
 
 
-def finished(mine, theirs, loss_scale):
+def finished(mine, theirs, force_mine, force_theirs, loss_scale):
     f32 = jnp.float32
+    _, width_x, width_y, half = force_mine.shape
     return pl.pallas_call(
         functools.partial(finish_kernel, loss_scale),
         out_shape=(
+            jax.ShapeDtypeStruct((3, width_x, width_y, 2 * half), jnp.bfloat16),
             jax.ShapeDtypeStruct((CH, 27), f32),
             jax.ShapeDtypeStruct((CH, 27 * CH), f32),
             jax.ShapeDtypeStruct((CH, 27 * CH), f32),
             jax.ShapeDtypeStruct((3, 2 * CH), f32),
         ),
-        in_specs=[pl.BlockSpec(memory_space=pltpu.VMEM)] * 2,
-        out_specs=(pl.BlockSpec(memory_space=pltpu.VMEM),) * 4,
+        in_specs=[pl.BlockSpec(memory_space=pltpu.VMEM)] * 4,
+        out_specs=(pl.BlockSpec(memory_space=pltpu.VMEM),) * 5,
         compiler_params=pltpu.CompilerParams(vmem_limit_bytes=4 * 1024 * 1024),
         name="finish",
-    )(mine, theirs)
+    )(mine, theirs, force_mine, force_theirs)
 
 
 def per_device(part_cells, part_offsets, part_counts, w_first, w_mid, w_last, w_head, cotangent):
@@ -633,9 +673,10 @@
     near_mine, far_mine, whead = lax.optimization_barrier((outward(near, 1), outward(far, 2), whead))
     near_theirs, far_theirs = exchanged(near_mine, "sub", 1), exchanged(far_mine, "sub", 1)
     pieces = (near, near_mine, near_theirs, far_mine, far_theirs, ct_middle, ct_mine, ct_theirs)
-    force, mine = chain(pieces, mats, wfirst, whead, width_x, width_y, depth_z)
+    force_mine, force_theirs, mine, theirs = chain(pieces, mats, wfirst, whead, width_x, width_y, depth_z)
     loss_scale = 1.0 / math.sqrt(width_x * n_slab * width_y * n_sub * depth_z)
-    return (force, *finished(*summed(mine), loss_scale))
+    force_theirs = exchanged(force_theirs, "sub", 1)
+    return finished(*summed(mine, theirs), force_mine, force_theirs, loss_scale)
 
 
 def solution(mesh):

time: 67.8 us -> 64.9 us (0.957)
  Pallas kernels: 24.5 us -> 20.2 us
  waiting for transfers between devices: 20.9 us -> 21.6 us
  starting transfers between devices: 19.7 us -> 20.4 us
    pallas_call x1, Pallas kernels: 12.9 us -> 8.72 us  [chain(): pl.pallas_call(functools.partial(chain_kernel, width_x, width_y), out_sha...]
    ppermute x12 -> x14, starting transfers between devices: 9.11 us -> 9.82 us  [exchanged(): lax.ppermute(x, axis, [(i, i ^ mask) for i in range(lax.axis_size(axis))])]
    ppermute x12 -> x14, waiting for transfers between devices: 8.62 us -> 9.18 us  [exchanged(): lax.ppermute(x, axis, [(i, i ^ mask) for i in range(lax.axis_size(axis))])]
  transfers between devices with their start and end apart: 16 -> 18, of which waited for: 13 -> 13; matrix products, arithmetic and copies ran while one was open for 1% -> 1% of each run, Pallas kernels for 8% -> 8%
where the time goes in v3:
time: 64.9 us; the launch traced here: 64.6 us
  waiting for transfers between devices  21.6 us (33%)
  starting transfers between devices  20.4 us (31%)
  Pallas kernels  20.2 us (31%)
  other arithmetic  0.8 us (1%)
  local copies, waits for them, and re-layouts  0.79 us (1%)
  between operations  0.73 us (1%)
    ppermute x3, waiting for transfers between devices, outward(): return lax.ppermute(x, axes, pairs)  12.3 us
    ppermute x14, starting transfers between devices, exchanged(): lax.ppermute(x, axis, [(i, i ^ mask) for i in range(lax.axis_size(axis))])  9.82 us
    ppermute x14, waiting for transfers between devices, exchanged(): lax.ppermute(x, axis, [(i, i ^ mask) for i in range(lax.axis_size(axis))])  9.18 us
    pallas_call x1, Pallas kernels, chain(): pl.pallas_call(functools.partial(chain_kernel, width_x, width_y), out_sha...  8.72 us
    all_to_all x1, starting transfers between devices, per_device(): got = lax.all_to_all(words, axes, split_axis=0, concat_axis=0, tiled=True)  6.97 us
    pallas_call x1, Pallas kernels, deposit(): pl.pallas_call(functools.partial(deposit_kernel, width_x, width_y, depth_...  5.82 us
    ppermute x3, starting transfers between devices, outward(): return lax.ppermute(x, axes, pairs)  3.63 us
    pallas_call x1, Pallas kernels, weight_matrices(): pl.pallas_call(functools.partial(weights_kernel, full_y), out_shape=(jax....  2.93 us
  transfers between devices with their start and end apart: 18, of which 13 were waited for; matrix products, arithmetic and copies ran while one was open for 1% of the time, Pallas kernels for 8%

profile of v3, /device:TPU:0, one launch (start us, length us, event | category | flops | bytes accessed | tf_op | source)
XLA Modules:
  0.0 64.6 jit_solution(12785980868156194085)
XLA Ops:
  1.1 2.0 %pack.1 = s32[32,1,2560]{2,1,0:T(1,128)} custom-call(s32[32,1024]{1,0:T(8,128)} %bitcast.7, f32[3,32,1024]{2,1,0:T(8,128)} %bitcast.6, s32[1,32]{1,0:T(1,128)} %counts_hbm.1), custom_call_target="tpu_custom_call" | custom-call | tf_op jit(solution)/shard_map/pack/pallas_call | solution.py:46
  3.2 7.0 %all-to-all-start = ((s32[32,1,2560]{2,1,0:T(1,128)}), s32[32,1,2560]{2,1,0:T(1,128)S(1)}, u32[]{:S(2)}, u32[]{:S(2)}) async-start(s32[32,1,2560]{2,1,0:T(1,128)} %pack.1), calls=%async_computation | async-start | bytes 655360 | tf_op jit(solution)/shard_map/all_to_all | solution.py:669
  10.2 0.8 %copy-done = bf16[3,4,8,256]{3,2,1,0:T(8,128)(2,1)S(1)} copy-done((bf16[3,4,8,256]{3,2,1,0:T(8,128)(2,1)S(1)}, bf16[3,4,8,256]{3,2,1,0:T(8,128)(2,1)}, u32[]{:S(2)}) %copy-start) | copy-done | bytes 49176
  11.0 1.8 %collective-permute-start.1 = (bf16[2,48,256]{2,1,0:T(8,128)(2,1)S(1)}, bf16[2,48,256]{2,1,0:T(8,128)(2,1)S(1)}, u32[]{:S(2)}, u32[]{:S(2)}) collective-permute-start(bf16[2,48,256]{2,1,0:T(8,128)(2,1)S(1)} %get-tuple-element.23), channel_id=1, source_target_pairs={{0,2},{1,31},{2,4},{3,1},{4,6},{5,3},{6,8},{7,5},{8,10},{9,7},{10,... | collective-permute-start | bytes 147464 | tf_op jit(solution)/shard_map/ppermute | solution.py:660
  12.8 0.8 %fusion.7.late_ref.raw_ref = bf16[16,1280]{1,0:T(8,128)(2,1)S(1)} fusion(bf16[3,32]{1,0:T(4,128)(2,1)} %param.14, bf16[16,27]{1,0:T(8,128)(2,1)} %param.11, bf16[16,432]{1,0:T(8,128)(2,1)} %param.13, bf16[16,432]{1,0:T(8,128)(2,1)} %param.12), kind=kLoop, calls=%fused_computation.13 | loop fusion | flops 409600 | bytes 69664 | tf_op jit(solution)/shard_map/concatenate | solution.py:263
  13.6 8.9 %collective-permute-done.1.after_ref.ct_mine = bf16[2,48,256]{2,1,0:T(8,128)(2,1)S(1)} collective-permute-done((bf16[2,48,256]{2,1,0:T(8,128)(2,1)S(1)}, bf16[2,48,256]{2,1,0:T(8,128)(2,1)S(1)}, u32[]{:S(2)}, u32[]{:S(2)}) %collective-permute-start.1) | collective-permute-done | bytes 49184 | tf_op jit(solution)/shard_map/ppermute | solution.py:660
  22.7 5.8 %deposit.1.own_ref = f32[48,256]{1,0:T(8,128)S(1)} custom-call(s32[640,128]{1,0:T(8,128)S(1)} %bitcast.5, bf16[2,48,256]{2,1,0:T(8,128)(2,1)S(1)} %collective-permute-done.1.after_ref.ct_mine, bf16[16,1280]{1,0:T(8,128)(2,1)S(1)} %fusion.7.late_ref.raw_ref), custom_call_target="tpu_custom_call" | custom-call | tf_op jit(solution)/shard_map/deposit/pallas_call | solution.py:125
  28.6 1.2 %collective-permute-done.2.other_ref = f32[48,256]{1,0:T(8,128)S(1)} collective-permute-done((f32[48,256]{1,0:T(8,128)S(1)}, f32[48,256]{1,0:T(8,128)S(1)}, u32[]{:S(2)}, u32[]{:S(2)}) %collective-permute-start.2) | collective-permute-done | bytes 49184 | tf_op jit(solution)/shard_map/ppermute | solution.py:589
  30.3 1.3 %collective-permute-start.4 = (f32[32,256]{1,0:T(8,128)S(1)}, f32[32,256]{1,0:T(8,128)S(1)}, u32[]{:S(2)}, u32[]{:S(2)}) collective-permute-start(f32[32,256]{1,0:T(8,128)S(1)} %get-tuple-element.25.after_ref), channel_id=1, source_target_pairs={{0,4},{1,29},{2,6},{3,31},{4,8},{5,1},{6,10},{7,3},{8,12},{9,5},{1... | collective-permute-start | bytes 98312 | tf_op jit(solution)/shard_map/ppermute | solution.py:660
  31.6 2.9 %weights.1 = (bf16[4,3,768,256]{3,2,1,0:T(8,128)(2,1)S(1)}, bf16[144,256]{1,0:T(8,128)(2,1)S(1)}, bf16[2,48,256]{2,1,0:T(8,128)(2,1)S(1)}) custom-call(bf16[16,1280]{1,0:T(8,128)(2,1)S(1)} %fusion.7.late_ref.raw_ref, f32[32,256]{1,0:T(8,128)S(1)} %get-tuple-element.25.after_ref), custom_call_target="tpu_custom_call" | custom-call | flops 603979776 | bytes 8388608 | tf_op jit(solution)/shard_map/weights/pallas_call | solution.py:268
  34.6 2.4 %collective-permute-done.4.far_mine = f32[32,256]{1,0:T(8,128)S(1)} collective-permute-done((f32[32,256]{1,0:T(8,128)S(1)}, f32[32,256]{1,0:T(8,128)S(1)}, u32[]{:S(2)}, u32[]{:S(2)}) %collective-permute-start.4) | collective-permute-done | bytes 32800 | tf_op jit(solution)/shard_map/ppermute | solution.py:660
  37.0 1.0 %collective-permute-done.3.near_mine = f32[80,256]{1,0:T(8,128)S(1)} collective-permute-done((f32[80,256]{1,0:T(8,128)S(1)}, f32[80,256]{1,0:T(8,128)S(1)}, u32[]{:S(2)}, u32[]{:S(2)}) %collective-permute-start.3) | collective-permute-done | bytes 81952 | tf_op jit(solution)/shard_map/ppermute | solution.py:660
  38.4 0.9 %collective-permute-done.7.ct_theirs = bf16[2,48,256]{2,1,0:T(8,128)(2,1)S(1)} collective-permute-done((bf16[2,48,256]{2,1,0:T(8,128)(2,1)S(1)}, bf16[2,48,256]{2,1,0:T(8,128)(2,1)S(1)}, u32[]{:S(2)}, u32[]{:S(2)}) %collective-permute-start.7) | collective-permute-done | bytes 49184 | tf_op jit(solution)/shard_map/ppermute | solution.py:589
  39.7 8.7 %chain.1 = (bf16[3,4,8,128]{3,2,1,0:T(8,128)(2,1)S(1)}, bf16[3,4,8,128]{3,2,1,0:T(8,128)(2,1)S(1)}, f32[16,512]{1,0:T(8,128)S(1)}, f32[16,512]{1,0:T(8,128)S(1)}) custom-call(f32[80,256]{1,0:T(8,128)S(1)} %get-tuple-element.24.near_ref, f32[80,256]{1,0:T(8,128)S(1)} %collective-permute-done.3.near_mine, f32[80,256]{1,0:T(8,128)S(1)} %collective-permute-done.5.near_theirs, ...), custom_call_target="tpu_custom_call" | custom-call | tf_op jit(solution)/shard_map/chain/pallas_call | solution.py:555
  48.6 1.0 %collective-permute-done.8 = f32[16,512]{1,0:T(8,128)S(1)} collective-permute-done((f32[16,512]{1,0:T(8,128)S(1)}, f32[16,512]{1,0:T(8,128)S(1)}, u32[]{:S(2)}, u32[]{:S(2)}) %collective-permute-start.8) | collective-permute-done | bytes 32800 | tf_op jit(solution)/shard_map/ppermute | solution.py:589
  49.7 2.4 %collective-permute-start.10 = (f32[16,512]{1,0:T(8,128)S(1)}, f32[16,512]{1,0:T(8,128)S(1)}, u32[]{:S(2)}, u32[]{:S(2)}) collective-permute-start(f32[16,512]{1,0:T(8,128)S(1)} %add.29), channel_id=1, source_target_pairs={{0,4},{2,6},{4,0},{6,2},{8,12},{10,14},{12,8},{14,10},{16,20},{18,... | collective-permute-start | bytes 98312 | tf_op jit(solution)/shard_map/ppermute | solution.py:589
  52.0 1.1 %collective-permute-start.9 = (f32[16,512]{1,0:T(8,128)S(1)}, f32[16,512]{1,0:T(8,128)S(1)}, u32[]{:S(2)}, u32[]{:S(2)}) collective-permute-start(f32[16,512]{1,0:T(8,128)S(1)} %add.29), channel_id=1, source_target_pairs={{0,2},{2,0},{4,6},{6,4},{8,10},{10,8},{12,14},{14,12},{16,18},{18,... | collective-permute-start | bytes 98312 | tf_op jit(solution)/shard_map/ppermute | solution.py:589
  53.1 1.5 %collective-permute-done.11 = f32[16,512]{1,0:T(8,128)S(1)} collective-permute-done((f32[16,512]{1,0:T(8,128)S(1)}, f32[16,512]{1,0:T(8,128)S(1)}, u32[]{:S(2)}, u32[]{:S(2)}) %collective-permute-start.11) | collective-permute-done | bytes 32800 | tf_op jit(solution)/shard_map/ppermute | solution.py:589
  54.7 1.3 %collective-permute-done.9 = f32[16,512]{1,0:T(8,128)S(1)} collective-permute-done((f32[16,512]{1,0:T(8,128)S(1)}, f32[16,512]{1,0:T(8,128)S(1)}, u32[]{:S(2)}, u32[]{:S(2)}) %collective-permute-start.9) | collective-permute-done | bytes 32800 | tf_op jit(solution)/shard_map/ppermute | solution.py:589
  56.0 0.9 %collective-permute-start.14 = (f32[16,512]{1,0:T(8,128)S(1)}, f32[16,512]{1,0:T(8,128)S(1)}, u32[]{:S(2)}, u32[]{:S(2)}) collective-permute-start(f32[16,512]{1,0:T(8,128)S(1)} %add_add_fusion.1), channel_id=1, source_target_pairs={{0,24},{2,26},{4,28},{6,30},{8,16},{10,18},{12,20},{14,22},{16,8},... | collective-permute-start | bytes 98312 | tf_op jit(solution)/shard_map/ppermute | solution.py:589
  56.8 3.6 %collective-permute-start.12 = (f32[16,512]{1,0:T(8,128)S(1)}, f32[16,512]{1,0:T(8,128)S(1)}, u32[]{:S(2)}, u32[]{:S(2)}) collective-permute-start(f32[16,512]{1,0:T(8,128)S(1)} %add_add_fusion.1), channel_id=1, source_target_pairs={{0,8},{2,10},{4,12},{6,14},{8,0},{10,2},{12,4},{14,6},{16,24},{18,... | collective-permute-start | bytes 98312 | tf_op jit(solution)/shard_map/ppermute | solution.py:589
  60.4 1.4 %collective-permute-done.14 = f32[16,512]{1,0:T(8,128)S(1)} collective-permute-done((f32[16,512]{1,0:T(8,128)S(1)}, f32[16,512]{1,0:T(8,128)S(1)}, u32[]{:S(2)}, u32[]{:S(2)}) %collective-permute-start.14) | collective-permute-done | bytes 32800 | tf_op jit(solution)/shard_map/ppermute | solution.py:589
  63.1 0.8 %collective-permute-done.16.force_theirs = bf16[3,4,8,128]{3,2,1,0:T(8,128)(2,1)S(1)} collective-permute-done((bf16[3,4,8,128]{3,2,1,0:T(8,128)(2,1)S(1)}, bf16[3,4,8,128]{3,2,1,0:T(8,128)(2,1)S(1)}, u32[]{:S(2)}, u32[]{:S(2)}) %collective-permute-start.16) | collective-permute-done | bytes 24608 | tf_op jit(solution)/shard_map/ppermute | solution.py:589
  63.9 0.7 %finish.1 = (bf16[3,4,8,256]{3,2,1,0:T(8,128)(2,1)}, f32[16,27]{1,0:T(8,128)}, f32[16,432]{1,0:T(8,128)}, f32[16,432]{1,0:T(8,128)}, f32[3,32]{1,0:T(4,128)}) custom-call(f32[16,512]{1,0:T(8,128)S(1)} %add_add_fusion.mine_ref, f32[16,512]{1,0:T(8,128)S(1)} %collective-permute-done.15.theirs_ref, bf16[3,4,8,128]{3,2,1,0:T(8,128)(2,1)S(1)} %get-tuple-element.35.force_mine, ...), custom_call_target="tpu_custom_call" | custom-call | tf_op jit(solution)/shard_map/finish/pallas_call | solution.py:630
  (25 shorter events, 3.6 us)
Async XLA Ops:
  0.6 2.6 %collective-permute-start = (bf16[3,4,8,256]{3,2,1,0:T(8,128)(2,1)}, bf16[3,4,8,256]{3,2,1,0:T(8,128)(2,1)S(1)}, u32[]{:S(2)}, u32[]{:S(2)}) collective-permute-start(bf16[3,4,8,256]{3,2,1,0:T(8,128)(2,1)} %own_ref.1), channel_id=1, source_target_pairs={{0,1},{1,0},{2,3},{3,2},{4,5},{5,4},{6,7},{7,6},{8,9},{9,8},{10,11... | collective-permute-start | bytes 147464 | tf_op jit(solution)/shard_map/ppermute | solution.py:589
  3.2 19.5 %all-to-all-start = ((s32[32,1,2560]{2,1,0:T(1,128)}), s32[32,1,2560]{2,1,0:T(1,128)S(1)}, u32[]{:S(2)}, u32[]{:S(2)}) async-start(s32[32,1,2560]{2,1,0:T(1,128)} %pack.1), calls=%async_computation | async-start | bytes 655360 | tf_op jit(solution)/shard_map/all_to_all | solution.py:669
  10.2 0.8 %copy-start = (bf16[3,4,8,256]{3,2,1,0:T(8,128)(2,1)S(1)}, bf16[3,4,8,256]{3,2,1,0:T(8,128)(2,1)}, u32[]{:S(2)}) copy-start(bf16[3,4,8,256]{3,2,1,0:T(8,128)(2,1)} %own_ref.1) | copy-start | bytes 147460
  11.0 11.5 %collective-permute-start.1 = (bf16[2,48,256]{2,1,0:T(8,128)(2,1)S(1)}, bf16[2,48,256]{2,1,0:T(8,128)(2,1)S(1)}, u32[]{:S(2)}, u32[]{:S(2)}) collective-permute-start(bf16[2,48,256]{2,1,0:T(8,128)(2,1)S(1)} %get-tuple-element.23), channel_id=1, source_target_pairs={{0,2},{1,31},{2,4},{3,1},{4,6},{5,3},{6,8},{7,5},{8,10},{9,7},{10,... | collective-permute-start | bytes 147464 | tf_op jit(solution)/shard_map/ppermute | solution.py:660
  28.5 1.3 %collective-permute-start.2 = (f32[48,256]{1,0:T(8,128)S(1)}, f32[48,256]{1,0:T(8,128)S(1)}, u32[]{:S(2)}, u32[]{:S(2)}) collective-permute-start(f32[48,256]{1,0:T(8,128)S(1)} %deposit.1.own_ref), channel_id=1, source_target_pairs={{0,1},{1,0},{2,3},{3,2},{4,5},{5,4},{6,7},{7,6},{8,9},{9,8},{10,11... | collective-permute-start | bytes 147464 | tf_op jit(solution)/shard_map/ppermute | solution.py:589
  29.8 8.1 %collective-permute-start.3 = (f32[80,256]{1,0:T(8,128)S(1)}, f32[80,256]{1,0:T(8,128)S(1)}, u32[]{:S(2)}, u32[]{:S(2)}) collective-permute-start(f32[80,256]{1,0:T(8,128)S(1)} %get-tuple-element.24.near_ref), channel_id=1, source_target_pairs={{0,2},{1,31},{2,4},{3,1},{4,6},{5,3},{6,8},{7,5},{8,10},{9,7},{10,... | collective-permute-start | bytes 245768 | tf_op jit(solution)/shard_map/ppermute | solution.py:660
  30.3 6.6 %collective-permute-start.4 = (f32[32,256]{1,0:T(8,128)S(1)}, f32[32,256]{1,0:T(8,128)S(1)}, u32[]{:S(2)}, u32[]{:S(2)}) collective-permute-start(f32[32,256]{1,0:T(8,128)S(1)} %get-tuple-element.25.after_ref), channel_id=1, source_target_pairs={{0,4},{1,29},{2,6},{3,31},{4,8},{5,1},{6,10},{7,3},{8,12},{9,5},{1... | collective-permute-start | bytes 98312 | tf_op jit(solution)/shard_map/ppermute | solution.py:660
  37.9 1.7 %collective-permute-start.5 = (f32[80,256]{1,0:T(8,128)S(1)}, f32[80,256]{1,0:T(8,128)S(1)}, u32[]{:S(2)}, u32[]{:S(2)}) collective-permute-start(f32[80,256]{1,0:T(8,128)S(1)} %collective-permute-done.3.near_mine), channel_id=1, source_target_pairs={{0,1},{1,0},{2,3},{3,2},{4,5},{5,4},{6,7},{7,6},{8,9},{9,8},{10,11... | collective-permute-start | bytes 245768 | tf_op jit(solution)/shard_map/ppermute | solution.py:589
  37.9 1.4 %collective-permute-start.7 = (bf16[2,48,256]{2,1,0:T(8,128)(2,1)S(1)}, bf16[2,48,256]{2,1,0:T(8,128)(2,1)S(1)}, u32[]{:S(2)}, u32[]{:S(2)}) collective-permute-start(bf16[2,48,256]{2,1,0:T(8,128)(2,1)S(1)} %collective-permute-done.1.after_ref.ct_mine), channel_id=1, source_target_pairs={{0,1},{1,0},{2,3},{3,2},{4,5},{5,4},{6,7},{7,6},{8,9},{9,8},{10,11... | collective-permute-start | bytes 147464 | tf_op jit(solution)/shard_map/ppermute | solution.py:589
  38.4 1.2 %collective-permute-start.6 = (f32[32,256]{1,0:T(8,128)S(1)}, f32[32,256]{1,0:T(8,128)S(1)}, u32[]{:S(2)}, u32[]{:S(2)}) collective-permute-start(f32[32,256]{1,0:T(8,128)S(1)} %collective-permute-done.4.far_mine), channel_id=1, source_target_pairs={{0,1},{1,0},{2,3},{3,2},{4,5},{5,4},{6,7},{7,6},{8,9},{9,8},{10,11... | collective-permute-start | bytes 98312 | tf_op jit(solution)/shard_map/ppermute | solution.py:589
  48.4 1.3 %collective-permute-start.8 = (f32[16,512]{1,0:T(8,128)S(1)}, f32[16,512]{1,0:T(8,128)S(1)}, u32[]{:S(2)}, u32[]{:S(2)}) collective-permute-start(f32[16,512]{1,0:T(8,128)S(1)} %get-tuple-element.34), channel_id=1, source_target_pairs={{0,1},{1,0},{2,3},{3,2},{4,5},{5,4},{6,7},{7,6},{8,9},{9,8},{10,11... | collective-permute-start | bytes 98312 | tf_op jit(solution)/shard_map/ppermute | solution.py:589
  49.6 5.0 %collective-permute-start.11 = (f32[16,512]{1,0:T(8,128)S(1)}, f32[16,512]{1,0:T(8,128)S(1)}, u32[]{:S(2)}, u32[]{:S(2)}) collective-permute-start(f32[16,512]{1,0:T(8,128)S(1)} %add.29), channel_id=1, source_target_pairs={{0,6},{2,4},{4,2},{6,0},{8,14},{10,12},{12,10},{14,8},{16,22},{18,... | collective-permute-start | bytes 98312 | tf_op jit(solution)/shard_map/ppermute | solution.py:589
  49.7 5.0 %collective-permute-start.10 = (f32[16,512]{1,0:T(8,128)S(1)}, f32[16,512]{1,0:T(8,128)S(1)}, u32[]{:S(2)}, u32[]{:S(2)}) collective-permute-start(f32[16,512]{1,0:T(8,128)S(1)} %add.29), channel_id=1, source_target_pairs={{0,4},{2,6},{4,0},{6,2},{8,12},{10,14},{12,8},{14,10},{16,20},{18,... | collective-permute-start | bytes 98312 | tf_op jit(solution)/shard_map/ppermute | solution.py:589
  52.0 3.9 %collective-permute-start.9 = (f32[16,512]{1,0:T(8,128)S(1)}, f32[16,512]{1,0:T(8,128)S(1)}, u32[]{:S(2)}, u32[]{:S(2)}) collective-permute-start(f32[16,512]{1,0:T(8,128)S(1)} %add.29), channel_id=1, source_target_pairs={{0,2},{2,0},{4,6},{6,4},{8,10},{10,8},{12,14},{14,12},{16,18},{18,... | collective-permute-start | bytes 98312 | tf_op jit(solution)/shard_map/ppermute | solution.py:589
  56.0 5.9 %collective-permute-start.14 = (f32[16,512]{1,0:T(8,128)S(1)}, f32[16,512]{1,0:T(8,128)S(1)}, u32[]{:S(2)}, u32[]{:S(2)}) collective-permute-start(f32[16,512]{1,0:T(8,128)S(1)} %add_add_fusion.1), channel_id=1, source_target_pairs={{0,24},{2,26},{4,28},{6,30},{8,16},{10,18},{12,20},{14,22},{16,8},... | collective-permute-start | bytes 98312 | tf_op jit(solution)/shard_map/ppermute | solution.py:589
  56.8 5.6 %collective-permute-start.13 = (f32[16,512]{1,0:T(8,128)S(1)}, f32[16,512]{1,0:T(8,128)S(1)}, u32[]{:S(2)}, u32[]{:S(2)}) collective-permute-start(f32[16,512]{1,0:T(8,128)S(1)} %add_add_fusion.1), channel_id=1, source_target_pairs={{0,16},{2,18},{4,20},{6,22},{8,24},{10,26},{12,28},{14,30},{16,0},... | collective-permute-start | bytes 98312 | tf_op jit(solution)/shard_map/ppermute | solution.py:589
  56.8 5.6 %collective-permute-start.12 = (f32[16,512]{1,0:T(8,128)S(1)}, f32[16,512]{1,0:T(8,128)S(1)}, u32[]{:S(2)}, u32[]{:S(2)}) collective-permute-start(f32[16,512]{1,0:T(8,128)S(1)} %add_add_fusion.1), channel_id=1, source_target_pairs={{0,8},{2,10},{4,12},{6,14},{8,0},{10,2},{12,4},{14,6},{16,24},{18,... | collective-permute-start | bytes 98312 | tf_op jit(solution)/shard_map/ppermute | solution.py:589
  62.5 1.4 %collective-permute-start.15 = (f32[16,512]{1,0:T(8,128)S(1)}, f32[16,512]{1,0:T(8,128)S(1)}, u32[]{:S(2)}, u32[]{:S(2)}) collective-permute-start(f32[16,512]{1,0:T(8,128)S(1)} %add_add_fusion.mine_ref), channel_id=1, source_target_pairs={{0,1},{1,0},{2,3},{3,2},{4,5},{5,4},{6,7},{7,6},{8,9},{9,8},{10,11... | collective-permute-start | bytes 98312 | tf_op jit(solution)/shard_map/ppermute | solution.py:589
  62.6 1.3 %collective-permute-start.16 = (bf16[3,4,8,128]{3,2,1,0:T(8,128)(2,1)S(1)}, bf16[3,4,8,128]{3,2,1,0:T(8,128)(2,1)S(1)}, u32[]{:S(2)}, u32[]{:S(2)}) collective-permute-start(bf16[3,4,8,128]{3,2,1,0:T(8,128)(2,1)S(1)} %get-tuple-element.36), channel_id=1, source_target_pairs={{0,1},{1,0},{2,3},{3,2},{4,5},{5,4},{6,7},{7,6},{8,9},{9,8},{10,11... | collective-permute-start | bytes 73736 | tf_op jit(solution)/shard_map/ppermute | solution.py:589

commit v4 on v3

--- a/solution.py
+++ b/solution.py
@@ -589,18 +589,20 @@
     return lax.ppermute(x, axis, [(i, i ^ mask) for i in range(lax.axis_size(axis))])
 
 
-def summed(mine, theirs):
+def summed(mine, theirs, beside):
     total = mine + exchanged(theirs, "sub", 1)
     stride, chips = 1, lax.axis_size("slab")
     while stride < chips:
         if chips // stride >= 4:
             got = [exchanged(total, "slab", stride * i) for i in (1, 2, 3)]
             total = (total + got[0]) + (got[1] + got[2])
+            if stride == 1:
+                total, beside = lax.optimization_barrier((total, beside))
             stride *= 4
         else:
             total = total + exchanged(total, "slab", stride)
             stride *= 2
-    return total, exchanged(total, "sub", 1)
+    return total, exchanged(total, "sub", 1), beside
 
 
 def finish_kernel(
@@ -676,7 +678,8 @@
     force_mine, force_theirs, mine, theirs = chain(pieces, mats, wfirst, whead, width_x, width_y, depth_z)
     loss_scale = 1.0 / math.sqrt(width_x * n_slab * width_y * n_sub * depth_z)
     force_theirs = exchanged(force_theirs, "sub", 1)
-    return finished(*summed(mine, theirs), force_mine, force_theirs, loss_scale)
+    mine, theirs, force_theirs = summed(mine, theirs, force_theirs)
+    return finished(mine, theirs, force_mine, force_theirs, loss_scale)
 
 
 def solution(mesh):

time: 64.9 us -> 64.8 us (level)
  no operation moved by 1% of the time
where the time goes in v4:
time: 64.8 us; the launch traced here: 64.5 us
  waiting for transfers between devices  22 us (34%)
  Pallas kernels  20.2 us (31%)
  starting transfers between devices  19.9 us (31%)
  other arithmetic  0.8 us (1%)
  local copies, waits for them, and re-layouts  0.79 us (1%)
  between operations  0.74 us (1%)
    ppermute x3, waiting for transfers between devices, outward(): return lax.ppermute(x, axes, pairs)  12.3 us
    ppermute x14, waiting for transfers between devices, exchanged(): lax.ppermute(x, axis, [(i, i ^ mask) for i in range(lax.axis_size(axis))])  9.53 us
    ppermute x14, starting transfers between devices, exchanged(): lax.ppermute(x, axis, [(i, i ^ mask) for i in range(lax.axis_size(axis))])  9.32 us
    pallas_call x1, Pallas kernels, chain(): pl.pallas_call(functools.partial(chain_kernel, width_x, width_y), out_sha...  8.72 us
    all_to_all x1, starting transfers between devices, per_device(): got = lax.all_to_all(words, axes, split_axis=0, concat_axis=0, tiled=True)  6.97 us
    pallas_call x1, Pallas kernels, deposit(): pl.pallas_call(functools.partial(deposit_kernel, width_x, width_y, depth_...  5.82 us
    ppermute x3, starting transfers between devices, outward(): return lax.ppermute(x, axes, pairs)  3.63 us
    pallas_call x1, Pallas kernels, weight_matrices(): pl.pallas_call(functools.partial(weights_kernel, full_y), out_shape=(jax....  2.93 us
  transfers between devices with their start and end apart: 18, of which 13 were waited for; matrix products, arithmetic and copies ran while one was open for 1% of the time, Pallas kernels for 8%

profile of v4, /device:TPU:0, one launch (start us, length us, event | category | flops | bytes accessed | tf_op | source)
XLA Modules:
  0.0 64.5 jit_solution(3839894190657171906)
XLA Ops:
  1.1 2.0 %pack.1 = s32[32,1,2560]{2,1,0:T(1,128)} custom-call(s32[32,1024]{1,0:T(8,128)} %bitcast.7, f32[3,32,1024]{2,1,0:T(8,128)} %bitcast.6, s32[1,32]{1,0:T(1,128)} %counts_hbm.1), custom_call_target="tpu_custom_call" | custom-call | tf_op jit(solution)/shard_map/pack/pallas_call | solution.py:46
  3.2 7.0 %all-to-all-start = ((s32[32,1,2560]{2,1,0:T(1,128)}), s32[32,1,2560]{2,1,0:T(1,128)S(1)}, u32[]{:S(2)}, u32[]{:S(2)}) async-start(s32[32,1,2560]{2,1,0:T(1,128)} %pack.1), calls=%async_computation | async-start | bytes 655360 | tf_op jit(solution)/shard_map/all_to_all | solution.py:671
  10.2 0.8 %copy-done = bf16[3,4,8,256]{3,2,1,0:T(8,128)(2,1)S(1)} copy-done((bf16[3,4,8,256]{3,2,1,0:T(8,128)(2,1)S(1)}, bf16[3,4,8,256]{3,2,1,0:T(8,128)(2,1)}, u32[]{:S(2)}) %copy-start) | copy-done | bytes 49176
  11.0 1.8 %collective-permute-start.1 = (bf16[2,48,256]{2,1,0:T(8,128)(2,1)S(1)}, bf16[2,48,256]{2,1,0:T(8,128)(2,1)S(1)}, u32[]{:S(2)}, u32[]{:S(2)}) collective-permute-start(bf16[2,48,256]{2,1,0:T(8,128)(2,1)S(1)} %get-tuple-element.25), channel_id=1, source_target_pairs={{0,2},{1,31},{2,4},{3,1},{4,6},{5,3},{6,8},{7,5},{8,10},{9,7},{10,... | collective-permute-start | bytes 147464 | tf_op jit(solution)/shard_map/ppermute | solution.py:662
  12.8 0.8 %fusion.7.late_ref.raw_ref = bf16[16,1280]{1,0:T(8,128)(2,1)S(1)} fusion(bf16[3,32]{1,0:T(4,128)(2,1)} %param.14, bf16[16,27]{1,0:T(8,128)(2,1)} %param.11, bf16[16,432]{1,0:T(8,128)(2,1)} %param.13, bf16[16,432]{1,0:T(8,128)(2,1)} %param.12), kind=kLoop, calls=%fused_computation.13 | loop fusion | flops 409600 | bytes 69664 | tf_op jit(solution)/shard_map/concatenate | solution.py:263
  13.6 8.9 %collective-permute-done.1.after_ref.ct_mine = bf16[2,48,256]{2,1,0:T(8,128)(2,1)S(1)} collective-permute-done((bf16[2,48,256]{2,1,0:T(8,128)(2,1)S(1)}, bf16[2,48,256]{2,1,0:T(8,128)(2,1)S(1)}, u32[]{:S(2)}, u32[]{:S(2)}) %collective-permute-start.1) | collective-permute-done | bytes 49184 | tf_op jit(solution)/shard_map/ppermute | solution.py:662
  22.7 5.8 %deposit.1.own_ref = f32[48,256]{1,0:T(8,128)S(1)} custom-call(s32[640,128]{1,0:T(8,128)S(1)} %bitcast.5, bf16[2,48,256]{2,1,0:T(8,128)(2,1)S(1)} %collective-permute-done.1.after_ref.ct_mine, bf16[16,1280]{1,0:T(8,128)(2,1)S(1)} %fusion.7.late_ref.raw_ref), custom_call_target="tpu_custom_call" | custom-call | tf_op jit(solution)/shard_map/deposit/pallas_call | solution.py:125
  28.6 1.2 %collective-permute-done.2.other_ref = f32[48,256]{1,0:T(8,128)S(1)} collective-permute-done((f32[48,256]{1,0:T(8,128)S(1)}, f32[48,256]{1,0:T(8,128)S(1)}, u32[]{:S(2)}, u32[]{:S(2)}) %collective-permute-start.2) | collective-permute-done | bytes 49184 | tf_op jit(solution)/shard_map/ppermute | solution.py:589
  30.3 1.3 %collective-permute-start.4 = (f32[32,256]{1,0:T(8,128)S(1)}, f32[32,256]{1,0:T(8,128)S(1)}, u32[]{:S(2)}, u32[]{:S(2)}) collective-permute-start(f32[32,256]{1,0:T(8,128)S(1)} %get-tuple-element.27.after_ref), channel_id=1, source_target_pairs={{0,4},{1,29},{2,6},{3,31},{4,8},{5,1},{6,10},{7,3},{8,12},{9,5},{1... | collective-permute-start | bytes 98312 | tf_op jit(solution)/shard_map/ppermute | solution.py:662
  31.6 2.9 %weights.1 = (bf16[4,3,768,256]{3,2,1,0:T(8,128)(2,1)S(1)}, bf16[144,256]{1,0:T(8,128)(2,1)S(1)}, bf16[2,48,256]{2,1,0:T(8,128)(2,1)S(1)}) custom-call(bf16[16,1280]{1,0:T(8,128)(2,1)S(1)} %fusion.7.late_ref.raw_ref, f32[32,256]{1,0:T(8,128)S(1)} %get-tuple-element.27.after_ref), custom_call_target="tpu_custom_call" | custom-call | flops 603979776 | bytes 8388608 | tf_op jit(solution)/shard_map/weights/pallas_call | solution.py:268
  34.6 2.4 %collective-permute-done.4.far_mine = f32[32,256]{1,0:T(8,128)S(1)} collective-permute-done((f32[32,256]{1,0:T(8,128)S(1)}, f32[32,256]{1,0:T(8,128)S(1)}, u32[]{:S(2)}, u32[]{:S(2)}) %collective-permute-start.4) | collective-permute-done | bytes 32800 | tf_op jit(solution)/shard_map/ppermute | solution.py:662
  37.0 1.0 %collective-permute-done.3.near_mine = f32[80,256]{1,0:T(8,128)S(1)} collective-permute-done((f32[80,256]{1,0:T(8,128)S(1)}, f32[80,256]{1,0:T(8,128)S(1)}, u32[]{:S(2)}, u32[]{:S(2)}) %collective-permute-start.3) | collective-permute-done | bytes 81952 | tf_op jit(solution)/shard_map/ppermute | solution.py:662
  38.4 0.9 %collective-permute-done.7.ct_theirs = bf16[2,48,256]{2,1,0:T(8,128)(2,1)S(1)} collective-permute-done((bf16[2,48,256]{2,1,0:T(8,128)(2,1)S(1)}, bf16[2,48,256]{2,1,0:T(8,128)(2,1)S(1)}, u32[]{:S(2)}, u32[]{:S(2)}) %collective-permute-start.7) | collective-permute-done | bytes 49184 | tf_op jit(solution)/shard_map/ppermute | solution.py:589
  39.7 8.7 %chain.1 = (bf16[3,4,8,128]{3,2,1,0:T(8,128)(2,1)S(1)}, bf16[3,4,8,128]{3,2,1,0:T(8,128)(2,1)S(1)}, f32[16,512]{1,0:T(8,128)S(1)}, f32[16,512]{1,0:T(8,128)S(1)}) custom-call(f32[80,256]{1,0:T(8,128)S(1)} %get-tuple-element.26.near_ref, f32[80,256]{1,0:T(8,128)S(1)} %collective-permute-done.3.near_mine, f32[80,256]{1,0:T(8,128)S(1)} %collective-permute-done.5.near_theirs, ...), custom_call_target="tpu_custom_call" | custom-call | tf_op jit(solution)/shard_map/chain/pallas_call | solution.py:555
  48.6 1.0 %collective-permute-done.8 = f32[16,512]{1,0:T(8,128)S(1)} collective-permute-done((f32[16,512]{1,0:T(8,128)S(1)}, f32[16,512]{1,0:T(8,128)S(1)}, u32[]{:S(2)}, u32[]{:S(2)}) %collective-permute-start.8) | collective-permute-done | bytes 32800 | tf_op jit(solution)/shard_map/ppermute | solution.py:589
  49.7 2.4 %collective-permute-start.10 = (f32[16,512]{1,0:T(8,128)S(1)}, f32[16,512]{1,0:T(8,128)S(1)}, u32[]{:S(2)}, u32[]{:S(2)}) collective-permute-start(f32[16,512]{1,0:T(8,128)S(1)} %add.29), channel_id=1, source_target_pairs={{0,4},{2,6},{4,0},{6,2},{8,12},{10,14},{12,8},{14,10},{16,20},{18,... | collective-permute-start | bytes 98312 | tf_op jit(solution)/shard_map/ppermute | solution.py:589
  52.0 1.1 %collective-permute-start.9 = (f32[16,512]{1,0:T(8,128)S(1)}, f32[16,512]{1,0:T(8,128)S(1)}, u32[]{:S(2)}, u32[]{:S(2)}) collective-permute-start(f32[16,512]{1,0:T(8,128)S(1)} %add.29), channel_id=1, source_target_pairs={{0,2},{2,0},{4,6},{6,4},{8,10},{10,8},{12,14},{14,12},{16,18},{18,... | collective-permute-start | bytes 98312 | tf_op jit(solution)/shard_map/ppermute | solution.py:589
  53.1 1.5 %collective-permute-done.11 = f32[16,512]{1,0:T(8,128)S(1)} collective-permute-done((f32[16,512]{1,0:T(8,128)S(1)}, f32[16,512]{1,0:T(8,128)S(1)}, u32[]{:S(2)}, u32[]{:S(2)}) %collective-permute-start.11) | collective-permute-done | bytes 32800 | tf_op jit(solution)/shard_map/ppermute | solution.py:589
  54.7 1.3 %collective-permute-done.9 = f32[16,512]{1,0:T(8,128)S(1)} collective-permute-done((f32[16,512]{1,0:T(8,128)S(1)}, f32[16,512]{1,0:T(8,128)S(1)}, u32[]{:S(2)}, u32[]{:S(2)}) %collective-permute-start.9) | collective-permute-done | bytes 32800 | tf_op jit(solution)/shard_map/ppermute | solution.py:589
  56.0 0.9 %collective-permute-start.15 = (f32[16,512]{1,0:T(8,128)S(1)}, f32[16,512]{1,0:T(8,128)S(1)}, u32[]{:S(2)}, u32[]{:S(2)}) collective-permute-start(f32[16,512]{1,0:T(8,128)S(1)} %add_add_fusion.1), channel_id=1, source_target_pairs={{0,24},{2,26},{4,28},{6,30},{8,16},{10,18},{12,20},{14,22},{16,8},... | collective-permute-start | bytes 98312 | tf_op jit(solution)/shard_map/ppermute | solution.py:589
  56.8 3.6 %collective-permute-start.13 = (f32[16,512]{1,0:T(8,128)S(1)}, f32[16,512]{1,0:T(8,128)S(1)}, u32[]{:S(2)}, u32[]{:S(2)}) collective-permute-start(f32[16,512]{1,0:T(8,128)S(1)} %add_add_fusion.1), channel_id=1, source_target_pairs={{0,8},{2,10},{4,12},{6,14},{8,0},{10,2},{12,4},{14,6},{16,24},{18,... | collective-permute-start | bytes 98312 | tf_op jit(solution)/shard_map/ppermute | solution.py:589
  60.4 1.4 %collective-permute-done.15 = f32[16,512]{1,0:T(8,128)S(1)} collective-permute-done((f32[16,512]{1,0:T(8,128)S(1)}, f32[16,512]{1,0:T(8,128)S(1)}, u32[]{:S(2)}, u32[]{:S(2)}) %collective-permute-start.15) | collective-permute-done | bytes 32800 | tf_op jit(solution)/shard_map/ppermute | solution.py:589
  62.6 1.2 %collective-permute-done.16.theirs_ref = f32[16,512]{1,0:T(8,128)S(1)} collective-permute-done((f32[16,512]{1,0:T(8,128)S(1)}, f32[16,512]{1,0:T(8,128)S(1)}, u32[]{:S(2)}, u32[]{:S(2)}) %collective-permute-start.16) | collective-permute-done | bytes 32800 | tf_op jit(solution)/shard_map/ppermute | solution.py:589
  63.8 0.7 %finish.1 = (bf16[3,4,8,256]{3,2,1,0:T(8,128)(2,1)}, f32[16,27]{1,0:T(8,128)}, f32[16,432]{1,0:T(8,128)}, f32[16,432]{1,0:T(8,128)}, f32[3,32]{1,0:T(4,128)}) custom-call(f32[16,512]{1,0:T(8,128)S(1)} %add_add_fusion.mine_ref, f32[16,512]{1,0:T(8,128)S(1)} %collective-permute-done.16.theirs_ref, bf16[3,4,8,128]{3,2,1,0:T(8,128)(2,1)S(1)} %get-tuple-element.39.force_mine, ...), custom_call_target="tpu_custom_call" | custom-call | tf_op jit(solution)/shard_map/finish/pallas_call | solution.py:632
  (25 shorter events, 3.1 us)
Async XLA Ops:
  0.6 2.6 %collective-permute-start = (bf16[3,4,8,256]{3,2,1,0:T(8,128)(2,1)}, bf16[3,4,8,256]{3,2,1,0:T(8,128)(2,1)S(1)}, u32[]{:S(2)}, u32[]{:S(2)}) collective-permute-start(bf16[3,4,8,256]{3,2,1,0:T(8,128)(2,1)} %own_ref.1), channel_id=1, source_target_pairs={{0,1},{1,0},{2,3},{3,2},{4,5},{5,4},{6,7},{7,6},{8,9},{9,8},{10,11... | collective-permute-start | bytes 147464 | tf_op jit(solution)/shard_map/ppermute | solution.py:589
  3.2 19.5 %all-to-all-start = ((s32[32,1,2560]{2,1,0:T(1,128)}), s32[32,1,2560]{2,1,0:T(1,128)S(1)}, u32[]{:S(2)}, u32[]{:S(2)}) async-start(s32[32,1,2560]{2,1,0:T(1,128)} %pack.1), calls=%async_computation | async-start | bytes 655360 | tf_op jit(solution)/shard_map/all_to_all | solution.py:671
  10.2 0.8 %copy-start = (bf16[3,4,8,256]{3,2,1,0:T(8,128)(2,1)S(1)}, bf16[3,4,8,256]{3,2,1,0:T(8,128)(2,1)}, u32[]{:S(2)}) copy-start(bf16[3,4,8,256]{3,2,1,0:T(8,128)(2,1)} %own_ref.1) | copy-start | bytes 147460
  11.0 11.5 %collective-permute-start.1 = (bf16[2,48,256]{2,1,0:T(8,128)(2,1)S(1)}, bf16[2,48,256]{2,1,0:T(8,128)(2,1)S(1)}, u32[]{:S(2)}, u32[]{:S(2)}) collective-permute-start(bf16[2,48,256]{2,1,0:T(8,128)(2,1)S(1)} %get-tuple-element.25), channel_id=1, source_target_pairs={{0,2},{1,31},{2,4},{3,1},{4,6},{5,3},{6,8},{7,5},{8,10},{9,7},{10,... | collective-permute-start | bytes 147464 | tf_op jit(solution)/shard_map/ppermute | solution.py:662
  28.5 1.3 %collective-permute-start.2 = (f32[48,256]{1,0:T(8,128)S(1)}, f32[48,256]{1,0:T(8,128)S(1)}, u32[]{:S(2)}, u32[]{:S(2)}) collective-permute-start(f32[48,256]{1,0:T(8,128)S(1)} %deposit.1.own_ref), channel_id=1, source_target_pairs={{0,1},{1,0},{2,3},{3,2},{4,5},{5,4},{6,7},{7,6},{8,9},{9,8},{10,11... | collective-permute-start | bytes 147464 | tf_op jit(solution)/shard_map/ppermute | solution.py:589
  29.8 8.1 %collective-permute-start.3 = (f32[80,256]{1,0:T(8,128)S(1)}, f32[80,256]{1,0:T(8,128)S(1)}, u32[]{:S(2)}, u32[]{:S(2)}) collective-permute-start(f32[80,256]{1,0:T(8,128)S(1)} %get-tuple-element.26.near_ref), channel_id=1, source_target_pairs={{0,2},{1,31},{2,4},{3,1},{4,6},{5,3},{6,8},{7,5},{8,10},{9,7},{10,... | collective-permute-start | bytes 245768 | tf_op jit(solution)/shard_map/ppermute | solution.py:662
  30.3 6.6 %collective-permute-start.4 = (f32[32,256]{1,0:T(8,128)S(1)}, f32[32,256]{1,0:T(8,128)S(1)}, u32[]{:S(2)}, u32[]{:S(2)}) collective-permute-start(f32[32,256]{1,0:T(8,128)S(1)} %get-tuple-element.27.after_ref), channel_id=1, source_target_pairs={{0,4},{1,29},{2,6},{3,31},{4,8},{5,1},{6,10},{7,3},{8,12},{9,5},{1... | collective-permute-start | bytes 98312 | tf_op jit(solution)/shard_map/ppermute | solution.py:662
  37.9 1.7 %collective-permute-start.5 = (f32[80,256]{1,0:T(8,128)S(1)}, f32[80,256]{1,0:T(8,128)S(1)}, u32[]{:S(2)}, u32[]{:S(2)}) collective-permute-start(f32[80,256]{1,0:T(8,128)S(1)} %collective-permute-done.3.near_mine), channel_id=1, source_target_pairs={{0,1},{1,0},{2,3},{3,2},{4,5},{5,4},{6,7},{7,6},{8,9},{9,8},{10,11... | collective-permute-start | bytes 245768 | tf_op jit(solution)/shard_map/ppermute | solution.py:589
  37.9 1.4 %collective-permute-start.7 = (bf16[2,48,256]{2,1,0:T(8,128)(2,1)S(1)}, bf16[2,48,256]{2,1,0:T(8,128)(2,1)S(1)}, u32[]{:S(2)}, u32[]{:S(2)}) collective-permute-start(bf16[2,48,256]{2,1,0:T(8,128)(2,1)S(1)} %collective-permute-done.1.after_ref.ct_mine), channel_id=1, source_target_pairs={{0,1},{1,0},{2,3},{3,2},{4,5},{5,4},{6,7},{7,6},{8,9},{9,8},{10,11... | collective-permute-start | bytes 147464 | tf_op jit(solution)/shard_map/ppermute | solution.py:589
  38.4 1.2 %collective-permute-start.6 = (f32[32,256]{1,0:T(8,128)S(1)}, f32[32,256]{1,0:T(8,128)S(1)}, u32[]{:S(2)}, u32[]{:S(2)}) collective-permute-start(f32[32,256]{1,0:T(8,128)S(1)} %collective-permute-done.4.far_mine), channel_id=1, source_target_pairs={{0,1},{1,0},{2,3},{3,2},{4,5},{5,4},{6,7},{7,6},{8,9},{9,8},{10,11... | collective-permute-start | bytes 98312 | tf_op jit(solution)/shard_map/ppermute | solution.py:589
  48.4 1.3 %collective-permute-start.8 = (f32[16,512]{1,0:T(8,128)S(1)}, f32[16,512]{1,0:T(8,128)S(1)}, u32[]{:S(2)}, u32[]{:S(2)}) collective-permute-start(f32[16,512]{1,0:T(8,128)S(1)} %get-tuple-element.36), channel_id=1, source_target_pairs={{0,1},{1,0},{2,3},{3,2},{4,5},{5,4},{6,7},{7,6},{8,9},{9,8},{10,11... | collective-permute-start | bytes 98312 | tf_op jit(solution)/shard_map/ppermute | solution.py:589
  49.6 5.0 %collective-permute-start.11 = (f32[16,512]{1,0:T(8,128)S(1)}, f32[16,512]{1,0:T(8,128)S(1)}, u32[]{:S(2)}, u32[]{:S(2)}) collective-permute-start(f32[16,512]{1,0:T(8,128)S(1)} %add.29), channel_id=1, source_target_pairs={{0,6},{2,4},{4,2},{6,0},{8,14},{10,12},{12,10},{14,8},{16,22},{18,... | collective-permute-start | bytes 98312 | tf_op jit(solution)/shard_map/ppermute | solution.py:589
  49.7 5.0 %collective-permute-start.10 = (f32[16,512]{1,0:T(8,128)S(1)}, f32[16,512]{1,0:T(8,128)S(1)}, u32[]{:S(2)}, u32[]{:S(2)}) collective-permute-start(f32[16,512]{1,0:T(8,128)S(1)} %add.29), channel_id=1, source_target_pairs={{0,4},{2,6},{4,0},{6,2},{8,12},{10,14},{12,8},{14,10},{16,20},{18,... | collective-permute-start | bytes 98312 | tf_op jit(solution)/shard_map/ppermute | solution.py:589
  52.0 3.9 %collective-permute-start.9 = (f32[16,512]{1,0:T(8,128)S(1)}, f32[16,512]{1,0:T(8,128)S(1)}, u32[]{:S(2)}, u32[]{:S(2)}) collective-permute-start(f32[16,512]{1,0:T(8,128)S(1)} %add.29), channel_id=1, source_target_pairs={{0,2},{2,0},{4,6},{6,4},{8,10},{10,8},{12,14},{14,12},{16,18},{18,... | collective-permute-start | bytes 98312 | tf_op jit(solution)/shard_map/ppermute | solution.py:589
  53.1 2.8 %collective-permute-start.12 = (bf16[3,4,8,128]{3,2,1,0:T(8,128)(2,1)S(1)}, bf16[3,4,8,128]{3,2,1,0:T(8,128)(2,1)S(1)}, u32[]{:S(2)}, u32[]{:S(2)}) collective-permute-start(bf16[3,4,8,128]{3,2,1,0:T(8,128)(2,1)S(1)} %get-tuple-element.37), channel_id=1, source_target_pairs={{0,1},{1,0},{2,3},{3,2},{4,5},{5,4},{6,7},{7,6},{8,9},{9,8},{10,11... | collective-permute-start | bytes 73736 | tf_op jit(solution)/shard_map/ppermute | solution.py:589
  56.0 5.9 %collective-permute-start.15 = (f32[16,512]{1,0:T(8,128)S(1)}, f32[16,512]{1,0:T(8,128)S(1)}, u32[]{:S(2)}, u32[]{:S(2)}) collective-permute-start(f32[16,512]{1,0:T(8,128)S(1)} %add_add_fusion.1), channel_id=1, source_target_pairs={{0,24},{2,26},{4,28},{6,30},{8,16},{10,18},{12,20},{14,22},{16,8},... | collective-permute-start | bytes 98312 | tf_op jit(solution)/shard_map/ppermute | solution.py:589
  56.8 5.6 %collective-permute-start.14 = (f32[16,512]{1,0:T(8,128)S(1)}, f32[16,512]{1,0:T(8,128)S(1)}, u32[]{:S(2)}, u32[]{:S(2)}) collective-permute-start(f32[16,512]{1,0:T(8,128)S(1)} %add_add_fusion.1), channel_id=1, source_target_pairs={{0,16},{2,18},{4,20},{6,22},{8,24},{10,26},{12,28},{14,30},{16,0},... | collective-permute-start | bytes 98312 | tf_op jit(solution)/shard_map/ppermute | solution.py:589
  56.8 5.6 %collective-permute-start.13 = (f32[16,512]{1,0:T(8,128)S(1)}, f32[16,512]{1,0:T(8,128)S(1)}, u32[]{:S(2)}, u32[]{:S(2)}) collective-permute-start(f32[16,512]{1,0:T(8,128)S(1)} %add_add_fusion.1), channel_id=1, source_target_pairs={{0,8},{2,10},{4,12},{6,14},{8,0},{10,2},{12,4},{14,6},{16,24},{18,... | collective-permute-start | bytes 98312 | tf_op jit(solution)/shard_map/ppermute | solution.py:589
  62.5 1.3 %collective-permute-start.16 = (f32[16,512]{1,0:T(8,128)S(1)}, f32[16,512]{1,0:T(8,128)S(1)}, u32[]{:S(2)}, u32[]{:S(2)}) collective-permute-start(f32[16,512]{1,0:T(8,128)S(1)} %add_add_fusion.mine_ref), channel_id=1, source_target_pairs={{0,1},{1,0},{2,3},{3,2},{4,5},{5,4},{6,7},{7,6},{8,9},{9,8},{10,11... | collective-permute-start | bytes 98312 | tf_op jit(solution)/shard_map/ppermute | solution.py:589

commit v5 on v4

--- a/solution.py
+++ b/solution.py
@@ -666,14 +666,14 @@
     ct_other = exchanged(cotangent, "sub", 1)
     words, ct_other = lax.optimization_barrier((words, ct_other))
     ct_middle, ct_edge = edges(cotangent, ct_other)
-    ct_mine = outward(ct_edge, 1)
-    ct_theirs = exchanged(ct_mine, "sub", 1)
     got = lax.all_to_all(words, axes, split_axis=0, concat_axis=0, tiled=True)
-    own = deposit(got, ct_mine, raw, cap, width_x, width_y, depth_z)
+    own = deposit(got, ct_edge, raw, cap, width_x, width_y, depth_z)
     near, far = combined(own, exchanged(own, "sub", 1), width_x, width_y)
     mats, wfirst, whead = weight_matrices(raw, far, n_sub * width_y)
-    near_mine, far_mine, whead = lax.optimization_barrier((outward(near, 1), outward(far, 2), whead))
-    near_theirs, far_theirs = exchanged(near_mine, "sub", 1), exchanged(far_mine, "sub", 1)
+    near_mine, far_mine, ct_mine, whead = lax.optimization_barrier(
+        (outward(near, 1), outward(far, 2), outward(ct_edge, 1), whead)
+    )
+    near_theirs, far_theirs, ct_theirs = (exchanged(piece, "sub", 1) for piece in (near_mine, far_mine, ct_mine))
     pieces = (near, near_mine, near_theirs, far_mine, far_theirs, ct_middle, ct_mine, ct_theirs)
     force_mine, force_theirs, mine, theirs = chain(pieces, mats, wfirst, whead, width_x, width_y, depth_z)
     loss_scale = 1.0 / math.sqrt(width_x * n_slab * width_y * n_sub * depth_z)

time: 64.8 us -> 65 us (level)
    all_to_all x1, waiting for transfers between devices: 0.16 us -> 10.4 us  [per_device(): got = lax.all_to_all(words, axes, split_axis=0, concat_axis=0, tiled=True)]
    ppermute x3, waiting for transfers between devices: 12.3 us -> 2.21 us  [outward(): return lax.ppermute(x, axes, pairs)]
  transfers between devices with their start and end apart: 18 -> 18, of which waited for: 13 -> 11; matrix products, arithmetic and copies ran while one was open for 1% -> 1% of each run, Pallas kernels for 8% -> 8%
where the time goes in v5:
time: 65 us; the launch traced here: 64.7 us
  waiting for transfers between devices  22 us (34%)
  Pallas kernels  20.2 us (31%)
  starting transfers between devices  20.1 us (31%)
  other arithmetic  0.81 us (1%)
  local copies, waits for them, and re-layouts  0.79 us (1%)
  between operations  0.74 us (1%)
    all_to_all x1, waiting for transfers between devices, per_device(): got = lax.all_to_all(words, axes, split_axis=0, concat_axis=0, tiled=True)  10.4 us
    ppermute x14, waiting for transfers between devices, exchanged(): lax.ppermute(x, axis, [(i, i ^ mask) for i in range(lax.axis_size(axis))])  9.36 us
    ppermute x14, starting transfers between devices, exchanged(): lax.ppermute(x, axis, [(i, i ^ mask) for i in range(lax.axis_size(axis))])  9.33 us
    pallas_call x1, Pallas kernels, chain(): pl.pallas_call(functools.partial(chain_kernel, width_x, width_y), out_sha...  8.72 us
    all_to_all x1, starting transfers between devices, per_device(): got = lax.all_to_all(words, axes, split_axis=0, concat_axis=0, tiled=True)  6.97 us
    pallas_call x1, Pallas kernels, deposit(): pl.pallas_call(functools.partial(deposit_kernel, width_x, width_y, depth_...  5.83 us
    ppermute x3, starting transfers between devices, outward(): return lax.ppermute(x, axes, pairs)  3.83 us
    pallas_call x1, Pallas kernels, weight_matrices(): pl.pallas_call(functools.partial(weights_kernel, full_y), out_shape=(jax....  2.92 us
  transfers between devices with their start and end apart: 18, of which 11 were waited for; matrix products, arithmetic and copies ran while one was open for 1% of the time, Pallas kernels for 8%

profile of v5, /device:TPU:0, one launch (start us, length us, event | category | flops | bytes accessed | tf_op | source)
XLA Modules:
  0.0 64.7 jit_solution(17532873440551243362)
XLA Ops:
  0.6 0.5 collective-permute-start
  1.1 2.0 %pack.1 = s32[32,1,2560]{2,1,0:T(1,128)} custom-call(s32[32,1024]{1,0:T(8,128)} %bitcast.7, f32[3,32,1024]{2,1,0:T(8,128)} %bitcast.6, s32[1,32]{1,0:T(1,128)} %counts_hbm.1), custom_call_target="tpu_custom_call" | custom-call | tf_op jit(solution)/shard_map/pack/pallas_call | solution.py:46
  3.2 7.0 %all-to-all-start = ((s32[32,1,2560]{2,1,0:T(1,128)}), s32[32,1,2560]{2,1,0:T(1,128)S(1)}, u32[]{:S(2)}, u32[]{:S(2)}) async-start(s32[32,1,2560]{2,1,0:T(1,128)} %pack.1), calls=%async_computation | async-start | bytes 655360 | tf_op jit(solution)/shard_map/all_to_all | solution.py:669
  10.2 0.8 %fusion.7.late_ref.raw_ref = bf16[16,1280]{1,0:T(8,128)(2,1)S(1)} fusion(bf16[3,32]{1,0:T(4,128)(2,1)} %param.14, bf16[16,27]{1,0:T(8,128)(2,1)} %param.11, bf16[16,432]{1,0:T(8,128)(2,1)} %param.13, bf16[16,432]{1,0:T(8,128)(2,1)} %param.12), kind=kLoop, calls=%fused_computation.13 | loop fusion | flops 409600 | bytes 69664 | tf_op jit(solution)/shard_map/concatenate | solution.py:263
  11.0 0.8 %copy-done = bf16[3,4,8,256]{3,2,1,0:T(8,128)(2,1)S(1)} copy-done((bf16[3,4,8,256]{3,2,1,0:T(8,128)(2,1)S(1)}, bf16[3,4,8,256]{3,2,1,0:T(8,128)(2,1)}, u32[]{:S(2)}) %copy-start) | copy-done | bytes 49176
  11.8 10.4 %all-to-all-done = s32[32,1,2560]{2,1,0:T(1,128)S(1)} async-done(((s32[32,1,2560]{2,1,0:T(1,128)}), s32[32,1,2560]{2,1,0:T(1,128)S(1)}, u32[]{:S(2)}, u32[]{:S(2)}) %all-to-all-start) | async-done | bytes 327712 | tf_op jit(solution)/shard_map/all_to_all | solution.py:669
  22.2 5.8 %deposit.1.own_ref = f32[48,256]{1,0:T(8,128)S(1)} custom-call(s32[640,128]{1,0:T(8,128)S(1)} %bitcast.5, bf16[2,48,256]{2,1,0:T(8,128)(2,1)S(1)} %get-tuple-element.26.after_ref, bf16[16,1280]{1,0:T(8,128)(2,1)S(1)} %fusion.7.late_ref.raw_ref), custom_call_target="tpu_custom_call" | custom-call | tf_op jit(solution)/shard_map/deposit/pallas_call | solution.py:125
  28.1 1.2 %collective-permute-done.1.other_ref = f32[48,256]{1,0:T(8,128)S(1)} collective-permute-done((f32[48,256]{1,0:T(8,128)S(1)}, f32[48,256]{1,0:T(8,128)S(1)}, u32[]{:S(2)}, u32[]{:S(2)}) %collective-permute-start.1) | collective-permute-done | bytes 49184 | tf_op jit(solution)/shard_map/ppermute | solution.py:589
  29.8 1.9 %collective-permute-start.4 = (bf16[2,48,256]{2,1,0:T(8,128)(2,1)S(1)}, bf16[2,48,256]{2,1,0:T(8,128)(2,1)S(1)}, u32[]{:S(2)}, u32[]{:S(2)}) collective-permute-start(bf16[2,48,256]{2,1,0:T(8,128)(2,1)S(1)} %get-tuple-element.26.after_ref), channel_id=1, source_target_pairs={{0,2},{1,31},{2,4},{3,1},{4,6},{5,3},{6,8},{7,5},{8,10},{9,7},{10,... | collective-permute-start | bytes 147464 | tf_op jit(solution)/shard_map/ppermute | solution.py:662
  31.7 1.5 %collective-permute-start.3 = (f32[32,256]{1,0:T(8,128)S(1)}, f32[32,256]{1,0:T(8,128)S(1)}, u32[]{:S(2)}, u32[]{:S(2)}) collective-permute-start(f32[32,256]{1,0:T(8,128)S(1)} %get-tuple-element.28.after_ref), channel_id=1, source_target_pairs={{0,4},{1,29},{2,6},{3,31},{4,8},{5,1},{6,10},{7,3},{8,12},{9,5},{1... | collective-permute-start | bytes 98312 | tf_op jit(solution)/shard_map/ppermute | solution.py:662
  33.2 2.9 %weights.1 = (bf16[4,3,768,256]{3,2,1,0:T(8,128)(2,1)S(1)}, bf16[144,256]{1,0:T(8,128)(2,1)S(1)}, bf16[2,48,256]{2,1,0:T(8,128)(2,1)S(1)}) custom-call(bf16[16,1280]{1,0:T(8,128)(2,1)S(1)} %fusion.7.late_ref.raw_ref, f32[32,256]{1,0:T(8,128)S(1)} %get-tuple-element.28.after_ref), custom_call_target="tpu_custom_call" | custom-call | flops 603979776 | bytes 8388608 | tf_op jit(solution)/shard_map/weights/pallas_call | solution.py:268
  36.1 1.9 %collective-permute-done.4.ct_mine = bf16[2,48,256]{2,1,0:T(8,128)(2,1)S(1)} collective-permute-done((bf16[2,48,256]{2,1,0:T(8,128)(2,1)S(1)}, bf16[2,48,256]{2,1,0:T(8,128)(2,1)S(1)}, u32[]{:S(2)}, u32[]{:S(2)}) %collective-permute-start.4) | collective-permute-done | bytes 49184 | tf_op jit(solution)/shard_map/ppermute | solution.py:662
  38.8 1.2 %collective-permute-done.6.far_theirs = f32[32,256]{1,0:T(8,128)S(1)} collective-permute-done((f32[32,256]{1,0:T(8,128)S(1)}, f32[32,256]{1,0:T(8,128)S(1)}, u32[]{:S(2)}, u32[]{:S(2)}) %collective-permute-start.6) | collective-permute-done | bytes 32800 | tf_op jit(solution)/shard_map/ppermute | solution.py:589
  40.0 8.7 %chain.1 = (bf16[3,4,8,128]{3,2,1,0:T(8,128)(2,1)S(1)}, bf16[3,4,8,128]{3,2,1,0:T(8,128)(2,1)S(1)}, f32[16,512]{1,0:T(8,128)S(1)}, f32[16,512]{1,0:T(8,128)S(1)}) custom-call(f32[80,256]{1,0:T(8,128)S(1)} %get-tuple-element.27.near_ref, f32[80,256]{1,0:T(8,128)S(1)} %collective-permute-done.2.near_mine, f32[80,256]{1,0:T(8,128)S(1)} %collective-permute-done.5.near_theirs, ...), custom_call_target="tpu_custom_call" | custom-call | tf_op jit(solution)/shard_map/chain/pallas_call | solution.py:555
  49.0 1.0 %collective-permute-done.8 = f32[16,512]{1,0:T(8,128)S(1)} collective-permute-done((f32[16,512]{1,0:T(8,128)S(1)}, f32[16,512]{1,0:T(8,128)S(1)}, u32[]{:S(2)}, u32[]{:S(2)}) %collective-permute-start.8) | collective-permute-done | bytes 32800 | tf_op jit(solution)/shard_map/ppermute | solution.py:589
  50.0 2.4 %collective-permute-start.10 = (f32[16,512]{1,0:T(8,128)S(1)}, f32[16,512]{1,0:T(8,128)S(1)}, u32[]{:S(2)}, u32[]{:S(2)}) collective-permute-start(f32[16,512]{1,0:T(8,128)S(1)} %add.29), channel_id=1, source_target_pairs={{0,4},{2,6},{4,0},{6,2},{8,12},{10,14},{12,8},{14,10},{16,20},{18,... | collective-permute-start | bytes 98312 | tf_op jit(solution)/shard_map/ppermute | solution.py:589
  52.4 1.1 %collective-permute-start.9 = (f32[16,512]{1,0:T(8,128)S(1)}, f32[16,512]{1,0:T(8,128)S(1)}, u32[]{:S(2)}, u32[]{:S(2)}) collective-permute-start(f32[16,512]{1,0:T(8,128)S(1)} %add.29), channel_id=1, source_target_pairs={{0,2},{2,0},{4,6},{6,4},{8,10},{10,8},{12,14},{14,12},{16,18},{18,... | collective-permute-start | bytes 98312 | tf_op jit(solution)/shard_map/ppermute | solution.py:589
  53.5 1.5 %collective-permute-done.11 = f32[16,512]{1,0:T(8,128)S(1)} collective-permute-done((f32[16,512]{1,0:T(8,128)S(1)}, f32[16,512]{1,0:T(8,128)S(1)}, u32[]{:S(2)}, u32[]{:S(2)}) %collective-permute-start.11) | collective-permute-done | bytes 32800 | tf_op jit(solution)/shard_map/ppermute | solution.py:589
  55.0 1.3 %collective-permute-done.9 = f32[16,512]{1,0:T(8,128)S(1)} collective-permute-done((f32[16,512]{1,0:T(8,128)S(1)}, f32[16,512]{1,0:T(8,128)S(1)}, u32[]{:S(2)}, u32[]{:S(2)}) %collective-permute-start.9) | collective-permute-done | bytes 32800 | tf_op jit(solution)/shard_map/ppermute | solution.py:589
  56.8 4.0 %collective-permute-start.13 = (f32[16,512]{1,0:T(8,128)S(1)}, f32[16,512]{1,0:T(8,128)S(1)}, u32[]{:S(2)}, u32[]{:S(2)}) collective-permute-start(f32[16,512]{1,0:T(8,128)S(1)} %add_add_fusion.1), channel_id=1, source_target_pairs={{0,8},{2,10},{4,12},{6,14},{8,0},{10,2},{12,4},{14,6},{16,24},{18,... | collective-permute-start | bytes 98312 | tf_op jit(solution)/shard_map/ppermute | solution.py:589
  60.8 1.3 %collective-permute-done.15 = f32[16,512]{1,0:T(8,128)S(1)} collective-permute-done((f32[16,512]{1,0:T(8,128)S(1)}, f32[16,512]{1,0:T(8,128)S(1)}, u32[]{:S(2)}, u32[]{:S(2)}) %collective-permute-start.15) | collective-permute-done | bytes 32800 | tf_op jit(solution)/shard_map/ppermute | solution.py:589
  62.1 0.6 collective-permute-done.13
  62.8 1.2 %collective-permute-done.16.theirs_ref = f32[16,512]{1,0:T(8,128)S(1)} collective-permute-done((f32[16,512]{1,0:T(8,128)S(1)}, f32[16,512]{1,0:T(8,128)S(1)}, u32[]{:S(2)}, u32[]{:S(2)}) %collective-permute-start.16) | collective-permute-done | bytes 32800 | tf_op jit(solution)/shard_map/ppermute | solution.py:589
  64.0 0.7 %finish.1 = (bf16[3,4,8,256]{3,2,1,0:T(8,128)(2,1)}, f32[16,27]{1,0:T(8,128)}, f32[16,432]{1,0:T(8,128)}, f32[16,432]{1,0:T(8,128)}, f32[3,32]{1,0:T(4,128)}) custom-call(f32[16,512]{1,0:T(8,128)S(1)} %add_add_fusion.mine_ref, f32[16,512]{1,0:T(8,128)S(1)} %collective-permute-done.16.theirs_ref, bf16[3,4,8,128]{3,2,1,0:T(8,128)(2,1)S(1)} %get-tuple-element.41.force_mine, ...), custom_call_target="tpu_custom_call" | custom-call | tf_op jit(solution)/shard_map/finish/pallas_call | solution.py:632
  (25 shorter events, 2.2 us)
Async XLA Ops:
  0.6 2.6 %collective-permute-start = (bf16[3,4,8,256]{3,2,1,0:T(8,128)(2,1)}, bf16[3,4,8,256]{3,2,1,0:T(8,128)(2,1)S(1)}, u32[]{:S(2)}, u32[]{:S(2)}) collective-permute-start(bf16[3,4,8,256]{3,2,1,0:T(8,128)(2,1)} %own_ref.1), channel_id=1, source_target_pairs={{0,1},{1,0},{2,3},{3,2},{4,5},{5,4},{6,7},{7,6},{8,9},{9,8},{10,11... | collective-permute-start | bytes 147464 | tf_op jit(solution)/shard_map/ppermute | solution.py:589
  3.2 19.0 %all-to-all-start = ((s32[32,1,2560]{2,1,0:T(1,128)}), s32[32,1,2560]{2,1,0:T(1,128)S(1)}, u32[]{:S(2)}, u32[]{:S(2)}) async-start(s32[32,1,2560]{2,1,0:T(1,128)} %pack.1), calls=%async_computation | async-start | bytes 655360 | tf_op jit(solution)/shard_map/all_to_all | solution.py:669
  11.0 0.8 %copy-start = (bf16[3,4,8,256]{3,2,1,0:T(8,128)(2,1)S(1)}, bf16[3,4,8,256]{3,2,1,0:T(8,128)(2,1)}, u32[]{:S(2)}) copy-start(bf16[3,4,8,256]{3,2,1,0:T(8,128)(2,1)} %own_ref.1) | copy-start | bytes 147460
  28.0 1.3 %collective-permute-start.1 = (f32[48,256]{1,0:T(8,128)S(1)}, f32[48,256]{1,0:T(8,128)S(1)}, u32[]{:S(2)}, u32[]{:S(2)}) collective-permute-start(f32[48,256]{1,0:T(8,128)S(1)} %deposit.1.own_ref), channel_id=1, source_target_pairs={{0,1},{1,0},{2,3},{3,2},{4,5},{5,4},{6,7},{7,6},{8,9},{9,8},{10,11... | collective-permute-start | bytes 147464 | tf_op jit(solution)/shard_map/ppermute | solution.py:589
  29.3 9.0 %collective-permute-start.2 = (f32[80,256]{1,0:T(8,128)S(1)}, f32[80,256]{1,0:T(8,128)S(1)}, u32[]{:S(2)}, u32[]{:S(2)}) collective-permute-start(f32[80,256]{1,0:T(8,128)S(1)} %get-tuple-element.27.near_ref), channel_id=1, source_target_pairs={{0,2},{1,31},{2,4},{3,1},{4,6},{5,3},{6,8},{7,5},{8,10},{9,7},{10,... | collective-permute-start | bytes 245768 | tf_op jit(solution)/shard_map/ppermute | solution.py:662
  29.8 8.1 %collective-permute-start.4 = (bf16[2,48,256]{2,1,0:T(8,128)(2,1)S(1)}, bf16[2,48,256]{2,1,0:T(8,128)(2,1)S(1)}, u32[]{:S(2)}, u32[]{:S(2)}) collective-permute-start(bf16[2,48,256]{2,1,0:T(8,128)(2,1)S(1)} %get-tuple-element.26.after_ref), channel_id=1, source_target_pairs={{0,2},{1,31},{2,4},{3,1},{4,6},{5,3},{6,8},{7,5},{8,10},{9,7},{10,... | collective-permute-start | bytes 147464 | tf_op jit(solution)/shard_map/ppermute | solution.py:662
  31.7 6.6 %collective-permute-start.3 = (f32[32,256]{1,0:T(8,128)S(1)}, f32[32,256]{1,0:T(8,128)S(1)}, u32[]{:S(2)}, u32[]{:S(2)}) collective-permute-start(f32[32,256]{1,0:T(8,128)S(1)} %get-tuple-element.28.after_ref), channel_id=1, source_target_pairs={{0,4},{1,29},{2,6},{3,31},{4,8},{5,1},{6,10},{7,3},{8,12},{9,5},{1... | collective-permute-start | bytes 98312 | tf_op jit(solution)/shard_map/ppermute | solution.py:662
  38.3 1.7 %collective-permute-start.5 = (f32[80,256]{1,0:T(8,128)S(1)}, f32[80,256]{1,0:T(8,128)S(1)}, u32[]{:S(2)}, u32[]{:S(2)}) collective-permute-start(f32[80,256]{1,0:T(8,128)S(1)} %collective-permute-done.2.near_mine), channel_id=1, source_target_pairs={{0,1},{1,0},{2,3},{3,2},{4,5},{5,4},{6,7},{7,6},{8,9},{9,8},{10,11... | collective-permute-start | bytes 245768 | tf_op jit(solution)/shard_map/ppermute | solution.py:589
  38.3 1.7 %collective-permute-start.7 = (bf16[2,48,256]{2,1,0:T(8,128)(2,1)S(1)}, bf16[2,48,256]{2,1,0:T(8,128)(2,1)S(1)}, u32[]{:S(2)}, u32[]{:S(2)}) collective-permute-start(bf16[2,48,256]{2,1,0:T(8,128)(2,1)S(1)} %collective-permute-done.4.ct_mine), channel_id=1, source_target_pairs={{0,1},{1,0},{2,3},{3,2},{4,5},{5,4},{6,7},{7,6},{8,9},{9,8},{10,11... | collective-permute-start | bytes 147464 | tf_op jit(solution)/shard_map/ppermute | solution.py:589
  38.8 1.2 %collective-permute-start.6 = (f32[32,256]{1,0:T(8,128)S(1)}, f32[32,256]{1,0:T(8,128)S(1)}, u32[]{:S(2)}, u32[]{:S(2)}) collective-permute-start(f32[32,256]{1,0:T(8,128)S(1)} %collective-permute-done.3.far_mine), channel_id=1, source_target_pairs={{0,1},{1,0},{2,3},{3,2},{4,5},{5,4},{6,7},{7,6},{8,9},{9,8},{10,11... | collective-permute-start | bytes 98312 | tf_op jit(solution)/shard_map/ppermute | solution.py:589
  48.7 1.3 %collective-permute-start.8 = (f32[16,512]{1,0:T(8,128)S(1)}, f32[16,512]{1,0:T(8,128)S(1)}, u32[]{:S(2)}, u32[]{:S(2)}) collective-permute-start(f32[16,512]{1,0:T(8,128)S(1)} %get-tuple-element.38), channel_id=1, source_target_pairs={{0,1},{1,0},{2,3},{3,2},{4,5},{5,4},{6,7},{7,6},{8,9},{9,8},{10,11... | collective-permute-start | bytes 98312 | tf_op jit(solution)/shard_map/ppermute | solution.py:589
  50.0 5.0 %collective-permute-start.11 = (f32[16,512]{1,0:T(8,128)S(1)}, f32[16,512]{1,0:T(8,128)S(1)}, u32[]{:S(2)}, u32[]{:S(2)}) collective-permute-start(f32[16,512]{1,0:T(8,128)S(1)} %add.29), channel_id=1, source_target_pairs={{0,6},{2,4},{4,2},{6,0},{8,14},{10,12},{12,10},{14,8},{16,22},{18,... | collective-permute-start | bytes 98312 | tf_op jit(solution)/shard_map/ppermute | solution.py:589
  50.0 5.0 %collective-permute-start.10 = (f32[16,512]{1,0:T(8,128)S(1)}, f32[16,512]{1,0:T(8,128)S(1)}, u32[]{:S(2)}, u32[]{:S(2)}) collective-permute-start(f32[16,512]{1,0:T(8,128)S(1)} %add.29), channel_id=1, source_target_pairs={{0,4},{2,6},{4,0},{6,2},{8,12},{10,14},{12,8},{14,10},{16,20},{18,... | collective-permute-start | bytes 98312 | tf_op jit(solution)/shard_map/ppermute | solution.py:589
  52.4 3.9 %collective-permute-start.9 = (f32[16,512]{1,0:T(8,128)S(1)}, f32[16,512]{1,0:T(8,128)S(1)}, u32[]{:S(2)}, u32[]{:S(2)}) collective-permute-start(f32[16,512]{1,0:T(8,128)S(1)} %add.29), channel_id=1, source_target_pairs={{0,2},{2,0},{4,6},{6,4},{8,10},{10,8},{12,14},{14,12},{16,18},{18,... | collective-permute-start | bytes 98312 | tf_op jit(solution)/shard_map/ppermute | solution.py:589
  53.5 2.8 %collective-permute-start.12 = (bf16[3,4,8,128]{3,2,1,0:T(8,128)(2,1)S(1)}, bf16[3,4,8,128]{3,2,1,0:T(8,128)(2,1)S(1)}, u32[]{:S(2)}, u32[]{:S(2)}) collective-permute-start(bf16[3,4,8,128]{3,2,1,0:T(8,128)(2,1)S(1)} %get-tuple-element.39), channel_id=1, source_target_pairs={{0,1},{1,0},{2,3},{3,2},{4,5},{5,4},{6,7},{7,6},{8,9},{9,8},{10,11... | collective-permute-start | bytes 73736 | tf_op jit(solution)/shard_map/ppermute | solution.py:589
  56.3 5.8 %collective-permute-start.15 = (f32[16,512]{1,0:T(8,128)S(1)}, f32[16,512]{1,0:T(8,128)S(1)}, u32[]{:S(2)}, u32[]{:S(2)}) collective-permute-start(f32[16,512]{1,0:T(8,128)S(1)} %add_add_fusion.1), channel_id=1, source_target_pairs={{0,24},{2,26},{4,28},{6,30},{8,16},{10,18},{12,20},{14,22},{16,8},... | collective-permute-start | bytes 98312 | tf_op jit(solution)/shard_map/ppermute | solution.py:589
  56.8 5.3 %collective-permute-start.14 = (f32[16,512]{1,0:T(8,128)S(1)}, f32[16,512]{1,0:T(8,128)S(1)}, u32[]{:S(2)}, u32[]{:S(2)}) collective-permute-start(f32[16,512]{1,0:T(8,128)S(1)} %add_add_fusion.1), channel_id=1, source_target_pairs={{0,16},{2,18},{4,20},{6,22},{8,24},{10,26},{12,28},{14,30},{16,0},... | collective-permute-start | bytes 98312 | tf_op jit(solution)/shard_map/ppermute | solution.py:589
  56.8 5.9 %collective-permute-start.13 = (f32[16,512]{1,0:T(8,128)S(1)}, f32[16,512]{1,0:T(8,128)S(1)}, u32[]{:S(2)}, u32[]{:S(2)}) collective-permute-start(f32[16,512]{1,0:T(8,128)S(1)} %add_add_fusion.1), channel_id=1, source_target_pairs={{0,8},{2,10},{4,12},{6,14},{8,0},{10,2},{12,4},{14,6},{16,24},{18,... | collective-permute-start | bytes 98312 | tf_op jit(solution)/shard_map/ppermute | solution.py:589
  62.7 1.3 %collective-permute-start.16 = (f32[16,512]{1,0:T(8,128)S(1)}, f32[16,512]{1,0:T(8,128)S(1)}, u32[]{:S(2)}, u32[]{:S(2)}) collective-permute-start(f32[16,512]{1,0:T(8,128)S(1)} %add_add_fusion.mine_ref), channel_id=1, source_target_pairs={{0,1},{1,0},{2,3},{3,2},{4,5},{5,4},{6,7},{7,6},{8,9},{9,8},{10,11... | collective-permute-start | bytes 98312 | tf_op jit(solution)/shard_map/ppermute | solution.py:589
